TPU v7x, 512 devices: a whole 4x8x8 slice. The times are simulated.
512 devices in a mesh: frame: 64 (over z, x, core), pool: 8 (over y).
Axes of the slice: x: 4, y: 8, z: 8, core: 2. Of those that a mesh axis runs over, the one named last changes fastest.
Arguments:
- frames_in: bfloat16 [256, 256, 1408], P('frame'), may hold values from -6 to 6
- qkv_weight: bfloat16 [1408, 3, 1408], P('frame', None, 'pool')
- out_weight: bfloat16 [1408, 1408], P('pool', 'frame'), may hold values from -0.15625 to 0.15625
- owners: int32 [256], P('frame'), may hold values from 0 to 7, as said below
- slots: int32 [256], P('frame'), may hold values from 0 to 0, as said below
Outputs:
- shipped: bfloat16 [512, 256, 1408], P(('frame', 'pool'))
- shipped_scales: bfloat16 [512, 11, 256], P(('frame', 'pool'))
Inputs may be any that keep to these rules, and one draw needn't show every extreme that they name: `owners`: within each group of 4 frames f // 4, no owner receives more than 1 frames, and one owner receives exactly 1. Within each group of 4 frames, the frames sent to one owner hold distinct slots 0, 1, ... in the order of their count.
All inputs are finite; a program needn't handle non-finite values. Where the computation divides by a largest or mean magnitude, that divisor is 1e-20 or more.
Results may differ from a plain program's by a relative error of at most 0.015.
Values may be sent and summed in bfloat16 or wider, within the bound.
No kernel may reach another device: no remote copies, remote signals or barrier semaphores. Data moves between devices by JAX's collectives and lax.ppermute only.
A program may use at most 64 MiB of HBM per device.

v0:
```python
import jax
import jax.numpy as jnp
from jax import lax
from jax.sharding import PartitionSpec as P

HEAD_DIM = 88
GROUP = 128


def local(frames_in, qkv_weight, out_weight, owners, slots):
    fr_count, patch_count, width = frames_in.shape
    pool_size = lax.axis_size("pool")
    frame_size = lax.axis_size("frame")
    capacity = (fr_count + pool_size - 1) // pool_size
    head_width = qkv_weight.shape[2]
    heads_here = head_width // HEAD_DIM
    all_frames = fr_count * frame_size
    track_patches = patch_count // frame_size
    own_patches = patch_count // pool_size
    xf = frames_in.astype(jnp.float32)
    mean = jnp.mean(xf, axis=-1, keepdims=True)
    centred = xf - mean
    var = jnp.mean(centred * centred, axis=-1, keepdims=True)
    normed = (centred * lax.rsqrt(var + 1e-06)).astype(jnp.bfloat16)
    tokens = normed.reshape(fr_count * patch_count, width)
    projected = jnp.einsum(
        "td,dkc->tkc",
        tokens,
        lax.all_gather(qkv_weight, "frame", axis=0, tiled=True),
        preferred_element_type=jnp.float32,
    )
    query = projected[:, 0, :].astype(jnp.bfloat16).reshape(fr_count, patch_count, head_width)
    key = projected[:, 1, :].astype(jnp.bfloat16).reshape(fr_count, patch_count, head_width)
    value = projected[:, 2, :].astype(jnp.bfloat16).reshape(fr_count, patch_count, head_width)
    query, key, value = (
        lax.all_to_all(query, "frame", split_axis=1, concat_axis=0, tiled=True),
        lax.all_to_all(key, "frame", split_axis=1, concat_axis=0, tiled=True),
        lax.all_to_all(value, "frame", split_axis=1, concat_axis=0, tiled=True),
    )
    shape4 = (all_frames, track_patches, heads_here, HEAD_DIM)
    factor = 1.0 / HEAD_DIM**0.5
    scores = (
        jnp.einsum(
            "fphc,gphc->phfg",
            query.reshape(shape4),
            key.reshape(shape4),
            preferred_element_type=jnp.float32,
        )
        * factor
    )
    top = jnp.max(scores, axis=-1, keepdims=True)
    expo = jnp.exp(scores - top)
    weights = (expo / jnp.sum(expo, axis=-1, keepdims=True)).astype(jnp.bfloat16)
    attended = jnp.einsum(
        "phfg,gphc->fphc", weights, value.reshape(shape4), preferred_element_type=jnp.float32
    )
    attended = attended.astype(jnp.bfloat16).reshape(all_frames, track_patches, head_width)
    returned = lax.all_to_all(attended, "frame", split_axis=0, concat_axis=1, tiled=True)
    partial_value = jnp.einsum(
        "fpc,cn->fpn",
        returned,
        lax.all_gather(out_weight, "frame", axis=1, tiled=True),
        preferred_element_type=jnp.float32,
    )
    summed = lax.psum_scatter(
        partial_value.astype(jnp.bfloat16), "pool", scatter_dimension=1, tiled=True
    ).astype(jnp.float32)
    position = lax.axis_index("pool")
    own_rows = lax.dynamic_slice_in_dim(frames_in, position * own_patches, own_patches, 1).astype(
        jnp.float32
    )
    mixed = own_rows + summed
    group_count = width // GROUP
    grouped = mixed.reshape(fr_count, own_patches, group_count, GROUP)
    scale = (jnp.max(jnp.abs(grouped), axis=-1) + 1e-06).astype(jnp.bfloat16)
    coded = (
        (grouped / scale[..., None].astype(jnp.float32))
        .astype(jnp.bfloat16)
        .reshape(fr_count, own_patches, width)
    )
    scale_t = jnp.transpose(scale, (0, 2, 1))
    slot_ids = jnp.arange(capacity, dtype=jnp.int32)
    whole_rows, whole_scales = (
        lax.all_gather(coded, "pool", axis=1, tiled=True),
        lax.all_gather(scale_t, "pool", axis=2, tiled=True),
    )
    mine = ((owners[None, :] == position) & (slots[None, :] == slot_ids[:, None])).astype(
        jnp.bfloat16
    )
    shipped = jnp.einsum(
        "cj,jpd->cpd", mine, whole_rows, preferred_element_type=jnp.float32
    ).astype(jnp.bfloat16)
    shipped_scales = jnp.einsum(
        "cj,jgp->cgp", mine, whole_scales, preferred_element_type=jnp.float32
    ).astype(jnp.bfloat16)
    return (shipped, shipped_scales)


def solution(mesh):
    return jax.shard_map(
        local,
        mesh=mesh,
        in_specs=(
            P("frame", None, None),
            P("frame", None, "pool"),
            P("pool", "frame"),
            P("frame"),
            P("frame"),
        ),
        out_specs=(P(("frame", "pool"), None, None), P(("frame", "pool"), None, None)),
        check_vma=False,
    )
```

profile of v0, /device:TPU:1, one launch (start us, length us, event | category | flops | bytes accessed | tf_op | source)
XLA Modules:
  0.0 380.6 jit_solution(4834098870668226049)
XLA Ops:
  8.8 2.3 convert_reduce_fusion
  12.0 2.3 fusion.4
  14.3 87.6 %all-gather.4.cloned.1.call-done = bf16[1408,3,176]{2,1,0:T(4,128)(2,1)} async-done(((bf16[22,3,176]{2,1,0:T(4,128)(2,1)}), bf16[1408,3,176]{2,1,0:T(4,128)(2,1)}) %all-gather.4.cloned.1.call-update) | async-done | bytes 1486864 | tf_op jit(solution)/shard_map/all_gather | solution.py:29
  102.0 4.6 %fusion.10 = bf16[1024,3,176]{0,2,1:T(8,128)(2,1)S(1)} fusion(bf16[1024,1408,1]{1,0,2:T(8,128)(2,1)} %bitcast.56, bf16[1408,3,176]{2,1,0:T(4,128)(2,1)} %all-gather.4.cloned.1.call-done), kind=kOutput, calls=%fused_computation.16 | convolution fusion | flops 1523073024 | bytes 5451776 | tf_op jit(solution)/shard_map/td,dkc->tkc/dot_general | solution.py:26
  110.1 6.3 %all-to-all-start.1 = ((bf16[4,256,176]{2,0,1:T(4,128)(2,1)}), bf16[4,256,176]{2,0,1:T(4,128)(2,1)S(1)}, u32[]{:S(2)}, u32[]{:S(2)}) async-start(bf16[4,256,176]{2,0,1:T(4,128)(2,1)} %copy.31), calls=%async_computation.1 | async-start | bytes 1048576 | tf_op jit(solution)/shard_map/all_to_all | solution.py:36
  118.4 2.1 copy.33
  120.5 13.6 %all-to-all-done.1 = bf16[4,256,176]{2,0,1:T(4,128)(2,1)S(1)} async-done(((bf16[4,256,176]{2,0,1:T(4,128)(2,1)}), bf16[4,256,176]{2,0,1:T(4,128)(2,1)S(1)}, u32[]{:S(2)}, u32[]{:S(2)}) %all-to-all-start.1) | async-done | bytes 360480 | tf_op jit(solution)/shard_map/all_to_all | solution.py:36
  134.1 5.9 %all-to-all-start.2 = ((bf16[4,256,176]{2,0,1:T(4,128)(2,1)}), bf16[4,256,176]{2,0,1:T(4,128)(2,1)}, u32[]{:S(2)}, u32[]{:S(2)}) async-start(bf16[4,256,176]{2,0,1:T(4,128)(2,1)} %copy.33), calls=%async_computation.2 | async-start | bytes 1048576 | tf_op jit(solution)/shard_map/all_to_all | solution.py:37
  144.2 13.5 %all-to-all-done.2 = bf16[4,256,176]{2,0,1:T(4,128)(2,1)} async-done(((bf16[4,256,176]{2,0,1:T(4,128)(2,1)}), bf16[4,256,176]{2,0,1:T(4,128)(2,1)}, u32[]{:S(2)}, u32[]{:S(2)}) %all-to-all-start.2) | async-done | bytes 360480 | tf_op jit(solution)/shard_map/all_to_all | solution.py:37
  157.7 5.9 %all-to-all-start = ((bf16[4,256,176]{2,0,1:T(4,128)(2,1)}), bf16[4,256,176]{2,0,1:T(4,128)(2,1)}, u32[]{:S(2)}, u32[]{:S(2)}) async-start(bf16[4,256,176]{2,0,1:T(4,128)(2,1)} %copy.29), calls=%async_computation | async-start | bytes 1048576 | tf_op jit(solution)/shard_map/all_to_all | solution.py:38
  164.6 2.3 reshape.68
  169.3 12.0 %all-to-all-done = bf16[4,256,176]{2,0,1:T(4,128)(2,1)} async-done(((bf16[4,256,176]{2,0,1:T(4,128)(2,1)}), bf16[4,256,176]{2,0,1:T(4,128)(2,1)}, u32[]{:S(2)}, u32[]{:S(2)}) %all-to-all-start) | async-done | bytes 360480 | tf_op jit(solution)/shard_map/all_to_all | solution.py:38
  183.7 3.4 fusion.39
  187.1 2.7 convolution_convert_fusion.1
  191.8 5.9 %all-to-all-start.3 = ((bf16[256,4,176]{2,1,0:T(4,128)(2,1)}), bf16[256,4,176]{2,1,0:T(4,128)(2,1)S(1)}, u32[]{:S(2)}, u32[]{:S(2)}) async-start(bf16[256,4,176]{2,1,0:T(4,128)(2,1)} %copy.39), calls=%async_computation.3 | async-start | bytes 1048576 | tf_op jit(solution)/shard_map/all_to_all | solution.py:58
  197.8 62.1 %all-gather = bf16[64,22,176]{2,1,0:T(8,128)(2,1)} all-gather(bf16[1,22,176]{2,1,0:T(8,128)(2,1)S(1)} %bitcast.61), channel_id=1, replica_groups=mesh['frame'=64,'pool'=8] {'frame'}, dimensions={0}, use_global_device_ids=true | all-gather | bytes 503360 | tf_op jit(solution)/shard_map/all_gather | solution.py:62
  259.9 2.2 reshape.72
  262.3 3.7 convolution_convert_fusion
  266.1 42.9 %reduce-scatter.2.cloned.1.call-done = bf16[4,32,1408]{2,1,0:T(8,128)(2,1)} async-done(((bf16[4,256,1408]{2,1,0:T(8,128)(2,1)}), bf16[4,32,1408]{2,1,0:T(8,128)(2,1)}) %reduce-scatter.2.cloned.1.call-update) | async-done | bytes 360464 | tf_op jit(solution)/shard_map/reduce_scatter | solution.py:65
  310.9 2.3 abs.7
  316.1 2.2 div.30
  320.4 19.2 %all_gather.15 = bf16[4,11,256]{1,2,0:T(8,128)(2,1)S(1)} all-gather(bf16[4,11,32]{1,2,0:T(8,128)(2,1)S(1)} %get-tuple-element.5), channel_id=1, replica_groups=mesh['frame'=64,'pool'=8] {'pool'}, dimensions={2}, use_global_device_ids=true | all-gather | bytes 25344 | tf_op jit(solution)/shard_map/all_gather | solution.py:85
  340.5 28.5 %all-gather.6.cloned.1.call-done = bf16[4,256,1408]{2,1,0:T(8,128)(2,1)} async-done(((bf16[4,32,1408]{2,1,0:T(8,128)(2,1)}), bf16[4,256,1408]{2,1,0:T(8,128)(2,1)}) %all-gather.6.cloned.1.call-update) | async-done | bytes 2883600 | tf_op jit(solution)/shard_map/all_gather | solution.py:84
  369.0 4.1 %fusion.5 = bf16[1,256,1408]{2,0,1:T(2,128)(2,1)S(1)} fusion(pred[4,1,1]{0,1,2:T(4,128)(4,1)S(1)} %and_bitcast_fusion, bf16[4,256,1408]{2,1,0:T(8,128)(2,1)} %all-gather.6.cloned.1.call-done), kind=kOutput, calls=%fused_computation.8 | convolution fusion | flops 2883584 | bytes 3604484 | tf_op jit(solution)/shard_map/cj,jpd->cpd/dot_general | solution.py:90
  (46 shorter events, 29.1 us)
Async XLA Ops:
  7.2 3.9 %copy-start = (bf16[4,256,1408]{2,1,0:T(8,128)(2,1)S(1)}, bf16[4,256,1408]{2,1,0:T(8,128)(2,1)}, u32[]{:S(2)}) copy-start(bf16[4,256,1408]{2,1,0:T(8,128)(2,1)} %param.5) | copy-start | bytes 8650756
  7.2 94.8 %all-gather.4.cloned.1.call-start = ((), (), s32[]{:S(2)}) async-start(), calls=%async_computation.5 | async-start | bytes 2928640 | tf_op jit(solution)/shard_map/all_gather | solution.py:29
  110.1 24.1 %all-to-all-start.1 = ((bf16[4,256,176]{2,0,1:T(4,128)(2,1)}), bf16[4,256,176]{2,0,1:T(4,128)(2,1)S(1)}, u32[]{:S(2)}, u32[]{:S(2)}) async-start(bf16[4,256,176]{2,0,1:T(4,128)(2,1)} %copy.31), calls=%async_computation.1 | async-start | bytes 1048576 | tf_op jit(solution)/shard_map/all_to_all | solution.py:36
  134.1 23.6 %all-to-all-start.2 = ((bf16[4,256,176]{2,0,1:T(4,128)(2,1)}), bf16[4,256,176]{2,0,1:T(4,128)(2,1)}, u32[]{:S(2)}, u32[]{:S(2)}) async-start(bf16[4,256,176]{2,0,1:T(4,128)(2,1)} %copy.33), calls=%async_computation.2 | async-start | bytes 1048576 | tf_op jit(solution)/shard_map/all_to_all | solution.py:37
  157.7 23.6 %all-to-all-start = ((bf16[4,256,176]{2,0,1:T(4,128)(2,1)}), bf16[4,256,176]{2,0,1:T(4,128)(2,1)}, u32[]{:S(2)}, u32[]{:S(2)}) async-start(bf16[4,256,176]{2,0,1:T(4,128)(2,1)} %copy.29), calls=%async_computation | async-start | bytes 1048576 | tf_op jit(solution)/shard_map/all_to_all | solution.py:38
  183.7 3.4 copy-start.2
  187.1 10.7 %copy-start.3 = (bf16[176,22]{0,1:T(8,128)(2,1)S(1)}, bf16[176,22]{0,1:T(8,128)(2,1)}, u32[]{:S(2)}) copy-start(bf16[176,22]{0,1:T(8,128)(2,1)} %param.7) | copy-start | bytes 23236
  191.8 70.3 %all-to-all-start.3 = ((bf16[256,4,176]{2,1,0:T(4,128)(2,1)}), bf16[256,4,176]{2,1,0:T(4,128)(2,1)S(1)}, u32[]{:S(2)}, u32[]{:S(2)}) async-start(bf16[256,4,176]{2,1,0:T(4,128)(2,1)} %copy.39), calls=%async_computation.3 | async-start | bytes 1048576 | tf_op jit(solution)/shard_map/all_to_all | solution.py:58
  197.7 111.3 %reduce-scatter.2.cloned.1.call-start = ((), (), s32[]{:S(2)}) async-start(), calls=%async_computation.6 | async-start | bytes 3244032 | tf_op jit(solution)/shard_map/reduce_scatter | solution.py:65
  266.0 103.0 %all-gather.6.cloned.1.call-start = ((), (), s32[]{:S(2)}) async-start(), calls=%async_computation.7 | async-start | bytes 3244032 | tf_op jit(solution)/shard_map/all_gather | solution.py:84
  310.9 7.4 %copy-start.1 = (bf16[4,32,1408]{2,1,0:T(8,128)(2,1)S(1)}, bf16[4,32,1408]{2,1,0:T(8,128)(2,1)}, u32[]{:S(2)}) copy-start(bf16[4,32,1408]{2,1,0:T(8,128)(2,1)} %reduce-scatter.2.cloned.1.call-done) | copy-start | bytes 1081348
  314.8 5.6 %copy-start.4 = (s32[4]{0:T(128)S(1)}, s32[4]{0:T(128)}, u32[]{:S(2)}) copy-start(s32[4]{0:T(128)} %param.9) | copy-start | bytes 52
  314.8 5.6 %copy-start.5 = (s32[4]{0:T(128)S(1)}, s32[4]{0:T(128)}, u32[]{:S(2)}) copy-start(s32[4]{0:T(128)} %param.8) | copy-start | bytes 52
Sparse Core Ops, SparseCore 0:
  11.9 90.0 all-gather.3
  266.1 42.8 reduce-scatter.1
  320.4 48.4 all-gather.5
where the time goes:
time: 382 us; the launch traced here: 381 us
  waiting for transfers between devices  198 us (52%)
  blocking collectives  81.3 us (21%)
  local copies, waits for them, and re-layouts  33.3 us (9%)
  starting transfers between devices  24.2 us (6%)
  matrix products  18.6 us (5%)
  between operations  13.9 us (4%)
  other arithmetic  11.1 us (3%)
    all_gather x1, waiting for transfers between devices, local(): lax.all_gather(qkv_weight, 'frame', axis=0, tiled=True)  87.6 us
    all_gather x1, blocking collectives, local(): lax.all_gather(out_weight, 'frame', axis=1, tiled=True)  62.1 us
    reduce_scatter x1, waiting for transfers between devices, local(): lax.psum_scatter(partial_value.astype(jnp.bfloat16), 'pool', scatter_dime...  42.9 us
    all_gather x1, waiting for transfers between devices, local(): lax.all_gather(coded, 'pool', axis=1, tiled=True)  28.5 us
    all_gather x1, blocking collectives, local(): lax.all_gather(scale_t, 'pool', axis=2, tiled=True)  19.2 us
    all_to_all x1, waiting for transfers between devices, local(): lax.all_to_all(query, 'frame', split_axis=1, concat_axis=0, tiled=True)  13.6 us
    all_to_all x1, waiting for transfers between devices, local(): lax.all_to_all(key, 'frame', split_axis=1, concat_axis=0, tiled=True)  13.5 us
    all_to_all x1, waiting for transfers between devices, local(): lax.all_to_all(value, 'frame', split_axis=1, concat_axis=0, tiled=True)  12 us
  transfers between devices with their start and end apart: 7, of which 6 were waited for; matrix products, arithmetic and copies ran while one was open for 6% of the time, Pallas kernels for 0%

commit v1 on v0

v1 whole, which is shorter than its diff:
```python
import functools

import jax
import jax.numpy as jnp
from jax import lax
from jax.experimental import pallas as pl
from jax.experimental.pallas import tpu as pltpu
from jax.sharding import Mesh, PartitionSpec as P

HEAD_DIM = 88
GROUP = 128
MAIN = 64
SLOT = 32
FACTOR = 1.0 / HEAD_DIM**0.5
CHIP = ("zh", "zl", "x")
FRAME = CHIP + ("c",)
VMEM_LIMIT = 40 * 1024 * 1024
F32 = jnp.float32
BF16 = jnp.bfloat16


def lanes_of(shape):
    return lax.broadcasted_iota(jnp.int32, shape, len(shape) - 1)


def turn(value, shift):
    shift = shift % 128
    if shift == 0:
        return value
    return pltpu.roll(value, shift, len(value.shape) - 1)


def spread(value, axis):
    count = lax.axis_size(axis)
    copies = jnp.broadcast_to(value[None], (count,) + value.shape)
    return lax.all_to_all(copies, axis, 0, 0, tiled=True)


def project_kernel(core_ref, own_ref, other_ref, weight_ref, out_ref, rest_ref):
    step = pl.program_id(0)
    core = core_ref[0]
    chips = out_ref.shape[0]

    @pl.when(step == 0)
    def _():
        rest_ref[...] = jnp.zeros_like(rest_ref)

    lane = lanes_of(rest_ref.shape)
    for which, ref in enumerate((own_ref, other_ref)):
        frame = (core if which == 0 else 1 - core) * 4 + step
        rows = jnp.dot(ref[0], weight_ref[...], preferred_element_type=F32)
        for tile in range(2):
            block = rows[:, tile * 128 : (tile + 1) * 128].astype(BF16)
            out_ref[:, 2 * frame + tile] = block.reshape(chips, 8, 128)
        rest = jnp.where(lane < 8, rows[:, 256:384], 0.0)
        rest_ref[...] += pltpu.roll(rest, 8 * frame, 1)

    @pl.when(step == pl.num_programs(0) - 1)
    def _():
        out_ref[:, 16] = rest_ref[...].astype(BF16).reshape(chips, 8, 128)


def attend_kernel(x_ref, out_ref, q_ref, k_ref, v_ref, o_ref):
    chips = x_ref.shape[0]
    frames = chips * 8
    shape = (chips, 8, 128)
    lane = lanes_of(shape)
    rest = x_ref[:, 16].astype(F32)
    for fr in range(8):
        first = x_ref[:, 2 * fr].astype(F32)
        second = x_ref[:, 2 * fr + 1].astype(F32)
        rows = slice(fr * 8, fr * 8 + 8)
        q_ref[:, rows, :] = jnp.where(lane < HEAD_DIM, first, 0.0)
        k_ref[:, rows, :] = second
        v_ref[:, rows, :] = jnp.where(
            lane < 40,
            turn(first, 40),
            jnp.where(
                lane < 80,
                turn(second, 80),
                jnp.where(lane < HEAD_DIM, turn(rest, 80 - 8 * fr), 0.0),
            ),
        )
    for patch in range(8):
        pick = pl.ds(patch, 8, stride=8)
        query = q_ref[:, pick, :].reshape(frames, 128).astype(BF16)
        key = k_ref[:, pick, :].reshape(frames, 128).astype(BF16)
        value = v_ref[:, pick, :].reshape(frames, 128).astype(BF16)
        scores = lax.dot_general(query, key, (((1,), (1,)), ((), ())), preferred_element_type=F32)
        top = jnp.max(scores, axis=-1, keepdims=True)
        expo = jnp.exp((scores - top) * FACTOR)
        total = jnp.sum(expo, axis=-1, keepdims=True)
        mixed = jnp.dot(expo.astype(BF16), value, preferred_element_type=F32)
        o_ref[:, pick, :] = (mixed * (1.0 / total)).reshape(shape)
    for tile in range(4):
        even = o_ref[:, tile * 16 : tile * 16 + 8, :]
        odd = o_ref[:, tile * 16 + 8 : tile * 16 + 16, :]
        out_ref[:, tile] = jnp.where(lane < MAIN, even, turn(odd, MAIN)).astype(BF16)
    for tile in range(2):
        packed = None
        for part in range(4):
            fr = tile * 4 + part
            piece = turn(o_ref[:, fr * 8 : fr * 8 + 8, :], SLOT * part - MAIN)
            packed = piece if part == 0 else jnp.where(lane >= SLOT * part, piece, packed)
        out_ref[:, 4 + tile] = packed.astype(BF16)


def pack_kernel(owner_ref, x_ref, out_ref):
    chips = x_ref.shape[0]
    half, quarter = chips // 2, chips // 4
    out_ref[...] = jnp.zeros_like(out_ref)
    lane = lanes_of((half, 8, 128))
    lane_q = lanes_of((quarter, 8, 128))
    for fr in range(8):
        place = (fr // 4) * 8 + owner_ref[fr]
        tile = x_ref[:, fr // 2].astype(F32)
        low, high = tile[:half], tile[half:]
        side = fr % 2
        main = jnp.where(lane < MAIN, turn(low, MAIN * side), turn(high, MAIN * (1 - side)))
        out_ref[place, :half] = main.astype(BF16)
        tile = x_ref[:, 4 + fr // 4].astype(F32)
        packed = None
        for part in range(4):
            piece = turn(tile[part * quarter : (part + 1) * quarter], SLOT * (part - fr % 4))
            packed = piece if part == 0 else jnp.where(lane_q >= SLOT * part, piece, packed)
        out_ref[place, half:] = packed.astype(BF16)


def deliver_kernel(pick_ref, frame_ref, y_ref, weight_ref, out_ref, scale_ref):
    sources = y_ref.shape[0]
    patches, width = frame_ref.shape[1:]
    half, quarter = patches // 2, patches // 4
    tiles = half // 8
    valid = pick_ref[1] > 0
    lane = lanes_of((half, 128))
    lane_q = lanes_of((quarter, 128))
    mains, rests = [], []
    for pair in range(sources // 2):
        first = y_ref[2 * pair, :tiles].reshape(half, 128).astype(F32)
        second = y_ref[2 * pair + 1, :tiles].reshape(half, 128).astype(F32)
        low = jnp.where(lane < MAIN, first, turn(second, MAIN))
        high = jnp.where(lane < MAIN, turn(first, MAIN), second)
        mains.append(jnp.concatenate([low, high], axis=0).astype(BF16))
    for group in range(sources // 4):
        pieces = [
            y_ref[4 * group + part, tiles:].reshape(quarter, 128).astype(F32) for part in range(4)
        ]
        rows = []
        for block in range(4):
            packed = None
            for part in range(4):
                piece = turn(pieces[part], SLOT * (part - block))
                packed = piece if part == 0 else jnp.where(lane_q >= SLOT * part, piece, packed)
            rows.append(packed)
        rests.append(jnp.concatenate(rows, axis=0).astype(BF16))
    left = jnp.concatenate(mains, axis=1)
    left_rest = jnp.concatenate(rests, axis=1)
    lane_p = lanes_of((patches, 128))
    scales = jnp.zeros((patches, 128), F32)
    for start in range(0, width, 256):
        stop = min(start + 256, width)
        right = weight_ref[:, :MAIN, start:stop].reshape(sources * MAIN, stop - start)
        right_rest = weight_ref[:, MAIN:, start:stop].reshape(sources * SLOT, stop - start)
        total = jnp.dot(left, right, preferred_element_type=F32)
        total += jnp.dot(left_rest, right_rest, preferred_element_type=F32)
        total += frame_ref[0, :, start:stop].astype(F32)
        for at in range(0, stop - start, GROUP):
            part = total[:, at : at + GROUP]
            top = jnp.max(jnp.abs(part), axis=-1, keepdims=True)
            scale = (top + 1e-06).astype(BF16).astype(F32)
            coded = jnp.where(valid, part / scale, 0.0).astype(BF16)
            out_ref[0, :, start + at : start + at + GROUP] = coded
            scales = jnp.where(lane_p == (start + at) // GROUP, scale, scales)
    scales = jnp.where(valid, scales, 0.0).T
    scale_ref[0] = scales[: width // GROUP].astype(BF16)


def params():
    return pltpu.CompilerParams(vmem_limit_bytes=VMEM_LIMIT)


def local(frames_in, qkv_weight, out_weight, owners, slots):
    fr_count, patch_count, width = frames_in.shape
    rows_here = qkv_weight.shape[0]
    core = lax.axis_index("c")
    position = lax.axis_index("pool")
    chips = lax.axis_size("zh") * lax.axis_size("zl") * lax.axis_size("x")
    sources = 2 * lax.axis_size("pool")
    swap = [(0, 1), (1, 0)]

    xf = frames_in.astype(F32)
    mean = jnp.mean(xf, axis=-1, keepdims=True)
    centred = xf - mean
    var = jnp.mean(centred * centred, axis=-1, keepdims=True)
    normed = (centred * lax.rsqrt(var + 1e-06)).astype(BF16)
    normed_other = lax.ppermute(normed, "c", swap)
    owners_other = lax.ppermute(owners, "c", swap)

    parts = qkv_weight.reshape(rows_here, 3, 2, HEAD_DIM)
    query, key, value = parts[:, 0], parts[:, 1], parts[:, 2]
    back = out_weight.T.reshape(rows_here, 2, HEAD_DIM)
    blank = functools.partial(jnp.zeros, dtype=BF16)
    payload = jnp.concatenate(
        [
            query,
            value[..., :40],
            key,
            value[..., 40:80],
            value[..., 80:],
            blank((rows_here, 2, 24)),
            back,
            blank((rows_here, 2, 8)),
        ],
        axis=-1,
    )
    both = lax.all_gather(payload, "c", axis=0, tiled=True)
    mine = lax.dynamic_index_in_dim(both, core, 1, keepdims=False)
    mine = spread(mine, "zh").reshape(-1, mine.shape[-1])
    mine = spread(mine, ("zl", "x"))
    mine = mine.reshape(8, 4, 2 * rows_here, -1).transpose(1, 0, 2, 3).reshape(width, -1)

    projected = pl.pallas_call(
        project_kernel,
        grid=(fr_count,),
        in_specs=[
            pl.BlockSpec(memory_space=pltpu.SMEM),
            pl.BlockSpec((1, patch_count, width), lambda j: (j, 0, 0)),
            pl.BlockSpec((1, patch_count, width), lambda j: (j, 0, 0)),
            pl.BlockSpec((width, 384), lambda j: (0, 0)),
        ],
        out_specs=pl.BlockSpec((chips, 17, 8, 128), lambda j: (0, 0, 0, 0)),
        out_shape=jax.ShapeDtypeStruct((chips, 17, 8, 128), BF16),
        scratch_shapes=[pltpu.VMEM((patch_count, 128), F32)],
        compiler_params=params(),
        name="project",
    )(core.reshape(1), normed, normed_other, mine)
    tracks = lax.all_to_all(projected, CHIP, 0, 0, tiled=True)

    out_rows = lax.all_gather(mine[:, 288:].T, ("c", "pool"), axis=0, tiled=False)

    attended = pl.pallas_call(
        attend_kernel,
        out_shape=jax.ShapeDtypeStruct((chips, 6, 8, 128), BF16),
        scratch_shapes=[pltpu.VMEM((chips, 64, 128), F32)] * 4,
        compiler_params=params(),
        name="attend",
    )(tracks)
    returned = lax.all_to_all(attended, CHIP, 0, 0, tiled=True)

    pair = jnp.where(
        core == 0,
        jnp.concatenate([owners, owners_other]),
        jnp.concatenate([owners_other, owners]),
    )
    packed = pl.pallas_call(
        pack_kernel,
        in_specs=[
            pl.BlockSpec(memory_space=pltpu.SMEM),
            pl.BlockSpec(memory_space=pltpu.VMEM),
        ],
        out_specs=pl.BlockSpec(memory_space=pltpu.VMEM),
        out_shape=jax.ShapeDtypeStruct((sources, 3 * chips // 4, 8, 128), BF16),
        compiler_params=params(),
        name="pack",
    )(pair, returned)
    gathered = lax.all_to_all(packed, ("c", "pool"), 0, 0, tiled=True)

    match = (owners == position) & (slots == 0)
    chosen = jnp.sum(jnp.where(match, jnp.arange(fr_count, dtype=jnp.int32), 0))
    pick = jnp.stack([chosen, jnp.any(match).astype(jnp.int32)])
    groups = width // GROUP
    return pl.pallas_call(
        deliver_kernel,
        grid_spec=pltpu.PrefetchScalarGridSpec(
            num_scalar_prefetch=1,
            grid=(1,),
            in_specs=[
                pl.BlockSpec((1, patch_count, width), lambda g, pick: (pick[0], 0, 0)),
                pl.BlockSpec(gathered.shape, lambda g, pick: (0, 0, 0, 0)),
                pl.BlockSpec(out_rows.shape, lambda g, pick: (0, 0, 0)),
            ],
            out_specs=[
                pl.BlockSpec((1, patch_count, width), lambda g, pick: (0, 0, 0)),
                pl.BlockSpec((1, groups, patch_count), lambda g, pick: (0, 0, 0)),
            ],
        ),
        out_shape=[
            jax.ShapeDtypeStruct((1, patch_count, width), BF16),
            jax.ShapeDtypeStruct((1, groups, patch_count), BF16),
        ],
        compiler_params=params(),
        name="deliver",
    )(pick, frames_in, gathered, out_rows)


def solution(mesh):
    fine = Mesh(mesh.devices.reshape(4, 2, 4, 2, 8), ("zh", "zl", "x", "c", "pool"))
    run = jax.shard_map(
        local,
        mesh=fine,
        in_specs=(
            P(FRAME, None, None),
            P(FRAME, None, "pool"),
            P("pool", FRAME),
            P(FRAME),
            P(FRAME),
        ),
        out_specs=(P(FRAME + ("pool",), None, None), P(FRAME + ("pool",), None, None)),
        check_vma=False,
    )

    def whole(*args):
        shipped, scales = run(*args)
        return shipped, scales

    return whole
```

time: 382 us -> 174 us (0.46)
  waiting for transfers between devices: 198 us -> 42.9 us
  blocking collectives: 81.3 us -> 55.4 us
  local copies, waits for them, and re-layouts: 33.3 us -> 14.2 us
  matrix products: 18.6 us -> 0 us
  Pallas kernels: 0 us -> 11.5 us
  other arithmetic: 11.1 us -> 4.17 us
  starting transfers between devices: 24.2 us -> 29.9 us
    all_gather x2 -> x1, waiting for transfers between devices: 116 us -> 0.01 us  [local(): lax.all_gather(mine[:, 288:].T, ('c', 'pool'), axis=0, tiled=False)]
    all_gather x2 -> x1, blocking collectives: 81.3 us -> 8.39 us  [local(): both = lax.all_gather(payload, 'c', axis=0, tiled=True)]
    all_to_all x0 -> x2, blocking collectives: none -> 47 us  [the longest x1 35.1 us: local(): tracks = lax.all_to_all(projected, CHIP, 0, 0, tiled=True)]
    reduce_scatter x1 -> x0, waiting for transfers between devices: 42.9 us -> none  [local(): lax.psum_scatter(partial_value.astype(jnp.bfloat16), 'pool', scatter_dime...]
    dot_general x5 -> x0, matrix products: 15.2 us -> none  [the longest x1 4.57 us: local(): jnp.einsum('td,dkc->tkc', tokens, lax.all_gather(qkv_weight, 'frame', axi...]
    pallas_call x0 -> x4, Pallas kernels: none -> 11.5 us  [the longest x1 4.22 us: local(): pl.pallas_call(deliver_kernel, grid_spec=pltpu.PrefetchScalarGridSpec(num...]
    convert_element_type x6 -> x0, local copies, waits for them, and re-layouts: 10.7 us -> none  [the longest x2 4.12 us: local(): projected[:, 2, :].astype(jnp.bfloat16)]
    ppermute x0 -> x2, starting transfers between devices: none -> 10.2 us  [the longest x1 6.47 us: local(): normed_other = lax.ppermute(normed, 'c', swap)]
  transfers between devices with their start and end apart: 7 -> 6, of which waited for: 6 -> 5; matrix products, arithmetic and copies ran while one was open for 6% -> 2% of each run, Pallas kernels for 0% -> 4%
where the time goes in v1:
time: 174 us; the launch traced here: 173 us
  blocking collectives  55.4 us (32%)
  waiting for transfers between devices  42.9 us (25%)
  starting transfers between devices  29.9 us (17%)
  between operations  14.9 us (9%)
  local copies, waits for them, and re-layouts  14.2 us (8%)
  Pallas kernels  11.5 us (7%)
  other arithmetic  4.17 us (2%)
    all_to_all x1, blocking collectives, local(): tracks = lax.all_to_all(projected, CHIP, 0, 0, tiled=True)  35.1 us
    all_to_all x1, waiting for transfers between devices, local(): gathered = lax.all_to_all(packed, ('c', 'pool'), 0, 0, tiled=True)  18.7 us
    all_to_all x1, blocking collectives, spread(): return lax.all_to_all(copies, axis, 0, 0, tiled=True)  11.9 us
    all_to_all x1, starting transfers between devices, local(): gathered = lax.all_to_all(packed, ('c', 'pool'), 0, 0, tiled=True)  10.5 us
    all_to_all x1, waiting for transfers between devices, spread(): return lax.all_to_all(copies, axis, 0, 0, tiled=True)  10.2 us
    all_gather x1, blocking collectives, local(): both = lax.all_gather(payload, 'c', axis=0, tiled=True)  8.39 us
    all_to_all x1, waiting for transfers between devices, local(): returned = lax.all_to_all(attended, CHIP, 0, 0, tiled=True)  8.24 us
    ppermute x1, starting transfers between devices, local(): normed_other = lax.ppermute(normed, 'c', swap)  6.47 us
  transfers between devices with their start and end apart: 6, of which 5 were waited for; matrix products, arithmetic and copies ran while one was open for 2% of the time, Pallas kernels for 4%

profile of v1, /device:TPU:1, one launch (start us, length us, event | category | flops | bytes accessed | tf_op | source)
XLA Modules:
  0.0 172.9 jit_solution(12352787030086035807)
XLA Ops:
  7.2 1.0 reshape.35
  9.4 8.4 %all_gather.9 = bf16[44,2,384]{2,1,0:T(2,128)(2,1)S(1)} all-gather(bf16[22,2,384]{2,1,0:T(2,128)(2,1)S(1)} %concatenate.12), channel_id=1, replica_groups=mesh['zh'=4,'zl'=2,'x'=4,'c'=2,'pool'=8] {'c'}, dimensions={0}, use_global_device_ids=true | all-gather | bytes 101376 | tf_op jit(solution)/shard_map/all_gather | solution.py:216
  17.9 11.9 %all_to_all.25 = bf16[4,44,384]{2,1,0:T(8,128)(2,1)S(1)} all-to-all(bf16[4,44,384]{2,1,0:T(8,128)(2,1)S(1)} %broadcast_in_dim.28), channel_id=1, replica_groups=mesh['zh'=4,'zl'=2,'x'=4,'c'=2,'pool'=8] {'zh'}, dimensions={0} | all-to-all | bytes 270336 | tf_op jit(solution)/shard_map/all_to_all | solution.py:36
  29.8 1.1 broadcast_in_dim.30
  31.0 4.9 %all-to-all-start.1 = ((bf16[8,176,384]{2,1,0:T(8,128)(2,1)}), bf16[8,176,384]{2,1,0:T(8,128)(2,1)}, u32[]{:S(2)}, u32[]{:S(2)}) async-start(bf16[8,176,384]{2,1,0:T(8,128)(2,1)} %broadcast_in_dim.30), calls=%async_computation.1 | async-start | bytes 2162688 | tf_op jit(solution)/shard_map/all_to_all | solution.py:36
  36.4 0.9 fusion.2
  37.3 10.2 %all-to-all-done.1 = bf16[8,176,384]{2,1,0:T(8,128)(2,1)} async-done(((bf16[8,176,384]{2,1,0:T(8,128)(2,1)}), bf16[8,176,384]{2,1,0:T(8,128)(2,1)}, u32[]{:S(2)}, u32[]{:S(2)}) %all-to-all-start.1) | async-done | bytes 1081376 | tf_op jit(solution)/shard_map/all_to_all | solution.py:36
  47.5 1.5 copy.13
  49.0 1.2 copy.14
  50.2 2.2 %reshape.38.weight_ref = bf16[1408,384]{1,0:T(8,128)(2,1)} reshape(bf16[4,8,44,384]{3,2,1,0:T(8,128)(2,1)} %copy.14) | data formatting | bytes 2162688 | tf_op jit(solution)/shard_map/reshape | solution.py:220
  52.3 1.1 slice_bitcast_fusion
  53.5 0.9 copy.15
  55.2 6.5 %collective-permute-start.1 = (bf16[4,256,1408]{2,1,0:T(8,128)(2,1)S(1)}, bf16[4,256,1408]{2,1,0:T(8,128)(2,1)S(1)}, u32[]{:S(2)}, u32[]{:S(2)}) collective-permute-start(bf16[4,256,1408]{2,1,0:T(8,128)(2,1)S(1)} %fusion.3.own_ref), channel_id=1, source_target_pairs={{0,8},{8,0},{1,9},{9,1},{2,10},{10,2},{3,11},{11,3},{4,12},{12,4},... | collective-permute-start | bytes 8650760 | tf_op jit(solution)/shard_map/ppermute | solution.py:196
  61.7 4.9 %collective-permute-done.1.other_ref = bf16[4,256,1408]{2,1,0:T(8,128)(2,1)S(1)} collective-permute-done((bf16[4,256,1408]{2,1,0:T(8,128)(2,1)S(1)}, bf16[4,256,1408]{2,1,0:T(8,128)(2,1)S(1)}, u32[]{:S(2)}, u32[]{:S(2)}) %collective-permute-start.1) | collective-permute-done | bytes 2883616 | tf_op jit(solution)/shard_map/ppermute | solution.py:196
  66.6 4.1 %project.1 = bf16[32,17,8,128]{3,2,1,0:T(8,128)(2,1)S(1)} custom-call(s32[1]{0:T(128)} %bitcast.2.core_ref, bf16[4,256,1408]{2,1,0:T(8,128)(2,1)S(1)} %fusion.3.own_ref, bf16[4,256,1408]{2,1,0:T(8,128)(2,1)S(1)} %collective-permute-done.1.other_ref, bf16[1408,384]{1,0:T(8,128)(2,1)S(1)} %copy-done.1), custom_call_target="tpu_custom_call" | custom-call | tf_op jit(solution)/shard_map/project/pallas_call | solution.py:222
  70.7 35.1 %all_to_all.26.x_ref = bf16[32,17,8,128]{3,2,1,0:T(8,128)(2,1)S(1)} all-to-all(bf16[32,17,8,128]{3,2,1,0:T(8,128)(2,1)S(1)} %project.1), channel_id=1, replica_groups=mesh['zh'=4,'zl'=2,'x'=4,'c'=2,'pool'=8] {'zh','zl','x'}, dimensions={0} | all-to-all | bytes 2228224 | tf_op jit(solution)/shard_map/all_to_all | solution.py:237
  105.8 2.3 %attend.1 = bf16[32,6,8,128]{3,2,1,0:T(8,128)(2,1)S(1)} custom-call(bf16[32,17,8,128]{3,2,1,0:T(8,128)(2,1)S(1)} %all_to_all.26.x_ref), custom_call_target="tpu_custom_call" | custom-call | tf_op jit(solution)/shard_map/attend/pallas_call | solution.py:241
  108.9 4.3 %all-to-all-start.3 = ((bf16[32,6,8,128]{3,2,1,0:T(8,128)(2,1)}), bf16[32,6,8,128]{3,2,1,0:T(8,128)(2,1)S(1)}, u32[]{:S(2)}, u32[]{:S(2)}) async-start(bf16[32,6,8,128]{3,2,1,0:T(8,128)(2,1)} %copy-done.4), calls=%async_computation.3 | async-start | bytes 786432 | tf_op jit(solution)/shard_map/all_to_all | solution.py:248
  113.1 3.7 %collective-permute-start = (s32[4]{0:T(128)S(1)}, s32[4]{0:T(128)S(1)}, u32[]{:S(2)}, u32[]{:S(2)}) collective-permute-start(s32[4]{0:T(128)S(1)} %copy-done.5), channel_id=1, source_target_pairs={{0,8},{8,0},{1,9},{9,1},{2,10},{10,2},{3,11},{11,3},{4,12},{12,4},... | collective-permute-start | bytes 56 | tf_op jit(solution)/shard_map/ppermute | solution.py:197
  117.7 8.2 %all-to-all-done.3.x_ref = bf16[32,6,8,128]{3,2,1,0:T(8,128)(2,1)S(1)} async-done(((bf16[32,6,8,128]{3,2,1,0:T(8,128)(2,1)}), bf16[32,6,8,128]{3,2,1,0:T(8,128)(2,1)S(1)}, u32[]{:S(2)}, u32[]{:S(2)}) %all-to-all-start.3) | async-done | bytes 393248 | tf_op jit(solution)/shard_map/all_to_all | solution.py:248
  127.8 10.5 %all-to-all-start.4 = ((bf16[16,24,8,128]{3,2,1,0:T(8,128)(2,1)}), bf16[16,24,8,128]{3,2,1,0:T(8,128)(2,1)}, u32[]{:S(2)}, u32[]{:S(2)}) async-start(bf16[16,24,8,128]{3,2,1,0:T(8,128)(2,1)} %copy-done.3), calls=%async_computation.4 | async-start | bytes 1572864 | tf_op jit(solution)/shard_map/all_to_all | solution.py:266
  140.9 18.7 %all-to-all-done.4.y_ref = bf16[16,24,8,128]{3,2,1,0:T(8,128)(2,1)} async-done(((bf16[16,24,8,128]{3,2,1,0:T(8,128)(2,1)}), bf16[16,24,8,128]{3,2,1,0:T(8,128)(2,1)}, u32[]{:S(2)}, u32[]{:S(2)}) %all-to-all-start.4) | async-done | bytes 786464 | tf_op jit(solution)/shard_map/all_to_all | solution.py:266
  159.6 2.2 %copy-done.2 = bf16[1536,1408]{1,0:T(8,128)(2,1)S(1)} copy-done((bf16[1536,1408]{1,0:T(8,128)(2,1)S(1)}, bf16[1536,1408]{1,0:T(8,128)(2,1)}, u32[]{:S(2)}) %copy-start.2) | copy-done | bytes 4325400
  161.8 4.2 %deliver.1 = (bf16[1,256,1408]{2,1,0:T(8,128)(2,1)}, bf16[1,11,256]{2,1,0:T(8,128)(2,1)}) custom-call(s32[2]{0:T(128)S(1)} %pad_add_fusion.pick_ref, bf16[4,256,1408]{2,1,0:T(8,128)(2,1)S(1)} %copy-done, bf16[16,24,8,128]{3,2,1,0:T(8,128)(2,1)} %all-to-all-done.4.y_ref, bf16[16,96,1408]{2,1,0:T(8,128)(2,1)S(1)} %bitcast.22), custom_call_target="tpu_custom_call" | custom-call | tf_op jit(solution)/shard_map/deliver/pallas_call | solution.py:272
  (36 shorter events, 7.9 us)
Async XLA Ops:
  7.2 28.8 %copy-start = (bf16[4,256,1408]{2,1,0:T(8,128)(2,1)S(1)}, bf16[4,256,1408]{2,1,0:T(8,128)(2,1)}, u32[]{:S(2)}) copy-start(bf16[4,256,1408]{2,1,0:T(8,128)(2,1)} %frame_ref.1) | copy-start | bytes 8650756
  31.0 16.6 %all-to-all-start.1 = ((bf16[8,176,384]{2,1,0:T(8,128)(2,1)}), bf16[8,176,384]{2,1,0:T(8,128)(2,1)}, u32[]{:S(2)}, u32[]{:S(2)}) async-start(bf16[8,176,384]{2,1,0:T(8,128)(2,1)} %broadcast_in_dim.30), calls=%async_computation.1 | async-start | bytes 2162688 | tf_op jit(solution)/shard_map/all_to_all | solution.py:36
  35.9 123.7 %all-gather.3.cloned.1.call-start = ((), (), s32[]{:S(2)}) async-start(), calls=%async_computation.5 | async-start | bytes 4595712 | tf_op jit(solution)/shard_map/all_gather | solution.py:239
  54.4 12.1 %copy-start.1 = (bf16[1408,384]{1,0:T(8,128)(2,1)S(1)}, bf16[1408,384]{1,0:T(8,128)(2,1)}, u32[]{:S(2)}) copy-start(bf16[1408,384]{1,0:T(8,128)(2,1)} %reshape.38.weight_ref) | copy-start | bytes 3244036
  55.2 11.4 %collective-permute-start.1 = (bf16[4,256,1408]{2,1,0:T(8,128)(2,1)S(1)}, bf16[4,256,1408]{2,1,0:T(8,128)(2,1)S(1)}, u32[]{:S(2)}, u32[]{:S(2)}) collective-permute-start(bf16[4,256,1408]{2,1,0:T(8,128)(2,1)S(1)} %fusion.3.own_ref), channel_id=1, source_target_pairs={{0,8},{8,0},{1,9},{9,1},{2,10},{10,2},{3,11},{11,3},{4,12},{12,4},... | collective-permute-start | bytes 8650760 | tf_op jit(solution)/shard_map/ppermute | solution.py:196
  70.7 42.5 %copy-start.5 = (s32[4]{0:T(128)S(1)}, s32[4]{0:T(128)}, u32[]{:S(2)}) copy-start(s32[4]{0:T(128)} %param.8) | copy-start | bytes 52
  105.8 32.4 %copy-start.6 = (s32[4]{0:T(128)S(1)}, s32[4]{0:T(128)}, u32[]{:S(2)}) copy-start(s32[4]{0:T(128)} %param.9) | copy-start | bytes 52
  108.1 0.7 copy-start.4
  108.9 17.1 %all-to-all-start.3 = ((bf16[32,6,8,128]{3,2,1,0:T(8,128)(2,1)}), bf16[32,6,8,128]{3,2,1,0:T(8,128)(2,1)S(1)}, u32[]{:S(2)}, u32[]{:S(2)}) async-start(bf16[32,6,8,128]{3,2,1,0:T(8,128)(2,1)} %copy-done.4), calls=%async_computation.3 | async-start | bytes 786432 | tf_op jit(solution)/shard_map/all_to_all | solution.py:248
  113.1 4.5 %collective-permute-start = (s32[4]{0:T(128)S(1)}, s32[4]{0:T(128)S(1)}, u32[]{:S(2)}, u32[]{:S(2)}) collective-permute-start(s32[4]{0:T(128)S(1)} %copy-done.5), channel_id=1, source_target_pairs={{0,8},{8,0},{1,9},{9,1},{2,10},{10,2},{3,11},{11,3},{4,12},{12,4},... | collective-permute-start | bytes 56 | tf_op jit(solution)/shard_map/ppermute | solution.py:197
  126.9 0.9 copy-start.3
  127.8 31.8 %all-to-all-start.4 = ((bf16[16,24,8,128]{3,2,1,0:T(8,128)(2,1)}), bf16[16,24,8,128]{3,2,1,0:T(8,128)(2,1)}, u32[]{:S(2)}, u32[]{:S(2)}) async-start(bf16[16,24,8,128]{3,2,1,0:T(8,128)(2,1)} %copy-done.3), calls=%async_computation.4 | async-start | bytes 1572864 | tf_op jit(solution)/shard_map/all_to_all | solution.py:266
  159.6 2.2 %copy-start.2 = (bf16[1536,1408]{1,0:T(8,128)(2,1)S(1)}, bf16[1536,1408]{1,0:T(8,128)(2,1)}, u32[]{:S(2)}) copy-start(bf16[1536,1408]{1,0:T(8,128)(2,1)} %all-gather.3.cloned.1.call-done) | copy-start | bytes 12976132
Sparse Core Ops, SparseCore 0:
  54.5 45.7 all-gather.2

commit v2 on v1

--- a/solution.py
+++ b/solution.py
@@ -14,7 +14,6 @@
 FACTOR = 1.0 / HEAD_DIM**0.5
 CHIP = ("zh", "zl", "x")
 FRAME = CHIP + ("c",)
-VMEM_LIMIT = 40 * 1024 * 1024
 F32 = jnp.float32
 BF16 = jnp.bfloat16
 
@@ -36,23 +35,35 @@
     return lax.all_to_all(copies, axis, 0, 0, tiled=True)
 
 
-def project_kernel(core_ref, own_ref, other_ref, weight_ref, out_ref, rest_ref):
+def project_kernel(
+    core_ref, own_ref, other_ref, weight_ref, out_ref, back_ref, rest_ref, order_ref, right_ref
+):
     step = pl.program_id(0)
     core = core_ref[0]
     chips = out_ref.shape[0]
+    inner, height = weight_ref.shape[:2]
+    outer = 4
+    rows = height // outer
 
     @pl.when(step == 0)
     def _():
         rest_ref[...] = jnp.zeros_like(rest_ref)
+        for low in range(inner):
+            block = weight_ref[low].astype(F32)
+            for high in range(outer):
+                start = (high * inner + low) * rows
+                order_ref[start : start + rows, :] = block[high * rows : (high + 1) * rows]
+        right_ref[...] = order_ref[...].astype(BF16)
+        back_ref[...] = order_ref[:, 256:384].T[32:].astype(BF16)
 
     lane = lanes_of(rest_ref.shape)
     for which, ref in enumerate((own_ref, other_ref)):
         frame = (core if which == 0 else 1 - core) * 4 + step
-        rows = jnp.dot(ref[0], weight_ref[...], preferred_element_type=F32)
+        out = jnp.dot(ref[0], right_ref[...], preferred_element_type=F32)
         for tile in range(2):
-            block = rows[:, tile * 128 : (tile + 1) * 128].astype(BF16)
+            block = out[:, tile * 128 : (tile + 1) * 128].astype(BF16)
             out_ref[:, 2 * frame + tile] = block.reshape(chips, 8, 128)
-        rest = jnp.where(lane < 8, rows[:, 256:384], 0.0)
+        rest = jnp.where(lane < 8, out[:, 256:384], 0.0)
         rest_ref[...] += pltpu.roll(rest, 8 * frame, 1)
 
     @pl.when(step == pl.num_programs(0) - 1)
@@ -105,7 +116,7 @@
         out_ref[:, 4 + tile] = packed.astype(BF16)
 
 
-def pack_kernel(owner_ref, x_ref, out_ref):
+def pack_kernel(owner_ref, x_ref, ready_ref, out_ref):
     chips = x_ref.shape[0]
     half, quarter = chips // 2, chips // 4
     out_ref[...] = jnp.zeros_like(out_ref)
@@ -126,9 +137,19 @@
         out_ref[place, half:] = packed.astype(BF16)
 
 
-def deliver_kernel(pick_ref, frame_ref, y_ref, weight_ref, out_ref, scale_ref):
+def deliver_kernel(pick_ref, frame_ref, y_ref, far_ref, out_ref, scale_ref, weight_ref, sems):
     sources = y_ref.shape[0]
     patches, width = frame_ref.shape[1:]
+    chunks = [(start, min(start + 256, width)) for start in range(0, width, 256)]
+    copies = []
+    for index, (start, stop) in enumerate(chunks):
+        columns = pl.ds(start, stop - start)
+        copies.append(
+            pltpu.make_async_copy(
+                far_ref.at[:, :, columns], weight_ref.at[:, :, columns], sems.at[index]
+            )
+        )
+        copies[-1].start()
     half, quarter = patches // 2, patches // 4
     tiles = half // 8
     valid = pick_ref[1] > 0
@@ -157,8 +178,8 @@
     left_rest = jnp.concatenate(rests, axis=1)
     lane_p = lanes_of((patches, 128))
     scales = jnp.zeros((patches, 128), F32)
-    for start in range(0, width, 256):
-        stop = min(start + 256, width)
+    for copy, (start, stop) in zip(copies, chunks):
+        copy.wait()
         right = weight_ref[:, :MAIN, start:stop].reshape(sources * MAIN, stop - start)
         right_rest = weight_ref[:, MAIN:, start:stop].reshape(sources * SLOT, stop - start)
         total = jnp.dot(left, right, preferred_element_type=F32)
@@ -175,8 +196,16 @@
     scale_ref[0] = scales[: width // GROUP].astype(BF16)
 
 
-def params():
-    return pltpu.CompilerParams(vmem_limit_bytes=VMEM_LIMIT)
+def normalise(frames):
+    xf = frames.astype(F32)
+    mean = jnp.mean(xf, axis=-1, keepdims=True)
+    centred = xf - mean
+    var = jnp.mean(centred * centred, axis=-1, keepdims=True)
+    return (centred * lax.rsqrt(var + 1e-06)).astype(BF16)
+
+
+def params(mebibytes):
+    return pltpu.CompilerParams(vmem_limit_bytes=mebibytes * 1024 * 1024)
 
 
 def local(frames_in, qkv_weight, out_weight, owners, slots):
@@ -188,12 +217,8 @@
     sources = 2 * lax.axis_size("pool")
     swap = [(0, 1), (1, 0)]
 
-    xf = frames_in.astype(F32)
-    mean = jnp.mean(xf, axis=-1, keepdims=True)
-    centred = xf - mean
-    var = jnp.mean(centred * centred, axis=-1, keepdims=True)
-    normed = (centred * lax.rsqrt(var + 1e-06)).astype(BF16)
-    normed_other = lax.ppermute(normed, "c", swap)
+    normed = normalise(frames_in)
+    normed_other = normalise(lax.ppermute(frames_in, "c", swap))
     owners_other = lax.ppermute(owners, "c", swap)
 
     parts = qkv_weight.reshape(rows_here, 3, 2, HEAD_DIM)
@@ -217,32 +242,40 @@
     mine = lax.dynamic_index_in_dim(both, core, 1, keepdims=False)
     mine = spread(mine, "zh").reshape(-1, mine.shape[-1])
     mine = spread(mine, ("zl", "x"))
-    mine = mine.reshape(8, 4, 2 * rows_here, -1).transpose(1, 0, 2, 3).reshape(width, -1)
-
-    projected = pl.pallas_call(
+    projected, back = pl.pallas_call(
         project_kernel,
         grid=(fr_count,),
         in_specs=[
             pl.BlockSpec(memory_space=pltpu.SMEM),
             pl.BlockSpec((1, patch_count, width), lambda j: (j, 0, 0)),
             pl.BlockSpec((1, patch_count, width), lambda j: (j, 0, 0)),
-            pl.BlockSpec((width, 384), lambda j: (0, 0)),
-        ],
-        out_specs=pl.BlockSpec((chips, 17, 8, 128), lambda j: (0, 0, 0, 0)),
-        out_shape=jax.ShapeDtypeStruct((chips, 17, 8, 128), BF16),
-        scratch_shapes=[pltpu.VMEM((patch_count, 128), F32)],
-        compiler_params=params(),
+            pl.BlockSpec(mine.shape, lambda j: (0, 0, 0)),
+        ],
+        out_specs=[
+            pl.BlockSpec((chips, 17, 8, 128), lambda j: (0, 0, 0, 0)),
+            pl.BlockSpec((96, width), lambda j: (0, 0)),
+        ],
+        out_shape=[
+            jax.ShapeDtypeStruct((chips, 17, 8, 128), BF16),
+            jax.ShapeDtypeStruct((96, width), BF16),
+        ],
+        scratch_shapes=[
+            pltpu.VMEM((patch_count, 128), F32),
+            pltpu.VMEM((width, 384), F32),
+            pltpu.VMEM((width, 384), BF16),
+        ],
+        compiler_params=params(60),
         name="project",
     )(core.reshape(1), normed, normed_other, mine)
     tracks = lax.all_to_all(projected, CHIP, 0, 0, tiled=True)
 
-    out_rows = lax.all_gather(mine[:, 288:].T, ("c", "pool"), axis=0, tiled=False)
+    out_rows = lax.all_gather(back, ("c", "pool"), axis=0, tiled=False)
 
     attended = pl.pallas_call(
         attend_kernel,
         out_shape=jax.ShapeDtypeStruct((chips, 6, 8, 128), BF16),
         scratch_shapes=[pltpu.VMEM((chips, 64, 128), F32)] * 4,
-        compiler_params=params(),
+        compiler_params=params(60),
         name="attend",
     )(tracks)
     returned = lax.all_to_all(attended, CHIP, 0, 0, tiled=True)
@@ -257,12 +290,13 @@
         in_specs=[
             pl.BlockSpec(memory_space=pltpu.SMEM),
             pl.BlockSpec(memory_space=pltpu.VMEM),
+            pl.BlockSpec(memory_space=pltpu.VMEM),
         ],
         out_specs=pl.BlockSpec(memory_space=pltpu.VMEM),
         out_shape=jax.ShapeDtypeStruct((sources, 3 * chips // 4, 8, 128), BF16),
-        compiler_params=params(),
+        compiler_params=params(60),
         name="pack",
-    )(pair, returned)
+    )(pair, returned, out_rows[0, :16, :128])
     gathered = lax.all_to_all(packed, ("c", "pool"), 0, 0, tiled=True)
 
     match = (owners == position) & (slots == 0)
@@ -277,18 +311,22 @@
             in_specs=[
                 pl.BlockSpec((1, patch_count, width), lambda g, pick: (pick[0], 0, 0)),
                 pl.BlockSpec(gathered.shape, lambda g, pick: (0, 0, 0, 0)),
-                pl.BlockSpec(out_rows.shape, lambda g, pick: (0, 0, 0)),
+                pl.BlockSpec(memory_space=pltpu.HBM),
             ],
             out_specs=[
                 pl.BlockSpec((1, patch_count, width), lambda g, pick: (0, 0, 0)),
                 pl.BlockSpec((1, groups, patch_count), lambda g, pick: (0, 0, 0)),
             ],
+            scratch_shapes=[
+                pltpu.VMEM(out_rows.shape, BF16),
+                pltpu.SemaphoreType.DMA((-(-width // 256),)),
+            ],
         ),
         out_shape=[
             jax.ShapeDtypeStruct((1, patch_count, width), BF16),
             jax.ShapeDtypeStruct((1, groups, patch_count), BF16),
         ],
-        compiler_params=params(),
+        compiler_params=params(60),
         name="deliver",
     )(pick, frames_in, gathered, out_rows)
 

time: 174 us -> 172 us (0.989)
  other arithmetic: 4.17 us -> 17.8 us
  waiting for transfers between devices: 42.9 us -> 29.5 us
  blocking collectives: 55.4 us -> 42.2 us
  Pallas kernels: 11.5 us -> 22 us
  starting transfers between devices: 29.9 us -> 37.3 us
  local copies, waits for them, and re-layouts: 14.2 us -> 6.85 us
    all_to_all x1 -> x0, blocking collectives: 11.9 us -> none  [spread(): return lax.all_to_all(copies, axis, 0, 0, tiled=True)]
    reduce_sum x2 -> x4, other arithmetic: 1.36 us -> 8.15 us  [the longest x2 4.53 us: normalise(): mean = jnp.mean(xf, axis=-1, keepdims=True)]
    all_to_all x1 -> x2, waiting for transfers between devices: 10.2 us -> 4.23 us  [spread(): return lax.all_to_all(copies, axis, 0, 0, tiled=True)]
    convert_element_type x1 -> x2, other arithmetic: 0.74 us -> 6.49 us  [normalise(): return (centred * lax.rsqrt(var + 1e-06)).astype(BF16)]
    all_gather x1, blocking collectives: 8.39 us -> 2.84 us  [local(): both = lax.all_gather(payload, 'c', axis=0, tiled=True)]
    ppermute x1, waiting for transfers between devices: 4.89 us -> 0.01 us  [local(): normed_other = normalise(lax.ppermute(frames_in, 'c', swap))]
    all_to_all x1 -> x2, starting transfers between devices: 4.91 us -> 9.53 us  [spread(): return lax.all_to_all(copies, axis, 0, 0, tiled=True)]
    all_to_all x1, blocking collectives: 35.1 us -> 39.4 us  [local(): tracks = lax.all_to_all(projected, CHIP, 0, 0, tiled=True)]
  transfers between devices with their start and end apart: 6 -> 7, of which waited for: 5 -> 4; matrix products, arithmetic and copies ran while one was open for 2% -> 14% of each run, Pallas kernels for 4% -> 3%
where the time goes in v2:
time: 172 us; the launch traced here: 170 us
  blocking collectives  42.2 us (25%)
  starting transfers between devices  37.3 us (22%)
  waiting for transfers between devices  29.5 us (17%)
  Pallas kernels  22 us (13%)
  other arithmetic  17.8 us (10%)
  between operations  14.8 us (9%)
  local copies, waits for them, and re-layouts  6.85 us (4%)
    all_to_all x1, blocking collectives, local(): tracks = lax.all_to_all(projected, CHIP, 0, 0, tiled=True)  39.4 us
    all_to_all x1, waiting for transfers between devices, local(): gathered = lax.all_to_all(packed, ('c', 'pool'), 0, 0, tiled=True)  18 us
    all_to_all x1, starting transfers between devices, local(): gathered = lax.all_to_all(packed, ('c', 'pool'), 0, 0, tiled=True)  10.4 us
    all_to_all x2, starting transfers between devices, spread(): return lax.all_to_all(copies, axis, 0, 0, tiled=True)  9.53 us
    ppermute x1, starting transfers between devices, local(): normed_other = normalise(lax.ppermute(frames_in, 'c', swap))  9.05 us
    pallas_call x1, Pallas kernels, local(): pl.pallas_call(deliver_kernel, grid_spec=pltpu.PrefetchScalarGridSpec(num...  7.92 us
    pallas_call x1, Pallas kernels, local(): pl.pallas_call(project_kernel, grid=(fr_count,), in_specs=[pl.BlockSpec(m...  7.59 us
    convert_element_type x2, other arithmetic, normalise(): return (centred * lax.rsqrt(var + 1e-06)).astype(BF16)  6.49 us
  transfers between devices with their start and end apart: 7, of which 4 were waited for; matrix products, arithmetic and copies ran while one was open for 14% of the time, Pallas kernels for 3%

profile of v2, /device:TPU:1, one launch (start us, length us, event | category | flops | bytes accessed | tf_op | source)
XLA Modules:
  0.0 170.5 jit_solution(18058654853130563831)
XLA Ops:
  7.2 9.1 %collective-permute-start.1 = (bf16[4,256,1408]{2,1,0:T(8,128)(2,1)}, bf16[4,256,1408]{2,1,0:T(8,128)(2,1)}, u32[]{:S(2)}, u32[]{:S(2)}) collective-permute-start(bf16[4,256,1408]{2,1,0:T(8,128)(2,1)} %frame_ref.1), channel_id=1, source_target_pairs={{0,8},{8,0},{1,9},{9,1},{2,10},{10,2},{3,11},{11,3},{4,12},{12,4},... | collective-permute-start | bytes 8650760 | tf_op jit(solution)/shard_map/ppermute | solution.py:221
  18.3 2.8 %all_gather.9 = bf16[44,2,384]{2,1,0:T(2,128)(2,1)S(1)} all-gather(bf16[22,2,384]{2,1,0:T(2,128)(2,1)S(1)} %concatenate.12), channel_id=1, replica_groups=mesh['zh'=4,'zl'=2,'x'=4,'c'=2,'pool'=8] {'c'}, dimensions={0}, use_global_device_ids=true | all-gather | bytes 101376 | tf_op jit(solution)/shard_map/all_gather | solution.py:241
  21.9 4.6 %all-to-all-start = ((bf16[4,44,384]{2,1,0:T(8,128)(2,1)}), bf16[4,44,384]{2,1,0:T(8,128)(2,1)S(1)}, u32[]{:S(2)}, u32[]{:S(2)}) async-start(bf16[4,44,384]{2,1,0:T(8,128)(2,1)} %broadcast_in_dim.30), calls=%async_computation | async-start | bytes 294912 | tf_op jit(solution)/shard_map/all_to_all | solution.py:35
  26.6 2.3 %convert_reduce_fusion.1 = f32[4,256]{1,0:T(4,128)S(1)} fusion(bf16[4,256,1408]{2,1,0:T(8,128)(2,1)} %frame_ref.1), kind=kLoop, calls=%fused_computation.3 | loop fusion | flops 2882560 | bytes 2887680 | tf_op jit(solution)/shard_map/reduce_sum | solution.py:201
  28.9 0.9 fusion.6
  29.8 4.2 %all-to-all-done = bf16[4,44,384]{2,1,0:T(8,128)(2,1)S(1)} async-done(((bf16[4,44,384]{2,1,0:T(8,128)(2,1)}), bf16[4,44,384]{2,1,0:T(8,128)(2,1)S(1)}, u32[]{:S(2)}, u32[]{:S(2)}) %all-to-all-start) | async-done | bytes 135200 | tf_op jit(solution)/shard_map/all_to_all | solution.py:35
  34.0 1.1 broadcast_in_dim.32
  35.1 4.9 %all-to-all-start.1 = ((bf16[8,176,384]{2,1,0:T(8,128)(2,1)}), bf16[8,176,384]{2,1,0:T(8,128)(2,1)}, u32[]{:S(2)}, u32[]{:S(2)}) async-start(bf16[8,176,384]{2,1,0:T(8,128)(2,1)} %broadcast_in_dim.32), calls=%async_computation.1 | async-start | bytes 2162688 | tf_op jit(solution)/shard_map/all_to_all | solution.py:35
  40.1 2.3 %fusion.7.own_ref = bf16[4,256,1408]{2,1,0:T(8,128)(2,1)} fusion(bf16[4,256,1408]{2,1,0:T(8,128)(2,1)S(1)} %copy-done, f32[4,256]{1,0:T(4,128)S(1)} %add_rsqrt_fusion.1, f32[4,256]{1,0:T(4,128)S(1)} %broadcast_multiply_fusion.1), kind=kLoop, calls=%fused_computation.11 | loop fusion | flops 5767168 | bytes 5775360 | tf_op jit(solution)/shard_map/convert_element_type | solution.py:204
  42.4 2.3 %convert_reduce_fusion = f32[4,256]{1,0:T(4,128)S(1)} fusion(bf16[4,256,1408]{2,1,0:T(8,128)(2,1)} %collective-permute-done.1), kind=kLoop, calls=%fused_computation.1 | loop fusion | flops 2882560 | bytes 2887680 | tf_op jit(solution)/shard_map/reduce_sum | solution.py:201
  44.7 2.7 %fusion.4 = f32[4,256]{1,0:T(4,128)S(1)} fusion(bf16[4,256,1408]{2,1,0:T(8,128)(2,1)} %collective-permute-done.1, f32[4,256]{1,0:T(4,128)S(1)} %broadcast_multiply_fusion), kind=kLoop, calls=%fused_computation.8 | loop fusion | flops 5766144 | bytes 2891776 | tf_op jit(solution)/shard_map/reduce_sum | solution.py:203
  47.4 4.2 %fusion.5.other_ref = bf16[4,256,1408]{2,1,0:T(8,128)(2,1)} fusion(bf16[4,256,1408]{2,1,0:T(8,128)(2,1)} %collective-permute-done.1, f32[4,256]{1,0:T(4,128)S(1)} %add_rsqrt_fusion, f32[4,256]{1,0:T(4,128)S(1)} %broadcast_multiply_fusion), kind=kLoop, calls=%fused_computation.9 | loop fusion | flops 5767168 | bytes 5775360 | tf_op jit(solution)/shard_map/convert_element_type | solution.py:204
  51.6 7.6 %project.1 = (bf16[32,17,8,128]{3,2,1,0:T(8,128)(2,1)}, bf16[96,1408]{1,0:T(8,128)(2,1)}) custom-call(s32[1]{0:T(128)} %bitcast.2.core_ref, bf16[4,256,1408]{2,1,0:T(8,128)(2,1)} %fusion.7.own_ref, bf16[4,256,1408]{2,1,0:T(8,128)(2,1)} %fusion.5.other_ref, bf16[8,176,384]{2,1,0:T(8,128)(2,1)} %all-to-all-done.1.weight_ref), custom_call_target="tpu_custom_call" | custom-call | tf_op jit(solution)/shard_map/project/pallas_call | solution.py:245
  59.2 39.4 %all_to_all.25.x_ref = bf16[32,17,8,128]{3,2,1,0:T(8,128)(2,1)} all-to-all(bf16[32,17,8,128]{3,2,1,0:T(8,128)(2,1)} %get-tuple-element.4), channel_id=1, replica_groups=mesh['zh'=4,'zl'=2,'x'=4,'c'=2,'pool'=8] {'zh','zl','x'}, dimensions={0} | all-to-all | bytes 2228224 | tf_op jit(solution)/shard_map/all_to_all | solution.py:270
  98.6 4.3 %attend.1 = bf16[32,6,8,128]{3,2,1,0:T(8,128)(2,1)} custom-call(bf16[32,17,8,128]{3,2,1,0:T(8,128)(2,1)} %all_to_all.25.x_ref), custom_call_target="tpu_custom_call" | custom-call | tf_op jit(solution)/shard_map/attend/pallas_call | solution.py:274
  102.8 4.5 %all-to-all-start.3 = ((bf16[32,6,8,128]{3,2,1,0:T(8,128)(2,1)}), bf16[32,6,8,128]{3,2,1,0:T(8,128)(2,1)S(1)}, u32[]{:S(2)}, u32[]{:S(2)}) async-start(bf16[32,6,8,128]{3,2,1,0:T(8,128)(2,1)} %attend.1), calls=%async_computation.3 | async-start | bytes 786432 | tf_op jit(solution)/shard_map/all_to_all | solution.py:281
  107.3 3.8 %collective-permute-start = (s32[4]{0:T(128)S(1)}, s32[4]{0:T(128)S(1)}, u32[]{:S(2)}, u32[]{:S(2)}) collective-permute-start(s32[4]{0:T(128)S(1)} %copy-done.3), channel_id=1, source_target_pairs={{0,8},{8,0},{1,9},{9,1},{2,10},{10,2},{3,11},{11,3},{4,12},{12,4},... | collective-permute-start | bytes 56 | tf_op jit(solution)/shard_map/ppermute | solution.py:222
  112.6 1.3 slice_bitcast_fusion.3.ready_ref
  113.8 6.4 %all-to-all-done.3.x_ref = bf16[32,6,8,128]{3,2,1,0:T(8,128)(2,1)S(1)} async-done(((bf16[32,6,8,128]{3,2,1,0:T(8,128)(2,1)}), bf16[32,6,8,128]{3,2,1,0:T(8,128)(2,1)S(1)}, u32[]{:S(2)}, u32[]{:S(2)}) %all-to-all-start.3) | async-done | bytes 393248 | tf_op jit(solution)/shard_map/all_to_all | solution.py:281
  121.0 2.2 %pack.1 = bf16[16,24,8,128]{3,2,1,0:T(8,128)(2,1)} custom-call(s32[8]{0:T(128)} %broadcast_select_fusion.owner_ref, bf16[32,6,8,128]{3,2,1,0:T(8,128)(2,1)} %copy-done.2, bf16[16,128]{1,0:T(8,128)(2,1)} %slice_bitcast_fusion.3.ready_ref), custom_call_target="tpu_custom_call" | custom-call | tf_op jit(solution)/shard_map/pack/pallas_call | solution.py:288
  123.2 10.4 %all-to-all-start.4 = ((bf16[16,24,8,128]{3,2,1,0:T(8,128)(2,1)}), bf16[16,24,8,128]{3,2,1,0:T(8,128)(2,1)S(1)}, u32[]{:S(2)}, u32[]{:S(2)}) async-start(bf16[16,24,8,128]{3,2,1,0:T(8,128)(2,1)} %pack.1), calls=%async_computation.4 | async-start | bytes 1572864 | tf_op jit(solution)/shard_map/all_to_all | solution.py:300
  135.5 1.3 pad_add_fusion.pick_ref
  136.8 18.0 %all-to-all-done.4.y_ref = bf16[16,24,8,128]{3,2,1,0:T(8,128)(2,1)S(1)} async-done(((bf16[16,24,8,128]{3,2,1,0:T(8,128)(2,1)}), bf16[16,24,8,128]{3,2,1,0:T(8,128)(2,1)S(1)}, u32[]{:S(2)}, u32[]{:S(2)}) %all-to-all-start.4) | async-done | bytes 786464 | tf_op jit(solution)/shard_map/all_to_all | solution.py:300
  155.7 7.9 %deliver.1 = (bf16[1,256,1408]{2,1,0:T(8,128)(2,1)}, bf16[1,11,256]{2,1,0:T(8,128)(2,1)}) custom-call(s32[2]{0:T(128)} %pad_add_fusion.pick_ref, bf16[4,256,1408]{2,1,0:T(8,128)(2,1)} %frame_ref.1, bf16[16,24,8,128]{3,2,1,0:T(8,128)(2,1)} %copy-done.1, bf16[16,96,1408]{2,1,0:T(8,128)(2,1)} %bitcast.20), custom_call_target="tpu_custom_call" | custom-call | tf_op jit(solution)/shard_map/deliver/pallas_call | solution.py:306
  (34 shorter events, 7.2 us)
Async XLA Ops:
  7.2 21.7 %copy-start = (bf16[4,256,1408]{2,1,0:T(8,128)(2,1)S(1)}, bf16[4,256,1408]{2,1,0:T(8,128)(2,1)}, u32[]{:S(2)}) copy-start(bf16[4,256,1408]{2,1,0:T(8,128)(2,1)} %frame_ref.1) | copy-start | bytes 8650756
  7.2 35.2 %collective-permute-start.1 = (bf16[4,256,1408]{2,1,0:T(8,128)(2,1)}, bf16[4,256,1408]{2,1,0:T(8,128)(2,1)}, u32[]{:S(2)}, u32[]{:S(2)}) collective-permute-start(bf16[4,256,1408]{2,1,0:T(8,128)(2,1)} %frame_ref.1), channel_id=1, source_target_pairs={{0,8},{8,0},{1,9},{9,1},{2,10},{10,2},{3,11},{11,3},{4,12},{12,4},... | collective-permute-start | bytes 8650760 | tf_op jit(solution)/shard_map/ppermute | solution.py:221
  21.9 12.1 %all-to-all-start = ((bf16[4,44,384]{2,1,0:T(8,128)(2,1)}), bf16[4,44,384]{2,1,0:T(8,128)(2,1)S(1)}, u32[]{:S(2)}, u32[]{:S(2)}) async-start(bf16[4,44,384]{2,1,0:T(8,128)(2,1)} %broadcast_in_dim.30), calls=%async_computation | async-start | bytes 294912 | tf_op jit(solution)/shard_map/all_to_all | solution.py:35
  35.1 16.4 %all-to-all-start.1 = ((bf16[8,176,384]{2,1,0:T(8,128)(2,1)}), bf16[8,176,384]{2,1,0:T(8,128)(2,1)}, u32[]{:S(2)}, u32[]{:S(2)}) async-start(bf16[8,176,384]{2,1,0:T(8,128)(2,1)} %broadcast_in_dim.32), calls=%async_computation.1 | async-start | bytes 2162688 | tf_op jit(solution)/shard_map/all_to_all | solution.py:35
  40.0 72.5 %all-gather.3.cloned.1.call-start = ((), (), s32[]{:S(2)}) async-start(), calls=%async_computation.5 | async-start | bytes 4595712 | tf_op jit(solution)/shard_map/all_gather | solution.py:272
  51.6 55.7 %copy-start.3 = (s32[4]{0:T(128)S(1)}, s32[4]{0:T(128)}, u32[]{:S(2)}) copy-start(s32[4]{0:T(128)} %param.8) | copy-start | bytes 52
  59.2 74.4 %copy-start.4 = (s32[4]{0:T(128)S(1)}, s32[4]{0:T(128)}, u32[]{:S(2)}) copy-start(s32[4]{0:T(128)} %param.9) | copy-start | bytes 52
  102.8 17.4 %all-to-all-start.3 = ((bf16[32,6,8,128]{3,2,1,0:T(8,128)(2,1)}), bf16[32,6,8,128]{3,2,1,0:T(8,128)(2,1)S(1)}, u32[]{:S(2)}, u32[]{:S(2)}) async-start(bf16[32,6,8,128]{3,2,1,0:T(8,128)(2,1)} %attend.1), calls=%async_computation.3 | async-start | bytes 786432 | tf_op jit(solution)/shard_map/all_to_all | solution.py:281
  107.3 4.6 %collective-permute-start = (s32[4]{0:T(128)S(1)}, s32[4]{0:T(128)S(1)}, u32[]{:S(2)}, u32[]{:S(2)}) collective-permute-start(s32[4]{0:T(128)S(1)} %copy-done.3), channel_id=1, source_target_pairs={{0,8},{8,0},{1,9},{9,1},{2,10},{10,2},{3,11},{11,3},{4,12},{12,4},... | collective-permute-start | bytes 56 | tf_op jit(solution)/shard_map/ppermute | solution.py:222
  120.2 0.7 copy-start.2
  123.2 31.6 %all-to-all-start.4 = ((bf16[16,24,8,128]{3,2,1,0:T(8,128)(2,1)}), bf16[16,24,8,128]{3,2,1,0:T(8,128)(2,1)S(1)}, u32[]{:S(2)}, u32[]{:S(2)}) async-start(bf16[16,24,8,128]{3,2,1,0:T(8,128)(2,1)} %pack.1), calls=%async_computation.4 | async-start | bytes 1572864 | tf_op jit(solution)/shard_map/all_to_all | solution.py:300
  154.8 0.9 copy-start.1
Sparse Core Ops, SparseCore 0:
  59.3 45.8 all-gather.2

commit v3 on v1

v3 whole, which is shorter than its diff:
```python
import jax
import jax.numpy as jnp
from jax import lax
from jax.experimental import pallas as pl
from jax.experimental.pallas import tpu as pltpu
from jax.sharding import Mesh, PartitionSpec as P

HEAD_DIM = 88
GROUP = 128
MAIN = 64
SLOT = 32
TRACK, PACK, DELIVER = 60, 60, 30
FACTOR = 1.0 / HEAD_DIM**0.5
CHIP = ("zh", "zl", "x")
FRAME = CHIP + ("c",)
F32 = jnp.float32
BF16 = jnp.bfloat16


def lanes_of(shape):
    return lax.broadcasted_iota(jnp.int32, shape, len(shape) - 1)


def turn(value, shift):
    shift = shift % 128
    if shift == 0:
        return value
    return pltpu.roll(value, shift, len(value.shape) - 1)


def spread(value, axis):
    count = lax.axis_size(axis)
    copies = jnp.broadcast_to(value[None], (count,) + value.shape)
    return lax.all_to_all(copies, axis, 0, 0, tiled=True)


def order_rows(source_ref, order_ref):
    inner, height = source_ref.shape[:2]
    outer = 4
    rows = height // outer
    for low in range(inner):
        block = source_ref[low].astype(F32)
        for high in range(outer):
            start = (high * inner + low) * rows
            order_ref[start : start + rows, :] = block[high * rows : (high + 1) * rows]


def track_kernel(
    core_ref, tokens_ref, own_ref, other_ref, out_ref, back_ref, order_ref, right_ref, o_ref
):
    step = pl.program_id(0)
    core = core_ref[0]
    frames = 2 * tokens_ref.shape[1]
    lane = lanes_of((frames, 128))

    @pl.when(step == 0)
    def _():
        for which, ref in enumerate((own_ref, other_ref)):
            order_rows(ref, order_ref)
            right_ref[:, which * 384 : which * 384 + 384] = order_ref[...].astype(BF16)
            if which == 0:
                turned = [order_ref[:, at : at + 128].T[HEAD_DIM:] for at in (0, 128, 256)]
                back_ref[...] = jnp.concatenate(turned, axis=0)[:96].astype(BF16)

    tokens = tokens_ref[...].reshape(frames, tokens_ref.shape[2])
    both = jnp.dot(tokens, right_ref[...], preferred_element_type=F32)
    for which in range(2):
        head = core if which == 0 else 1 - core
        out = both[:, which * 384 : which * 384 + 384]
        query = jnp.where(lane < HEAD_DIM, out[:, :128], 0.0).astype(BF16)
        key = out[:, 128:256].astype(BF16)
        value = jnp.where(lane < HEAD_DIM, out[:, 256:], 0.0).astype(BF16)
        scores = lax.dot_general(query, key, (((1,), (1,)), ((), ())), preferred_element_type=F32)
        top = jnp.max(scores, axis=-1, keepdims=True)
        expo = jnp.exp((scores - top) * FACTOR)
        total = jnp.sum(expo, axis=-1, keepdims=True)
        mixed = jnp.dot(expo.astype(BF16), value, preferred_element_type=F32)
        mixed = (mixed * (1.0 / total)).reshape(frames // 8, 8, 128)
        o_ref[:, pl.ds(head * 4 + step, 8, stride=8), :] = mixed

    @pl.when(step == pl.num_programs(0) - 1)
    def _():
        pairs = frames // 16
        lane_o = lanes_of((pairs, 8, 128))

        def piece_of(side, owner, late, odd):
            start = (side * 4 + owner * 2 + odd) * 8
            return o_ref[late * pairs : (late + 1) * pairs, start : start + 8, :]

        for side in range(2):
            for owner in range(2):
                rest = None
                for late in range(2):
                    even, odd = (piece_of(side, owner, late, at) for at in range(2))
                    main = jnp.where(lane_o < MAIN, even, turn(odd, MAIN))
                    out_ref[:, side, owner * 2 + late] = main.astype(BF16)
                    for at, piece in enumerate((even, odd)):
                        part = late * 2 + at
                        piece = turn(piece, SLOT * part - MAIN)
                        rest = piece if part == 0 else jnp.where(lane_o >= SLOT * part, piece, rest)
                out_ref[:, side, 4 + owner] = rest.astype(BF16)


def half_turn(value):
    return pltpu.roll(value, 4, 1)


def pack_kernel(owner_ref, x_ref, out_ref):
    pairs = x_ref.shape[0]
    out_ref[...] = jnp.zeros_like(out_ref)

    def join(even, odd, lane, edges):
        shape = even[0].shape
        upper = lax.broadcasted_iota(jnp.int32, shape, 1) < 4
        first = jnp.where(upper, even[0], half_turn(odd[0]))
        second = jnp.where(upper, half_turn(even[1]), odd[1])
        return jnp.where(lane < edges, first, second)

    lane = lanes_of((pairs, 8, 128))
    lane_h = lanes_of((pairs // 2, 8, 128))
    for fr in range(8):
        place = (fr // 4) * 8 + owner_ref[fr]
        tiles = [x_ref[:, side, fr // 2].astype(F32) for side in range(2)]
        even, odd = (
            [turn(tile, MAIN * head - MAIN * (fr % 2)) for head in range(2)] for tile in tiles
        )
        out_ref[place, :pairs] = join(even, odd, lane, MAIN).astype(BF16)
        tiles = [x_ref[:, side, 4 + fr // 4].astype(F32) for side in range(2)]
        rests = []
        for half in range(2):
            rows = slice(half * (pairs // 2), (half + 1) * (pairs // 2))
            even, odd = (
                [
                    turn(tile[rows], 2 * SLOT * half + SLOT * head - SLOT * (fr % 4))
                    for head in range(2)
                ]
                for tile in tiles
            )
            rests.append(join(even, odd, lane_h, 2 * SLOT * half + SLOT))
        rest = jnp.where(lane_h < 2 * SLOT, rests[0], rests[1])
        out_ref[place, pairs:] = rest.astype(BF16)


def deliver_kernel(pick_ref, frame_ref, y_ref, first_ref, second_ref, out_ref, scale_ref):
    sources = y_ref.shape[0]
    heads = sources // 2
    patches, width = frame_ref.shape[1:]
    half = patches // 2
    tiles = half // 8
    valid = pick_ref[1] > 0
    lane = lanes_of((half, 128))

    def weave(first, second):
        upper = lax.broadcasted_iota(jnp.int32, first.shape, 1) < 4
        even = jnp.where(upper, first, half_turn(second))
        odd = jnp.where(upper, half_turn(first), second)
        return jnp.stack([even, odd], axis=1).reshape(first.shape[0] * 16, 128)

    mains, rests = [], []
    for at in range(heads):
        pair = [y_ref[core * heads + at, :tiles].astype(F32) for core in range(2)]
        mains.append(weave(*pair).astype(BF16))
    for at in range(0, heads, 2):
        first, second = (
            weave(*(y_ref[core * heads + one, tiles:].astype(F32) for core in range(2)))
            for one in (at, at + 1)
        )
        low = jnp.where(lane < MAIN, first, turn(second, MAIN))
        high = jnp.where(lane < MAIN, turn(first, MAIN), second)
        rests.append(jnp.concatenate([low, high], axis=0).astype(BF16))
    left = jnp.concatenate(mains, axis=1)
    left_rest = jnp.concatenate(rests, axis=1)
    lane_p = lanes_of((patches, 128))
    scales = jnp.zeros((patches, 128), F32)
    for start in range(0, width, 256):
        stop = min(start + 256, width)
        right, right_rest = (
            jnp.concatenate([ref[:, rows, start:stop] for ref in (first_ref, second_ref)], axis=1)
            for rows in (slice(0, MAIN), slice(MAIN, MAIN + SLOT))
        )
        right = right.reshape(heads * 2 * MAIN, stop - start)
        right_rest = right_rest.reshape(heads * 2 * SLOT, stop - start)
        total = jnp.dot(left, right, preferred_element_type=F32)
        total += jnp.dot(left_rest, right_rest, preferred_element_type=F32)
        total += frame_ref[0, :, start:stop].astype(F32)
        for at in range(0, stop - start, GROUP):
            part = total[:, at : at + GROUP]
            top = jnp.max(jnp.abs(part), axis=-1, keepdims=True)
            scale = (top + 1e-06).astype(BF16).astype(F32)
            coded = jnp.where(valid, part / scale, 0.0).astype(BF16)
            out_ref[0, :, start + at : start + at + GROUP] = coded
            scales = jnp.where(lane_p == (start + at) // GROUP, scale, scales)
    scales = jnp.where(valid, scales, 0.0).T
    scale_ref[0] = scales[: width // GROUP].astype(BF16)


def normalise(frames):
    xf = frames.astype(F32)
    mean = jnp.mean(xf, axis=-1, keepdims=True)
    centred = xf - mean
    var = jnp.mean(centred * centred, axis=-1, keepdims=True)
    return (centred * lax.rsqrt(var + 1e-06)).astype(BF16)


def params(mebibytes):
    return pltpu.CompilerParams(vmem_limit_bytes=mebibytes * 1024 * 1024)


def local(frames_in, qkv_weight, out_weight, owners, slots):
    fr_count, patch_count, width = frames_in.shape
    rows_here = qkv_weight.shape[0]
    core = lax.axis_index("c")
    position = lax.axis_index("pool")
    chips = lax.axis_size("zh") * lax.axis_size("zl") * lax.axis_size("x")
    sources = 2 * lax.axis_size("pool")
    swap = [(0, 1), (1, 0)]

    share = frames_in.reshape(2, 2, 2 * chips, 4, width)
    share = lax.dynamic_index_in_dim(share, position % 2, 0, keepdims=False)
    share = lax.dynamic_index_in_dim(share, position // 2, 2, keepdims=False)
    share = normalise(share).transpose(1, 0, 2)
    share = lax.all_to_all(share, FRAME, 0, 0, tiled=True).reshape(4 * chips, width)
    tracks = lax.all_gather(share, "pool", axis=0, tiled=False)
    owners_other = lax.ppermute(owners, "c", swap)

    parts = qkv_weight.reshape(rows_here, 3, 2, HEAD_DIM)
    query, key, value = parts[:, 0], parts[:, 1], parts[:, 2]
    back = out_weight.T.reshape(rows_here, 2, HEAD_DIM)
    payload = jnp.concatenate(
        [
            query,
            back[..., :40],
            key,
            back[..., 40:80],
            value,
            back[..., 80:],
            jnp.zeros((rows_here, 2, 32), BF16),
        ],
        axis=-1,
    )
    both = lax.all_gather(payload, "c", axis=0, tiled=True)
    mine = lax.dynamic_index_in_dim(both, core, 1, keepdims=False)
    mine = spread(mine, "zh").reshape(-1, mine.shape[-1])
    mine = spread(mine, ("zl", "x"))
    mine_other = lax.ppermute(mine, "c", swap)
    attended, back_rows = pl.pallas_call(
        track_kernel,
        grid=(4,),
        in_specs=[
            pl.BlockSpec(memory_space=pltpu.SMEM),
            pl.BlockSpec((2, 4 * chips, width), lambda p: (p, 0, 0)),
            pl.BlockSpec(mine.shape, lambda p: (0, 0, 0)),
            pl.BlockSpec(mine.shape, lambda p: (0, 0, 0)),
        ],
        out_specs=[
            pl.BlockSpec((chips // 2, 2, 6, 8, 128), lambda p: (0, 0, 0, 0, 0)),
            pl.BlockSpec((96, width), lambda p: (0, 0)),
        ],
        out_shape=[
            jax.ShapeDtypeStruct((chips // 2, 2, 6, 8, 128), BF16),
            jax.ShapeDtypeStruct((96, width), BF16),
        ],
        scratch_shapes=[
            pltpu.VMEM((width, 384), F32),
            pltpu.VMEM((width, 768), BF16),
            pltpu.VMEM((chips, 64, 128), F32),
        ],
        compiler_params=params(TRACK),
        name="track",
    )(core.reshape(1), tracks, mine, mine_other)
    attended = attended.reshape(chips, 6, 8, 128)
    out_rows = lax.all_gather(back_rows, "pool", axis=0, tiled=False)

    returned = lax.all_to_all(attended, CHIP, 0, 0, tiled=True)

    pair = jnp.where(
        core == 0,
        jnp.concatenate([owners, owners_other]),
        jnp.concatenate([owners_other, owners]),
    )
    packed = pl.pallas_call(
        pack_kernel,
        in_specs=[
            pl.BlockSpec(memory_space=pltpu.SMEM),
            pl.BlockSpec(memory_space=pltpu.VMEM),
        ],
        out_specs=pl.BlockSpec(memory_space=pltpu.VMEM),
        out_shape=jax.ShapeDtypeStruct((sources, 3 * chips // 4, 8, 128), BF16),
        compiler_params=params(PACK),
        name="pack",
    )(pair, returned.reshape(chips // 2, 2, 6, 8, 128))
    gathered = lax.all_to_all(packed, ("c", "pool"), 0, 0, tiled=True)

    match = (owners == position) & (slots == 0)
    chosen = jnp.sum(jnp.where(match, jnp.arange(fr_count, dtype=jnp.int32), 0))
    pick = jnp.stack([chosen, jnp.any(match).astype(jnp.int32)])
    groups = width // GROUP
    one = 1.0 - packed[0, 0, 0, 0].astype(F32) * 0.0
    near_rows = out_rows * one.astype(BF16)
    far_rows = lax.ppermute(near_rows, "c", swap)
    first_rows = jnp.where(core == 0, near_rows, far_rows)
    second_rows = jnp.where(core == 0, far_rows, near_rows)
    return pl.pallas_call(
        deliver_kernel,
        grid_spec=pltpu.PrefetchScalarGridSpec(
            num_scalar_prefetch=1,
            grid=(1,),
            in_specs=[
                pl.BlockSpec((1, patch_count, width), lambda g, pick: (pick[0], 0, 0)),
                pl.BlockSpec(gathered.shape, lambda g, pick: (0, 0, 0, 0)),
                pl.BlockSpec(out_rows.shape, lambda g, pick: (0, 0, 0)),
                pl.BlockSpec(out_rows.shape, lambda g, pick: (0, 0, 0)),
            ],
            out_specs=[
                pl.BlockSpec((1, patch_count, width), lambda g, pick: (0, 0, 0)),
                pl.BlockSpec((1, groups, patch_count), lambda g, pick: (0, 0, 0)),
            ],
        ),
        out_shape=[
            jax.ShapeDtypeStruct((1, patch_count, width), BF16),
            jax.ShapeDtypeStruct((1, groups, patch_count), BF16),
        ],
        compiler_params=params(DELIVER),
        name="deliver",
    )(pick, frames_in, gathered, first_rows, second_rows)


def solution(mesh):
    fine = Mesh(mesh.devices.reshape(4, 2, 4, 2, 8), ("zh", "zl", "x", "c", "pool"))
    run = jax.shard_map(
        local,
        mesh=fine,
        in_specs=(
            P(FRAME, None, None),
            P(FRAME, None, "pool"),
            P("pool", FRAME),
            P(FRAME),
            P(FRAME),
        ),
        out_specs=(P(FRAME + ("pool",), None, None), P(FRAME + ("pool",), None, None)),
        check_vma=False,
    )

    def whole(*args):
        shipped, scales = run(*args)
        return shipped, scales

    return whole
```

time: 174 us -> 185 us (1.063)
  other arithmetic: 4.17 us -> 12.6 us
  Pallas kernels: 11.5 us -> 15.4 us
  waiting for transfers between devices: 42.9 us -> 39.2 us
  blocking collectives: 55.4 us -> 58.2 us
  local copies, waits for them, and re-layouts: 14.2 us -> 12.2 us
    all_gather x1 -> x2, waiting for transfers between devices: 0.01 us -> 17.1 us  [the longest x1 14.8 us: local(): out_rows = lax.all_gather(back_rows, 'pool', axis=0, tiled=False)]
    all_to_all x1 -> x2, blocking collectives: 11.9 us -> 27.2 us  [spread(): return lax.all_to_all(copies, axis, 0, 0, tiled=True)]
    all_to_all x1 -> x0, waiting for transfers between devices: 10.2 us -> none  [spread(): return lax.all_to_all(copies, axis, 0, 0, tiled=True)]
    all_gather x1, blocking collectives: 8.39 us -> 1.85 us  [local(): both = lax.all_gather(payload, 'c', axis=0, tiled=True)]
    all_to_all x1, blocking collectives: 35.1 us -> 29.2 us  [local(): lax.all_to_all(share, FRAME, 0, 0, tiled=True).reshape(4 * chips, width)]
    all_to_all x1, starting transfers between devices: 10.5 us -> 4.52 us  [local(): gathered = lax.all_to_all(packed, ('c', 'pool'), 0, 0, tiled=True)]
    all_to_all x1, starting transfers between devices: 4.25 us -> 9.89 us  [local(): returned = lax.all_to_all(attended, CHIP, 0, 0, tiled=True)]
    ppermute x1 -> x2, starting transfers between devices: 6.47 us -> 12 us  [the longest x1 6.21 us: local(): far_rows = lax.ppermute(near_rows, 'c', swap)]
  transfers between devices with their start and end apart: 6 -> 7, of which waited for: 5 -> 6; matrix products, arithmetic and copies ran while one was open for 2% -> 5% of each run, Pallas kernels for 4% -> 1%
where the time goes in v3:
time: 185 us
  blocking collectives  58.2 us (31%)
  waiting for transfers between devices  39.2 us (21%)
  starting transfers between devices  31.4 us (17%)
  between operations  15.6 us (8%)
  Pallas kernels  15.4 us (8%)
  other arithmetic  12.6 us (7%)
  local copies, waits for them, and re-layouts  12.2 us (7%)
    all_to_all x1, blocking collectives, local(): lax.all_to_all(share, FRAME, 0, 0, tiled=True).reshape(4 * chips, width)  29.2 us
    all_to_all x2, blocking collectives, spread(): return lax.all_to_all(copies, axis, 0, 0, tiled=True)  27.2 us
    all_gather x1, waiting for transfers between devices, local(): out_rows = lax.all_gather(back_rows, 'pool', axis=0, tiled=False)  14.8 us
    all_to_all x1, waiting for transfers between devices, local(): gathered = lax.all_to_all(packed, ('c', 'pool'), 0, 0, tiled=True)  13.8 us
    all_to_all x1, starting transfers between devices, local(): returned = lax.all_to_all(attended, CHIP, 0, 0, tiled=True)  9.89 us
    pallas_call x1, Pallas kernels, local(): pl.pallas_call(track_kernel, grid=(4,), in_specs=[pl.BlockSpec(memory_spa...  8.77 us
    ppermute x1, starting transfers between devices, local(): far_rows = lax.ppermute(near_rows, 'c', swap)  6.21 us
    ppermute x1, starting transfers between devices, local(): mine_other = lax.ppermute(mine, 'c', swap)  5.78 us
  transfers between devices with their start and end apart: 7, of which 6 were waited for; matrix products, arithmetic and copies ran while one was open for 5% of the time, Pallas kernels for 1%

profile of v3, /device:TPU:1, one launch (start us, length us, event | category | flops | bytes accessed | tf_op | source)
XLA Modules:
  0.0 184.6 jit_solution(12459925610716913710)
XLA Ops:
  7.2 4.6 %reshape.47 = bf16[2,2,64,4,1408]{4,3,2,1,0:T(4,128)(2,1)S(1)} reshape(bf16[4,256,1408]{2,1,0:T(8,128)(2,1)} %frame_ref.1) | data formatting | bytes 5767168 | tf_op jit(solution)/shard_map/reshape | solution.py:218
  14.6 29.2 %all_to_all.25 = bf16[64,2,1408]{2,1,0:T(2,128)(2,1)S(1)} all-to-all(bf16[64,2,1408]{2,1,0:T(2,128)(2,1)S(1)} %fusion.5), channel_id=1, replica_groups=mesh['zh'=4,'zl'=2,'x'=4,'c'=2,'pool'=8] {'zh','zl','x','c'}, dimensions={0} | all-to-all | bytes 720896 | tf_op jit(solution)/shard_map/all_to_all | solution.py:222
  43.8 0.9 all_gather_reshape.3
  45.4 1.9 %all_gather.13 = bf16[44,2,384]{2,1,0:T(2,128)(2,1)S(1)} all-gather(bf16[22,2,384]{2,1,0:T(2,128)(2,1)S(1)} %concatenate.11), channel_id=1, replica_groups=mesh['zh'=4,'zl'=2,'x'=4,'c'=2,'pool'=8] {'c'}, dimensions={0}, use_global_device_ids=true | all-gather | bytes 101376 | tf_op jit(solution)/shard_map/all_gather | solution.py:241
  47.4 10.7 %all_to_all.26 = bf16[4,44,384]{2,1,0:T(8,128)(2,1)S(1)} all-to-all(bf16[4,44,384]{2,1,0:T(8,128)(2,1)S(1)} %broadcast_in_dim.24), channel_id=1, replica_groups=mesh['zh'=4,'zl'=2,'x'=4,'c'=2,'pool'=8] {'zh'}, dimensions={0} | all-to-all | bytes 270336 | tf_op jit(solution)/shard_map/all_to_all | solution.py:34
  58.3 16.4 %all_to_all.27.own_ref = bf16[8,176,384]{2,1,0:T(8,128)(2,1)S(1)} all-to-all(bf16[8,176,384]{2,1,0:T(8,128)(2,1)S(1)} %broadcast_in_dim.26), channel_id=1, replica_groups=mesh['zh'=4,'zl'=2,'x'=4,'c'=2,'pool'=8] {'zl','x'}, dimensions={0} | all-to-all | bytes 2162688 | tf_op jit(solution)/shard_map/all_to_all | solution.py:34
  74.7 5.8 %collective-permute-start.1 = (bf16[8,176,384]{2,1,0:T(8,128)(2,1)S(1)}, bf16[8,176,384]{2,1,0:T(8,128)(2,1)S(1)}, u32[]{:S(2)}, u32[]{:S(2)}) collective-permute-start(bf16[8,176,384]{2,1,0:T(8,128)(2,1)S(1)} %all_to_all.27.own_ref), channel_id=1, source_target_pairs={{0,8},{8,0},{1,9},{9,1},{2,10},{10,2},{3,11},{11,3},{4,12},{12,4},... | collective-permute-start | bytes 3244040 | tf_op jit(solution)/shard_map/ppermute | solution.py:245
  80.5 2.3 %collective-permute-done.1.other_ref = bf16[8,176,384]{2,1,0:T(8,128)(2,1)S(1)} collective-permute-done((bf16[8,176,384]{2,1,0:T(8,128)(2,1)S(1)}, bf16[8,176,384]{2,1,0:T(8,128)(2,1)S(1)}, u32[]{:S(2)}, u32[]{:S(2)}) %collective-permute-start.1) | collective-permute-done | bytes 1081376 | tf_op jit(solution)/shard_map/ppermute | solution.py:245
  82.8 2.3 %all-gather.4.cloned.1.call-done.tokens_ref = bf16[8,128,1408]{2,1,0:T(8,128)(2,1)} async-done(((bf16[1,128,1408]{2,1,0:T(8,128)(2,1)}), bf16[8,128,1408]{2,1,0:T(8,128)(2,1)}) %all-gather.4.cloned.1.call-update) | async-done | bytes 2883600 | tf_op jit(solution)/shard_map/all_gather | solution.py:223
  85.2 8.8 %track.1 = (bf16[16,2,6,8,128]{4,3,2,1,0:T(8,128)(2,1)}, bf16[96,1408]{1,0:T(8,128)(2,1)}) custom-call(s32[1]{0:T(128)} %bitcast.2.core_ref, bf16[8,128,1408]{2,1,0:T(8,128)(2,1)} %all-gather.4.cloned.1.call-done.tokens_ref, bf16[8,176,384]{2,1,0:T(8,128)(2,1)} %copy-done.3, bf16[8,176,384]{2,1,0:T(8,128)(2,1)} %copy-done.5), custom_call_target="tpu_custom_call" | custom-call | tf_op jit(solution)/shard_map/track/pallas_call | solution.py:246
  93.9 9.9 %all-to-all-start.3 = ((bf16[32,6,8,128]{3,2,1,0:T(8,128)(2,1)}), bf16[32,6,8,128]{3,2,1,0:T(8,128)(2,1)S(1)}, u32[]{:S(2)}, u32[]{:S(2)}) async-start(bf16[32,6,8,128]{3,2,1,0:T(8,128)(2,1)} %bitcast.36), calls=%async_computation.3 | async-start | bytes 786432 | tf_op jit(solution)/shard_map/all_to_all | solution.py:274
  103.9 4.9 %collective-permute-start = (s32[4]{0:T(128)S(1)}, s32[4]{0:T(128)S(1)}, u32[]{:S(2)}, u32[]{:S(2)}) collective-permute-start(s32[4]{0:T(128)S(1)} %copy-done.8), channel_id=1, source_target_pairs={{0,8},{8,0},{1,9},{9,1},{2,10},{10,2},{3,11},{11,3},{4,12},{12,4},... | collective-permute-start | bytes 56 | tf_op jit(solution)/shard_map/ppermute | solution.py:224
  110.2 5.1 %all-to-all-done.3 = bf16[32,6,8,128]{3,2,1,0:T(8,128)(2,1)S(1)} async-done(((bf16[32,6,8,128]{3,2,1,0:T(8,128)(2,1)}), bf16[32,6,8,128]{3,2,1,0:T(8,128)(2,1)S(1)}, u32[]{:S(2)}, u32[]{:S(2)}) %all-to-all-start.3) | async-done | bytes 393248 | tf_op jit(solution)/shard_map/all_to_all | solution.py:274
  116.1 2.4 %pack.1 = bf16[16,24,8,128]{3,2,1,0:T(8,128)(2,1)} custom-call(s32[8]{0:T(128)} %broadcast_select_fusion.2.owner_ref, bf16[16,2,6,8,128]{4,3,2,1,0:T(8,128)(2,1)} %bitcast.35), custom_call_target="tpu_custom_call" | custom-call | tf_op jit(solution)/shard_map/pack/pallas_call | solution.py:281
  118.5 1.2 slice.34
  120.3 14.8 %all-gather.6.cloned.1.call-done = bf16[768,1408]{1,0:T(8,128)(2,1)} async-done(((bf16[96,1408]{1,0:T(8,128)(2,1)}), bf16[768,1408]{1,0:T(8,128)(2,1)}) %all-gather.6.cloned.1.call-update) | async-done | bytes 2162704 | tf_op jit(solution)/shard_map/all_gather | solution.py:272
  135.1 3.2 %broadcast_multiply_fusion = bf16[768,1408]{1,0:T(8,128)(2,1)} fusion(bf16[768,1408]{1,0:T(8,128)(2,1)} %all-gather.6.cloned.1.call-done, bf16[]{:T(256)} %bitcast.12), kind=kLoop, calls=%fused_computation.2 | loop fusion | flops 1081344 | bytes 4325378 | tf_op jit(solution)/shard_map/mul | solution.py:299
  138.3 6.2 %collective-permute-start.2 = (bf16[8,96,1408]{2,1,0:T(8,128)(2,1)}, bf16[8,96,1408]{2,1,0:T(8,128)(2,1)}, u32[]{:S(2)}, u32[]{:S(2)}) collective-permute-start(bf16[8,96,1408]{2,1,0:T(8,128)(2,1)} %bitcast.13), channel_id=1, source_target_pairs={{0,8},{8,0},{1,9},{9,1},{2,10},{10,2},{3,11},{11,3},{4,12},{12,4},... | collective-permute-start | bytes 6488072 | tf_op jit(solution)/shard_map/ppermute | solution.py:300
  144.5 4.5 %all-to-all-start.4 = ((bf16[16,24,8,128]{3,2,1,0:T(8,128)(2,1)}), bf16[16,24,8,128]{3,2,1,0:T(8,128)(2,1)}, u32[]{:S(2)}, u32[]{:S(2)}) async-start(bf16[16,24,8,128]{3,2,1,0:T(8,128)(2,1)} %pack.1), calls=%async_computation.4 | async-start | bytes 1572864 | tf_op jit(solution)/shard_map/all_to_all | solution.py:292
  151.7 4.8 %broadcast_select_fusion = (bf16[8,96,1408]{2,1,0:T(8,128)(2,1)}, bf16[8,96,1408]{2,1,0:T(8,128)(2,1)}) fusion(bf16[8,96,1408]{2,1,0:T(8,128)(2,1)} %collective-permute-done.2, bf16[8,96,1408]{2,1,0:T(8,128)(2,1)} %bitcast.13, pred[]{:T(512)S(6)} %eq.19), kind=kLoop, calls=%fused_computation | loop fusion | flops 2162688 | bytes 8650753 | tf_op jit(solution)/shard_map/jit(_where)/select_n | solution.py:302
  156.5 13.8 %all-to-all-done.4.y_ref = bf16[16,24,8,128]{3,2,1,0:T(8,128)(2,1)} async-done(((bf16[16,24,8,128]{3,2,1,0:T(8,128)(2,1)}), bf16[16,24,8,128]{3,2,1,0:T(8,128)(2,1)}, u32[]{:S(2)}, u32[]{:S(2)}) %all-to-all-start.4) | async-done | bytes 786464 | tf_op jit(solution)/shard_map/all_to_all | solution.py:292
  170.4 1.6 copy-done.1
  172.0 1.6 copy-done.2
  173.6 4.1 %deliver.1 = (bf16[1,256,1408]{2,1,0:T(8,128)(2,1)}, bf16[1,11,256]{2,1,0:T(8,128)(2,1)}) custom-call(s32[2]{0:T(128)S(1)} %pad_add_fusion.pick_ref, bf16[4,256,1408]{2,1,0:T(8,128)(2,1)S(1)} %copy-done, bf16[16,24,8,128]{3,2,1,0:T(8,128)(2,1)} %all-to-all-done.4.y_ref, bf16[8,96,1408]{2,1,0:T(8,128)(2,1)S(1)} %copy-done.2, bf16[8,96,1408]{2,1,0:T(8,128)(2,1)S(1)} %copy-done.1), custom_call_target="tpu_custom_call" | custom-call | tf_op jit(solution)/shard_map/deliver/pallas_call | solution.py:303
  (46 shorter events, 7.9 us)
Async XLA Ops:
  7.2 78.0 %all-gather.4.cloned.1.call-start = ((), (), s32[]{:S(2)}) async-start(), calls=%async_computation.5 | async-start | bytes 3244032 | tf_op jit(solution)/shard_map/all_gather | solution.py:223
  12.6 32.1 %copy-start.7 = (bf16[176,22]{0,1:T(8,128)(2,1)S(1)}, bf16[176,22]{0,1:T(8,128)(2,1)}, u32[]{:S(2)}) copy-start(bf16[176,22]{0,1:T(8,128)(2,1)} %param.7) | copy-start | bytes 23236
  12.6 32.3 %copy-start.6 = (bf16[22,3,176]{2,0,1:T(8,128)(2,1)S(1)}, bf16[22,3,176]{2,0,1:T(8,128)(2,1)}, u32[]{:S(2)}) copy-start(bf16[22,3,176]{2,0,1:T(8,128)(2,1)} %param.6) | copy-start | bytes 69700
  44.7 90.4 %all-gather.6.cloned.1.call-start = ((), (), s32[]{:S(2)}) async-start(), calls=%async_computation.6 | async-start | bytes 2433024 | tf_op jit(solution)/shard_map/all_gather | solution.py:272
  74.7 10.4 %copy-start.3 = (bf16[8,176,384]{2,1,0:T(8,128)(2,1)}, bf16[8,176,384]{2,1,0:T(8,128)(2,1)S(1)}, u32[]{:S(2)}) copy-start(bf16[8,176,384]{2,1,0:T(8,128)(2,1)S(1)} %all_to_all.27.own_ref) | copy-start | bytes 3244036
  74.7 8.1 %collective-permute-start.1 = (bf16[8,176,384]{2,1,0:T(8,128)(2,1)S(1)}, bf16[8,176,384]{2,1,0:T(8,128)(2,1)S(1)}, u32[]{:S(2)}, u32[]{:S(2)}) collective-permute-start(bf16[8,176,384]{2,1,0:T(8,128)(2,1)S(1)} %all_to_all.27.own_ref), channel_id=1, source_target_pairs={{0,8},{8,0},{1,9},{9,1},{2,10},{10,2},{3,11},{11,3},{4,12},{12,4},... | collective-permute-start | bytes 3244040 | tf_op jit(solution)/shard_map/ppermute | solution.py:245
  82.8 2.3 %copy-start.5 = (bf16[8,176,384]{2,1,0:T(8,128)(2,1)}, bf16[8,176,384]{2,1,0:T(8,128)(2,1)S(1)}, u32[]{:S(2)}) copy-start(bf16[8,176,384]{2,1,0:T(8,128)(2,1)S(1)} %collective-permute-done.1.other_ref) | copy-start | bytes 3244036
  85.1 18.7 %copy-start.8 = (s32[4]{0:T(128)S(1)}, s32[4]{0:T(128)}, u32[]{:S(2)}) copy-start(s32[4]{0:T(128)} %param.8) | copy-start | bytes 52
  93.9 21.4 %all-to-all-start.3 = ((bf16[32,6,8,128]{3,2,1,0:T(8,128)(2,1)}), bf16[32,6,8,128]{3,2,1,0:T(8,128)(2,1)S(1)}, u32[]{:S(2)}, u32[]{:S(2)}) async-start(bf16[32,6,8,128]{3,2,1,0:T(8,128)(2,1)} %bitcast.36), calls=%async_computation.3 | async-start | bytes 786432 | tf_op jit(solution)/shard_map/all_to_all | solution.py:274
  103.9 5.7 %collective-permute-start = (s32[4]{0:T(128)S(1)}, s32[4]{0:T(128)S(1)}, u32[]{:S(2)}, u32[]{:S(2)}) collective-permute-start(s32[4]{0:T(128)S(1)} %copy-done.8), channel_id=1, source_target_pairs={{0,8},{8,0},{1,9},{9,1},{2,10},{10,2},{3,11},{11,3},{4,12},{12,4},... | collective-permute-start | bytes 56 | tf_op jit(solution)/shard_map/ppermute | solution.py:224
  115.3 0.7 copy-start.4
  135.1 13.9 %copy-start.9 = (s32[4]{0:T(128)S(1)}, s32[4]{0:T(128)}, u32[]{:S(2)}) copy-start(s32[4]{0:T(128)} %param.9) | copy-start | bytes 52
  138.3 13.4 %collective-permute-start.2 = (bf16[8,96,1408]{2,1,0:T(8,128)(2,1)}, bf16[8,96,1408]{2,1,0:T(8,128)(2,1)}, u32[]{:S(2)}, u32[]{:S(2)}) collective-permute-start(bf16[8,96,1408]{2,1,0:T(8,128)(2,1)} %bitcast.13), channel_id=1, source_target_pairs={{0,8},{8,0},{1,9},{9,1},{2,10},{10,2},{3,11},{11,3},{4,12},{12,4},... | collective-permute-start | bytes 6488072 | tf_op jit(solution)/shard_map/ppermute | solution.py:300
  144.5 25.9 %all-to-all-start.4 = ((bf16[16,24,8,128]{3,2,1,0:T(8,128)(2,1)}), bf16[16,24,8,128]{3,2,1,0:T(8,128)(2,1)}, u32[]{:S(2)}, u32[]{:S(2)}) async-start(bf16[16,24,8,128]{3,2,1,0:T(8,128)(2,1)} %pack.1), calls=%async_computation.4 | async-start | bytes 1572864 | tf_op jit(solution)/shard_map/all_to_all | solution.py:292
  151.7 18.7 %copy-start = (bf16[4,256,1408]{2,1,0:T(8,128)(2,1)S(1)}, bf16[4,256,1408]{2,1,0:T(8,128)(2,1)}, u32[]{:S(2)}) copy-start(bf16[4,256,1408]{2,1,0:T(8,128)(2,1)} %frame_ref.1) | copy-start | bytes 8650756
  170.3 1.6 copy-start.1
  172.0 1.6 copy-start.2
Sparse Core Ops, SparseCore 0:
  44.8 40.2 all-gather.3
  94.1 40.9 all-gather.5

commit v4 on v3

--- a/solution.py
+++ b/solution.py
@@ -9,7 +9,7 @@
 GROUP = 128
 MAIN = 64
 SLOT = 32
-TRACK, PACK, DELIVER = 60, 60, 30
+ORDER, TRACK, PACK, DELIVER = 30, 40, 40, 30
 FACTOR = 1.0 / HEAD_DIM**0.5
 CHIP = ("zh", "zl", "x")
 FRAME = CHIP + ("c",)
@@ -34,7 +34,7 @@
     return lax.all_to_all(copies, axis, 0, 0, tiled=True)
 
 
-def order_rows(source_ref, order_ref):
+def order_kernel(source_ref, right_ref, back_ref, order_ref):
     inner, height = source_ref.shape[:2]
     outer = 4
     rows = height // outer
@@ -43,27 +43,19 @@
         for high in range(outer):
             start = (high * inner + low) * rows
             order_ref[start : start + rows, :] = block[high * rows : (high + 1) * rows]
-
-
-def track_kernel(
-    core_ref, tokens_ref, own_ref, other_ref, out_ref, back_ref, order_ref, right_ref, o_ref
-):
+    right_ref[...] = order_ref[...].astype(BF16)
+    turned = [order_ref[:, at : at + 128].T[HEAD_DIM:] for at in (0, 128, 256)]
+    back_ref[...] = jnp.concatenate(turned, axis=0)[:96].astype(BF16)
+
+
+def track_kernel(core_ref, tokens_ref, own_ref, other_ref, out_ref, o_ref):
     step = pl.program_id(0)
     core = core_ref[0]
     frames = 2 * tokens_ref.shape[1]
     lane = lanes_of((frames, 128))
-
-    @pl.when(step == 0)
-    def _():
-        for which, ref in enumerate((own_ref, other_ref)):
-            order_rows(ref, order_ref)
-            right_ref[:, which * 384 : which * 384 + 384] = order_ref[...].astype(BF16)
-            if which == 0:
-                turned = [order_ref[:, at : at + 128].T[HEAD_DIM:] for at in (0, 128, 256)]
-                back_ref[...] = jnp.concatenate(turned, axis=0)[:96].astype(BF16)
-
     tokens = tokens_ref[...].reshape(frames, tokens_ref.shape[2])
-    both = jnp.dot(tokens, right_ref[...], preferred_element_type=F32)
+    right = jnp.concatenate([own_ref[...], other_ref[...]], axis=1)
+    both = jnp.dot(tokens, right, preferred_element_type=F32)
     for which in range(2):
         head = core if which == 0 else 1 - core
         out = both[:, which * 384 : which * 384 + 384]
@@ -141,7 +133,7 @@
         out_ref[place, pairs:] = rest.astype(BF16)
 
 
-def deliver_kernel(pick_ref, frame_ref, y_ref, first_ref, second_ref, out_ref, scale_ref):
+def deliver_kernel(pick_ref, frame_ref, y_ref, weight_ref, out_ref, scale_ref):
     sources = y_ref.shape[0]
     heads = sources // 2
     patches, width = frame_ref.shape[1:]
@@ -175,7 +167,9 @@
     for start in range(0, width, 256):
         stop = min(start + 256, width)
         right, right_rest = (
-            jnp.concatenate([ref[:, rows, start:stop] for ref in (first_ref, second_ref)], axis=1)
+            jnp.concatenate(
+                [weight_ref[at : at + heads, rows, start:stop] for at in (0, heads)], axis=1
+            )
             for rows in (slice(0, MAIN), slice(MAIN, MAIN + SLOT))
         )
         right = right.reshape(heads * 2 * MAIN, stop - start)
@@ -215,10 +209,12 @@
     sources = 2 * lax.axis_size("pool")
     swap = [(0, 1), (1, 0)]
 
-    share = frames_in.reshape(2, 2, 2 * chips, 4, width)
-    share = lax.dynamic_index_in_dim(share, position % 2, 0, keepdims=False)
-    share = lax.dynamic_index_in_dim(share, position // 2, 2, keepdims=False)
-    share = normalise(share).transpose(1, 0, 2)
+    share = lax.dynamic_slice_in_dim(frames_in, (position % 2) * 2, 2, 0)
+    share = share.reshape(2, chips, 8, width)
+    share = jnp.concatenate(
+        [lax.dynamic_slice_in_dim(share, position // 2 + at, 1, 2) for at in (0, 4)], axis=2
+    )
+    share = normalise(share).transpose(1, 2, 0, 3).reshape(2 * chips, 2, width)
     share = lax.all_to_all(share, FRAME, 0, 0, tiled=True).reshape(4 * chips, width)
     tracks = lax.all_gather(share, "pool", axis=0, tiled=False)
     owners_other = lax.ppermute(owners, "c", swap)
@@ -242,35 +238,35 @@
     mine = lax.dynamic_index_in_dim(both, core, 1, keepdims=False)
     mine = spread(mine, "zh").reshape(-1, mine.shape[-1])
     mine = spread(mine, ("zl", "x"))
+    mine, back_rows = pl.pallas_call(
+        order_kernel,
+        out_shape=[
+            jax.ShapeDtypeStruct((width, 384), BF16),
+            jax.ShapeDtypeStruct((96, width), BF16),
+        ],
+        scratch_shapes=[pltpu.VMEM((width, 384), F32)],
+        compiler_params=params(ORDER),
+        name="order",
+    )(mine)
     mine_other = lax.ppermute(mine, "c", swap)
-    attended, back_rows = pl.pallas_call(
+    out_rows = lax.all_gather(back_rows, ("c", "pool"), axis=0, tiled=False)
+
+    attended = pl.pallas_call(
         track_kernel,
         grid=(4,),
         in_specs=[
             pl.BlockSpec(memory_space=pltpu.SMEM),
             pl.BlockSpec((2, 4 * chips, width), lambda p: (p, 0, 0)),
-            pl.BlockSpec(mine.shape, lambda p: (0, 0, 0)),
-            pl.BlockSpec(mine.shape, lambda p: (0, 0, 0)),
-        ],
-        out_specs=[
-            pl.BlockSpec((chips // 2, 2, 6, 8, 128), lambda p: (0, 0, 0, 0, 0)),
-            pl.BlockSpec((96, width), lambda p: (0, 0)),
-        ],
-        out_shape=[
-            jax.ShapeDtypeStruct((chips // 2, 2, 6, 8, 128), BF16),
-            jax.ShapeDtypeStruct((96, width), BF16),
-        ],
-        scratch_shapes=[
-            pltpu.VMEM((width, 384), F32),
-            pltpu.VMEM((width, 768), BF16),
-            pltpu.VMEM((chips, 64, 128), F32),
-        ],
+            pl.BlockSpec(mine.shape, lambda p: (0, 0)),
+            pl.BlockSpec(mine.shape, lambda p: (0, 0)),
+        ],
+        out_specs=pl.BlockSpec((chips // 2, 2, 6, 8, 128), lambda p: (0, 0, 0, 0, 0)),
+        out_shape=jax.ShapeDtypeStruct((chips // 2, 2, 6, 8, 128), BF16),
+        scratch_shapes=[pltpu.VMEM((chips, 64, 128), F32)],
         compiler_params=params(TRACK),
         name="track",
     )(core.reshape(1), tracks, mine, mine_other)
     attended = attended.reshape(chips, 6, 8, 128)
-    out_rows = lax.all_gather(back_rows, "pool", axis=0, tiled=False)
-
     returned = lax.all_to_all(attended, CHIP, 0, 0, tiled=True)
 
     pair = jnp.where(
@@ -295,11 +291,6 @@
     chosen = jnp.sum(jnp.where(match, jnp.arange(fr_count, dtype=jnp.int32), 0))
     pick = jnp.stack([chosen, jnp.any(match).astype(jnp.int32)])
     groups = width // GROUP
-    one = 1.0 - packed[0, 0, 0, 0].astype(F32) * 0.0
-    near_rows = out_rows * one.astype(BF16)
-    far_rows = lax.ppermute(near_rows, "c", swap)
-    first_rows = jnp.where(core == 0, near_rows, far_rows)
-    second_rows = jnp.where(core == 0, far_rows, near_rows)
     return pl.pallas_call(
         deliver_kernel,
         grid_spec=pltpu.PrefetchScalarGridSpec(
@@ -308,7 +299,6 @@
             in_specs=[
                 pl.BlockSpec((1, patch_count, width), lambda g, pick: (pick[0], 0, 0)),
                 pl.BlockSpec(gathered.shape, lambda g, pick: (0, 0, 0, 0)),
-                pl.BlockSpec(out_rows.shape, lambda g, pick: (0, 0, 0)),
                 pl.BlockSpec(out_rows.shape, lambda g, pick: (0, 0, 0)),
             ],
             out_specs=[
@@ -322,7 +312,7 @@
         ],
         compiler_params=params(DELIVER),
         name="deliver",
-    )(pick, frames_in, gathered, first_rows, second_rows)
+    )(pick, frames_in, gathered, out_rows)
 
 
 def solution(mesh):

time: 185 us -> 160 us (0.86)
  waiting for transfers between devices: 39.2 us -> 29.7 us
  other arithmetic: 12.6 us -> 4.17 us
  local copies, waits for them, and re-layouts: 12.2 us -> 9.31 us
  Pallas kernels: 15.4 us -> 12.6 us
    all_gather x1, waiting for transfers between devices: 14.8 us -> 0.01 us  [local(): out_rows = lax.all_gather(back_rows, ('c', 'pool'), axis=0, tiled=False)]
    ppermute x1 -> x0, starting transfers between devices: 6.21 us -> none  [local(): far_rows = lax.ppermute(near_rows, 'c', swap)]
    all_to_all x1, waiting for transfers between devices: 13.8 us -> 19.8 us  [local(): gathered = lax.all_to_all(packed, ('c', 'pool'), 0, 0, tiled=True)]
    all_to_all x1, starting transfers between devices: 4.52 us -> 9.81 us  [local(): gathered = lax.all_to_all(packed, ('c', 'pool'), 0, 0, tiled=True)]
    select_n x1 -> x0, other arithmetic: 4.85 us -> none  [local(): second_rows = jnp.where(core == 0, far_rows, near_rows)]
    mul x1 -> x0, other arithmetic: 3.18 us -> none  [local(): near_rows = out_rows * one.astype(BF16)]
    reshape x1 -> x2, local copies, waits for them, and re-layouts: 4.58 us -> 1.85 us  [the longest x1 1.47 us: local(): share = share.reshape(2, chips, 8, width)]
    pallas_call x1, Pallas kernels: 8.77 us -> 6.25 us  [local(): pl.pallas_call(track_kernel, grid=(4,), in_specs=[pl.BlockSpec(memory_spa...]
  transfers between devices with their start and end apart: 7 -> 6, of which waited for: 6 -> 5; matrix products, arithmetic and copies ran while one was open for 5% -> 2% of each run, Pallas kernels for 1% -> 5%
where the time goes in v4:
time: 160 us
  blocking collectives  58.2 us (36%)
  starting transfers between devices  30.8 us (19%)
  waiting for transfers between devices  29.7 us (19%)
  between operations  15 us (9%)
  Pallas kernels  12.6 us (8%)
  local copies, waits for them, and re-layouts  9.31 us (6%)
  other arithmetic  4.17 us (3%)
    all_to_all x1, blocking collectives, local(): lax.all_to_all(share, FRAME, 0, 0, tiled=True).reshape(4 * chips, width)  29.2 us
    all_to_all x2, blocking collectives, spread(): return lax.all_to_all(copies, axis, 0, 0, tiled=True)  27.2 us
    all_to_all x1, waiting for transfers between devices, local(): gathered = lax.all_to_all(packed, ('c', 'pool'), 0, 0, tiled=True)  19.8 us
    all_to_all x1, starting transfers between devices, local(): returned = lax.all_to_all(attended, CHIP, 0, 0, tiled=True)  10.1 us
    all_to_all x1, starting transfers between devices, local(): gathered = lax.all_to_all(packed, ('c', 'pool'), 0, 0, tiled=True)  9.81 us
    pallas_call x1, Pallas kernels, local(): pl.pallas_call(track_kernel, grid=(4,), in_specs=[pl.BlockSpec(memory_spa...  6.25 us
    ppermute x1, starting transfers between devices, local(): mine_other = lax.ppermute(mine, 'c', swap)  5.79 us
    all_to_all x1, waiting for transfers between devices, local(): returned = lax.all_to_all(attended, CHIP, 0, 0, tiled=True)  5.61 us
  transfers between devices with their start and end apart: 6, of which 5 were waited for; matrix products, arithmetic and copies ran while one was open for 2% of the time, Pallas kernels for 5%

profile of v4, /device:TPU:1, one launch (start us, length us, event | category | flops | bytes accessed | tf_op | source)
XLA Modules:
  0.0 159.7 jit_solution(7490791601850271009)
XLA Ops:
  7.2 1.5 dynamic-slice_bitcast_fusion
  8.7 0.7 constant_dynamic-slice_fusion.2
  9.5 1.0 convert_reduce_fusion
  12.0 29.2 %all_to_all.25 = bf16[64,2,1408]{2,1,0:T(2,128)(2,1)S(1)} all-to-all(bf16[64,2,1408]{2,1,0:T(2,128)(2,1)S(1)} %bitcast.25), channel_id=1, replica_groups=mesh['zh'=4,'zl'=2,'x'=4,'c'=2,'pool'=8] {'zh','zl','x','c'}, dimensions={0} | all-to-all | bytes 720896 | tf_op jit(solution)/shard_map/all_to_all | solution.py:218
  41.2 0.9 all_gather_reshape.3
  42.8 1.9 %all_gather.13 = bf16[44,2,384]{2,1,0:T(2,128)(2,1)S(1)} all-gather(bf16[22,2,384]{2,1,0:T(2,128)(2,1)S(1)} %concatenate.15), channel_id=1, replica_groups=mesh['zh'=4,'zl'=2,'x'=4,'c'=2,'pool'=8] {'c'}, dimensions={0}, use_global_device_ids=true | all-gather | bytes 101376 | tf_op jit(solution)/shard_map/all_gather | solution.py:237
  44.8 10.7 %all_to_all.26 = bf16[4,44,384]{2,1,0:T(8,128)(2,1)S(1)} all-to-all(bf16[4,44,384]{2,1,0:T(8,128)(2,1)S(1)} %broadcast_in_dim.24), channel_id=1, replica_groups=mesh['zh'=4,'zl'=2,'x'=4,'c'=2,'pool'=8] {'zh'}, dimensions={0} | all-to-all | bytes 270336 | tf_op jit(solution)/shard_map/all_to_all | solution.py:34
  55.7 16.4 %all_to_all.27.source_ref = bf16[8,176,384]{2,1,0:T(8,128)(2,1)S(1)} all-to-all(bf16[8,176,384]{2,1,0:T(8,128)(2,1)S(1)} %broadcast_in_dim.26), channel_id=1, replica_groups=mesh['zh'=4,'zl'=2,'x'=4,'c'=2,'pool'=8] {'zl','x'}, dimensions={0} | all-to-all | bytes 2162688 | tf_op jit(solution)/shard_map/all_to_all | solution.py:34
  72.1 1.2 order.1
  73.3 5.8 %collective-permute-start.1 = (bf16[1408,384]{1,0:T(8,128)(2,1)S(1)}, bf16[1408,384]{1,0:T(8,128)(2,1)S(1)}, u32[]{:S(2)}, u32[]{:S(2)}) collective-permute-start(bf16[1408,384]{1,0:T(8,128)(2,1)S(1)} %get-tuple-element.4.own_ref), channel_id=1, source_target_pairs={{0,8},{8,0},{1,9},{9,1},{2,10},{10,2},{3,11},{11,3},{4,12},{12,4},... | collective-permute-start | bytes 3244040 | tf_op jit(solution)/shard_map/ppermute | solution.py:251
  79.1 2.3 %collective-permute-done.1.other_ref = bf16[1408,384]{1,0:T(8,128)(2,1)S(1)} collective-permute-done((bf16[1408,384]{1,0:T(8,128)(2,1)S(1)}, bf16[1408,384]{1,0:T(8,128)(2,1)S(1)}, u32[]{:S(2)}, u32[]{:S(2)}) %collective-permute-start.1) | collective-permute-done | bytes 1081376 | tf_op jit(solution)/shard_map/ppermute | solution.py:251
  81.4 1.1 all-gather.4.cloned.1.call-done.tokens_ref
  82.5 1.8 %copy-done.3 = bf16[8,128,1408]{2,1,0:T(8,128)(2,1)S(1)} copy-done((bf16[8,128,1408]{2,1,0:T(8,128)(2,1)S(1)}, bf16[8,128,1408]{2,1,0:T(8,128)(2,1)}, u32[]{:S(2)}) %copy-start.3) | copy-done | bytes 2883608
  84.4 6.3 %track.1 = bf16[16,2,6,8,128]{4,3,2,1,0:T(8,128)(2,1)} custom-call(s32[1]{0:T(128)} %bitcast.2.core_ref, bf16[8,128,1408]{2,1,0:T(8,128)(2,1)S(1)} %copy-done.3, bf16[1408,384]{1,0:T(8,128)(2,1)S(1)} %get-tuple-element.4.own_ref, bf16[1408,384]{1,0:T(8,128)(2,1)S(1)} %collective-permute-done.1.other_ref), custom_call_target="tpu_custom_call" | custom-call | tf_op jit(solution)/shard_map/track/pallas_call | solution.py:254
  90.6 10.1 %all-to-all-start.3 = ((bf16[32,6,8,128]{3,2,1,0:T(8,128)(2,1)}), bf16[32,6,8,128]{3,2,1,0:T(8,128)(2,1)S(1)}, u32[]{:S(2)}, u32[]{:S(2)}) async-start(bf16[32,6,8,128]{3,2,1,0:T(8,128)(2,1)} %bitcast.11), calls=%async_computation.3 | async-start | bytes 786432 | tf_op jit(solution)/shard_map/all_to_all | solution.py:270
  100.8 4.9 %collective-permute-start = (s32[4]{0:T(128)S(1)}, s32[4]{0:T(128)S(1)}, u32[]{:S(2)}, u32[]{:S(2)}) collective-permute-start(s32[4]{0:T(128)S(1)} %copy-done.6), channel_id=1, source_target_pairs={{0,8},{8,0},{1,9},{9,1},{2,10},{10,2},{3,11},{11,3},{4,12},{12,4},... | collective-permute-start | bytes 56 | tf_op jit(solution)/shard_map/ppermute | solution.py:220
  105.7 0.8 collective-permute-done
  106.6 5.6 %all-to-all-done.3 = bf16[32,6,8,128]{3,2,1,0:T(8,128)(2,1)S(1)} async-done(((bf16[32,6,8,128]{3,2,1,0:T(8,128)(2,1)}), bf16[32,6,8,128]{3,2,1,0:T(8,128)(2,1)S(1)}, u32[]{:S(2)}, u32[]{:S(2)}) %all-to-all-start.3) | async-done | bytes 393248 | tf_op jit(solution)/shard_map/all_to_all | solution.py:270
  112.2 1.1 pack.1
  113.3 0.9 copy-done.2
  114.2 9.8 %all-to-all-start.4 = ((bf16[16,24,8,128]{3,2,1,0:T(8,128)(2,1)}), bf16[16,24,8,128]{3,2,1,0:T(8,128)(2,1)}, u32[]{:S(2)}, u32[]{:S(2)}) async-start(bf16[16,24,8,128]{3,2,1,0:T(8,128)(2,1)} %copy-done.2), calls=%async_computation.4 | async-start | bytes 1572864 | tf_op jit(solution)/shard_map/all_to_all | solution.py:288
  126.7 19.8 %all-to-all-done.4.y_ref = bf16[16,24,8,128]{3,2,1,0:T(8,128)(2,1)} async-done(((bf16[16,24,8,128]{3,2,1,0:T(8,128)(2,1)}), bf16[16,24,8,128]{3,2,1,0:T(8,128)(2,1)}, u32[]{:S(2)}, u32[]{:S(2)}) %all-to-all-start.4) | async-done | bytes 786464 | tf_op jit(solution)/shard_map/all_to_all | solution.py:288
  146.5 2.2 %copy-done.1 = bf16[1536,1408]{1,0:T(8,128)(2,1)S(1)} copy-done((bf16[1536,1408]{1,0:T(8,128)(2,1)S(1)}, bf16[1536,1408]{1,0:T(8,128)(2,1)}, u32[]{:S(2)}) %copy-start.1) | copy-done | bytes 4325400
  148.7 4.1 %deliver.1 = (bf16[1,256,1408]{2,1,0:T(8,128)(2,1)}, bf16[1,11,256]{2,1,0:T(8,128)(2,1)}) custom-call(s32[2]{0:T(128)S(1)} %pad_add_fusion.pick_ref, bf16[4,256,1408]{2,1,0:T(8,128)(2,1)S(1)} %copy-done, bf16[16,24,8,128]{3,2,1,0:T(8,128)(2,1)} %all-to-all-done.4.y_ref, bf16[16,96,1408]{2,1,0:T(8,128)(2,1)S(1)} %bitcast.23), custom_call_target="tpu_custom_call" | custom-call | tf_op jit(solution)/shard_map/deliver/pallas_call | solution.py:294
  (39 shorter events, 4.5 us)
Async XLA Ops:
  7.2 75.4 %all-gather.4.cloned.1.call-start = ((), (), s32[]{:S(2)}) async-start(), calls=%async_computation.5 | async-start | bytes 3244032 | tf_op jit(solution)/shard_map/all_gather | solution.py:219
  11.6 30.5 %copy-start.4 = (bf16[22,3,176]{2,0,1:T(8,128)(2,1)S(1)}, bf16[22,3,176]{2,0,1:T(8,128)(2,1)}, u32[]{:S(2)}) copy-start(bf16[22,3,176]{2,0,1:T(8,128)(2,1)} %param.6) | copy-start | bytes 69700
  11.6 30.6 %copy-start.5 = (bf16[176,22]{0,1:T(8,128)(2,1)S(1)}, bf16[176,22]{0,1:T(8,128)(2,1)}, u32[]{:S(2)}) copy-start(bf16[176,22]{0,1:T(8,128)(2,1)} %param.7) | copy-start | bytes 23236
  42.1 104.4 %all-gather.6.cloned.1.call-start = ((), (), s32[]{:S(2)}) async-start(), calls=%async_computation.6 | async-start | bytes 4595712 | tf_op jit(solution)/shard_map/all_gather | solution.py:252
  73.3 8.1 %collective-permute-start.1 = (bf16[1408,384]{1,0:T(8,128)(2,1)S(1)}, bf16[1408,384]{1,0:T(8,128)(2,1)S(1)}, u32[]{:S(2)}, u32[]{:S(2)}) collective-permute-start(bf16[1408,384]{1,0:T(8,128)(2,1)S(1)} %get-tuple-element.4.own_ref), channel_id=1, source_target_pairs={{0,8},{8,0},{1,9},{9,1},{2,10},{10,2},{3,11},{11,3},{4,12},{12,4},... | collective-permute-start | bytes 3244040 | tf_op jit(solution)/shard_map/ppermute | solution.py:251
  82.5 1.8 %copy-start.3 = (bf16[8,128,1408]{2,1,0:T(8,128)(2,1)S(1)}, bf16[8,128,1408]{2,1,0:T(8,128)(2,1)}, u32[]{:S(2)}) copy-start(bf16[8,128,1408]{2,1,0:T(8,128)(2,1)} %all-gather.4.cloned.1.call-done.tokens_ref) | copy-start | bytes 8650756
  84.4 16.4 %copy-start.6 = (s32[4]{0:T(128)S(1)}, s32[4]{0:T(128)}, u32[]{:S(2)}) copy-start(s32[4]{0:T(128)} %param.8) | copy-start | bytes 52
  90.6 55.9 %copy-start = (bf16[4,256,1408]{2,1,0:T(8,128)(2,1)S(1)}, bf16[4,256,1408]{2,1,0:T(8,128)(2,1)}, u32[]{:S(2)}) copy-start(bf16[4,256,1408]{2,1,0:T(8,128)(2,1)} %frame_ref.1) | copy-start | bytes 8650756
  90.6 21.6 %all-to-all-start.3 = ((bf16[32,6,8,128]{3,2,1,0:T(8,128)(2,1)}), bf16[32,6,8,128]{3,2,1,0:T(8,128)(2,1)S(1)}, u32[]{:S(2)}, u32[]{:S(2)}) async-start(bf16[32,6,8,128]{3,2,1,0:T(8,128)(2,1)} %bitcast.11), calls=%async_computation.3 | async-start | bytes 786432 | tf_op jit(solution)/shard_map/all_to_all | solution.py:270
  100.8 23.2 %copy-start.7 = (s32[4]{0:T(128)S(1)}, s32[4]{0:T(128)}, u32[]{:S(2)}) copy-start(s32[4]{0:T(128)} %param.9) | copy-start | bytes 52
  100.8 5.7 %collective-permute-start = (s32[4]{0:T(128)S(1)}, s32[4]{0:T(128)S(1)}, u32[]{:S(2)}, u32[]{:S(2)}) collective-permute-start(s32[4]{0:T(128)S(1)} %copy-done.6), channel_id=1, source_target_pairs={{0,8},{8,0},{1,9},{9,1},{2,10},{10,2},{3,11},{11,3},{4,12},{12,4},... | collective-permute-start | bytes 56 | tf_op jit(solution)/shard_map/ppermute | solution.py:220
  113.3 0.9 copy-start.2
  114.2 32.3 %all-to-all-start.4 = ((bf16[16,24,8,128]{3,2,1,0:T(8,128)(2,1)}), bf16[16,24,8,128]{3,2,1,0:T(8,128)(2,1)}, u32[]{:S(2)}, u32[]{:S(2)}) async-start(bf16[16,24,8,128]{3,2,1,0:T(8,128)(2,1)} %copy-done.2), calls=%async_computation.4 | async-start | bytes 1572864 | tf_op jit(solution)/shard_map/all_to_all | solution.py:288
  146.5 2.2 %copy-start.1 = (bf16[1536,1408]{1,0:T(8,128)(2,1)S(1)}, bf16[1536,1408]{1,0:T(8,128)(2,1)}, u32[]{:S(2)}) copy-start(bf16[1536,1408]{1,0:T(8,128)(2,1)} %all-gather.6.cloned.1.call-done) | copy-start | bytes 12976132
Sparse Core Ops, SparseCore 0:
  42.2 40.2 all-gather.3
  84.7 50.0 all-gather.5

commit v5 on v4

--- a/solution.py
+++ b/solution.py
@@ -9,7 +9,7 @@
 GROUP = 128
 MAIN = 64
 SLOT = 32
-ORDER, TRACK, PACK, DELIVER = 30, 40, 40, 30
+ORDER, TRACK, PACK, DELIVER = 30, 57, 40, 30
 FACTOR = 1.0 / HEAD_DIM**0.5
 CHIP = ("zh", "zl", "x")
 FRAME = CHIP + ("c",)
@@ -85,12 +85,12 @@
                 for late in range(2):
                     even, odd = (piece_of(side, owner, late, at) for at in range(2))
                     main = jnp.where(lane_o < MAIN, even, turn(odd, MAIN))
-                    out_ref[:, side, owner * 2 + late] = main.astype(BF16)
+                    out_ref[:, side, owner, late] = main.astype(BF16)
                     for at, piece in enumerate((even, odd)):
                         part = late * 2 + at
                         piece = turn(piece, SLOT * part - MAIN)
                         rest = piece if part == 0 else jnp.where(lane_o >= SLOT * part, piece, rest)
-                out_ref[:, side, 4 + owner] = rest.astype(BF16)
+                out_ref[:, side, owner, 2] = rest.astype(BF16)
 
 
 def half_turn(value):
@@ -110,32 +110,32 @@
 
     lane = lanes_of((pairs, 8, 128))
     lane_h = lanes_of((pairs // 2, 8, 128))
-    for fr in range(8):
-        place = (fr // 4) * 8 + owner_ref[fr]
-        tiles = [x_ref[:, side, fr // 2].astype(F32) for side in range(2)]
-        even, odd = (
-            [turn(tile, MAIN * head - MAIN * (fr % 2)) for head in range(2)] for tile in tiles
-        )
-        out_ref[place, :pairs] = join(even, odd, lane, MAIN).astype(BF16)
-        tiles = [x_ref[:, side, 4 + fr // 4].astype(F32) for side in range(2)]
-        rests = []
-        for half in range(2):
-            rows = slice(half * (pairs // 2), (half + 1) * (pairs // 2))
+    for fr in range(4):
+        place = owner_ref[fr]
+        for core in range(2):
+            tiles = [x_ref[:, side, core, fr // 2].astype(F32) for side in range(2)]
             even, odd = (
-                [
-                    turn(tile[rows], 2 * SLOT * half + SLOT * head - SLOT * (fr % 4))
-                    for head in range(2)
-                ]
-                for tile in tiles
+                [turn(tile, MAIN * head - MAIN * (fr % 2)) for head in range(2)] for tile in tiles
             )
-            rests.append(join(even, odd, lane_h, 2 * SLOT * half + SLOT))
-        rest = jnp.where(lane_h < 2 * SLOT, rests[0], rests[1])
-        out_ref[place, pairs:] = rest.astype(BF16)
+            out_ref[place, core, :pairs] = join(even, odd, lane, MAIN).astype(BF16)
+            tiles = [x_ref[:, side, core, 2].astype(F32) for side in range(2)]
+            rests = []
+            for half in range(2):
+                rows = slice(half * (pairs // 2), (half + 1) * (pairs // 2))
+                even, odd = (
+                    [
+                        turn(tile[rows], 2 * SLOT * half + SLOT * head - SLOT * fr)
+                        for head in range(2)
+                    ]
+                    for tile in tiles
+                )
+                rests.append(join(even, odd, lane_h, 2 * SLOT * half + SLOT))
+            rest = jnp.where(lane_h < 2 * SLOT, rests[0], rests[1])
+            out_ref[place, core, pairs:] = rest.astype(BF16)
 
 
 def deliver_kernel(pick_ref, frame_ref, y_ref, weight_ref, out_ref, scale_ref):
-    sources = y_ref.shape[0]
-    heads = sources // 2
+    heads = y_ref.shape[0]
     patches, width = frame_ref.shape[1:]
     half = patches // 2
     tiles = half // 8
@@ -150,11 +150,11 @@
 
     mains, rests = [], []
     for at in range(heads):
-        pair = [y_ref[core * heads + at, :tiles].astype(F32) for core in range(2)]
+        pair = [y_ref[at, core, :tiles].astype(F32) for core in range(2)]
         mains.append(weave(*pair).astype(BF16))
     for at in range(0, heads, 2):
         first, second = (
-            weave(*(y_ref[core * heads + one, tiles:].astype(F32) for core in range(2)))
+            weave(*(y_ref[one, core, tiles:].astype(F32) for core in range(2)))
             for one in (at, at + 1)
         )
         low = jnp.where(lane < MAIN, first, turn(second, MAIN))
@@ -206,18 +206,22 @@
     core = lax.axis_index("c")
     position = lax.axis_index("pool")
     chips = lax.axis_size("zh") * lax.axis_size("zl") * lax.axis_size("x")
-    sources = 2 * lax.axis_size("pool")
+    pool = lax.axis_size("pool")
     swap = [(0, 1), (1, 0)]
 
-    share = lax.dynamic_slice_in_dim(frames_in, (position % 2) * 2, 2, 0)
-    share = share.reshape(2, chips, 8, width)
+    grid = frames_in.reshape(2, 2, chips, 8, width)
     share = jnp.concatenate(
-        [lax.dynamic_slice_in_dim(share, position // 2 + at, 1, 2) for at in (0, 4)], axis=2
+        [
+            lax.dynamic_slice(
+                grid, (position % 2, 0, 0, position // 2 + at, 0), (1, 2, chips, 1, width)
+            )[0]
+            for at in (0, 4)
+        ],
+        axis=2,
     )
     share = normalise(share).transpose(1, 2, 0, 3).reshape(2 * chips, 2, width)
     share = lax.all_to_all(share, FRAME, 0, 0, tiled=True).reshape(4 * chips, width)
     tracks = lax.all_gather(share, "pool", axis=0, tiled=False)
-    owners_other = lax.ppermute(owners, "c", swap)
 
     parts = qkv_weight.reshape(rows_here, 3, 2, HEAD_DIM)
     query, key, value = parts[:, 0], parts[:, 1], parts[:, 2]
@@ -260,20 +264,15 @@
             pl.BlockSpec(mine.shape, lambda p: (0, 0)),
             pl.BlockSpec(mine.shape, lambda p: (0, 0)),
         ],
-        out_specs=pl.BlockSpec((chips // 2, 2, 6, 8, 128), lambda p: (0, 0, 0, 0, 0)),
-        out_shape=jax.ShapeDtypeStruct((chips // 2, 2, 6, 8, 128), BF16),
+        out_specs=pl.BlockSpec((chips // 2, 2, 2, 3, 8, 128), lambda p: (0, 0, 0, 0, 0, 0)),
+        out_shape=jax.ShapeDtypeStruct((chips // 2, 2, 2, 3, 8, 128), BF16),
         scratch_shapes=[pltpu.VMEM((chips, 64, 128), F32)],
         compiler_params=params(TRACK),
         name="track",
     )(core.reshape(1), tracks, mine, mine_other)
-    attended = attended.reshape(chips, 6, 8, 128)
-    returned = lax.all_to_all(attended, CHIP, 0, 0, tiled=True)
-
-    pair = jnp.where(
-        core == 0,
-        jnp.concatenate([owners, owners_other]),
-        jnp.concatenate([owners_other, owners]),
-    )
+    attended = attended.reshape(2 * chips, 3, 8, 128)
+    returned = lax.all_to_all(attended, FRAME, 0, 0, tiled=True)
+
     packed = pl.pallas_call(
         pack_kernel,
         in_specs=[
@@ -281,11 +280,11 @@
             pl.BlockSpec(memory_space=pltpu.VMEM),
         ],
         out_specs=pl.BlockSpec(memory_space=pltpu.VMEM),
-        out_shape=jax.ShapeDtypeStruct((sources, 3 * chips // 4, 8, 128), BF16),
+        out_shape=jax.ShapeDtypeStruct((pool, 2, 3 * chips // 4, 8, 128), BF16),
         compiler_params=params(PACK),
         name="pack",
-    )(pair, returned.reshape(chips // 2, 2, 6, 8, 128))
-    gathered = lax.all_to_all(packed, ("c", "pool"), 0, 0, tiled=True)
+    )(owners, returned.reshape(chips // 2, 2, 2, 3, 8, 128))
+    gathered = lax.all_to_all(packed, "pool", 0, 0, tiled=True)
 
     match = (owners == position) & (slots == 0)
     chosen = jnp.sum(jnp.where(match, jnp.arange(fr_count, dtype=jnp.int32), 0))
@@ -298,7 +297,7 @@
             grid=(1,),
             in_specs=[
                 pl.BlockSpec((1, patch_count, width), lambda g, pick: (pick[0], 0, 0)),
-                pl.BlockSpec(gathered.shape, lambda g, pick: (0, 0, 0, 0)),
+                pl.BlockSpec(gathered.shape, lambda g, pick: (0, 0, 0, 0, 0)),
                 pl.BlockSpec(out_rows.shape, lambda g, pick: (0, 0, 0)),
             ],
             out_specs=[

time: 160 us -> 160 us (level)
  blocking collectives: 58.2 us -> 86.6 us
  starting transfers between devices: 30.8 us -> 10.1 us
  waiting for transfers between devices: 29.7 us -> 23.1 us
  Pallas kernels: 12.6 us -> 14.5 us
    all_to_all x0 -> x1, blocking collectives: none -> 28.4 us  [local(): returned = lax.all_to_all(attended, FRAME, 0, 0, tiled=True)]
    all_to_all x2 -> x1, starting transfers between devices: 19.9 us -> 4.23 us  [local(): gathered = lax.all_to_all(packed, 'pool', 0, 0, tiled=True)]
    all_to_all x2 -> x1, waiting for transfers between devices: 25.5 us -> 19.6 us  [local(): gathered = lax.all_to_all(packed, 'pool', 0, 0, tiled=True)]
    ppermute x1 -> x0, starting transfers between devices: 4.94 us -> none  [local(): owners_other = lax.ppermute(owners, 'c', swap)]
    reshape x2 -> x0, local copies, waits for them, and re-layouts: 1.85 us -> none  [the longest x1 1.47 us: local(): share = share.reshape(2, chips, 8, width)]
    pallas_call x1, Pallas kernels: 6.25 us -> 8.09 us  [local(): pl.pallas_call(track_kernel, grid=(4,), in_specs=[pl.BlockSpec(memory_spa...]
    dynamic_slice x1, local copies, waits for them, and re-layouts: 0.75 us -> 2.55 us  [local(): lax.dynamic_slice(grid, (position % 2, 0, 0, position // 2 + at, 0), (1,...]
    unnamed x17 -> x20, local copies, waits for them, and re-layouts: 4.98 us -> 3.23 us
  transfers between devices with their start and end apart: 6 -> 4, of which waited for: 5 -> 3; matrix products, arithmetic and copies ran while one was open for 2% -> 2% of each run, Pallas kernels for 5% -> 6%
where the time goes in v5:
time: 160 us
  blocking collectives  86.6 us (54%)
  waiting for transfers between devices  23.1 us (14%)
  between operations  14.9 us (9%)
  Pallas kernels  14.5 us (9%)
  starting transfers between devices  10.1 us (6%)
  local copies, waits for them, and re-layouts  7.79 us (5%)
  other arithmetic  2.61 us (2%)
    all_to_all x1, blocking collectives, local(): lax.all_to_all(share, FRAME, 0, 0, tiled=True).reshape(4 * chips, width)  29.2 us
    all_to_all x1, blocking collectives, local(): returned = lax.all_to_all(attended, FRAME, 0, 0, tiled=True)  28.4 us
    all_to_all x2, blocking collectives, spread(): return lax.all_to_all(copies, axis, 0, 0, tiled=True)  27.2 us
    all_to_all x1, waiting for transfers between devices, local(): gathered = lax.all_to_all(packed, 'pool', 0, 0, tiled=True)  19.6 us
    pallas_call x1, Pallas kernels, local(): pl.pallas_call(track_kernel, grid=(4,), in_specs=[pl.BlockSpec(memory_spa...  8.09 us
    ppermute x1, starting transfers between devices, local(): mine_other = lax.ppermute(mine, 'c', swap)  5.79 us
    all_to_all x1, starting transfers between devices, local(): gathered = lax.all_to_all(packed, 'pool', 0, 0, tiled=True)  4.23 us
    pallas_call x1, Pallas kernels, local(): pl.pallas_call(deliver_kernel, grid_spec=pltpu.PrefetchScalarGridSpec(num...  4.13 us
  transfers between devices with their start and end apart: 4, of which 3 were waited for; matrix products, arithmetic and copies ran while one was open for 2% of the time, Pallas kernels for 6%

profile of v5, /device:TPU:1, one launch (start us, length us, event | category | flops | bytes accessed | tf_op | source)
XLA Modules:
  0.0 159.5 jit_solution(4245327848073201691)
XLA Ops:
  7.2 2.5 %constant_dynamic-slice_fusion.2 = (bf16[1,2,32,1,1408]{4,3,2,1,0:T(2,128)(2,1)S(1)}, bf16[1,2,32,1,1408]{4,3,2,1,0:T(2,128)(2,1)S(1)}) fusion(bf16[2,2,32,8,1408]{4,3,2,1,0:T(8,128)(2,1)} %bitcast.26, s32[]{:T(128)S(6)} %select_n.34, s32[]{:T(128)S(6)} %select_n.36, s32[]{:T(128)S(6)} %select_n.37), kind=kLoop, calls=%fused_computation.19 | loop fusion | bytes 720908 | tf_op jit(solution)/shard_map/dynamic_slice | solution.py:215
  10.0 0.2 fusion.2
  10.5 0.3 copy.8
  10.8 29.2 %all_to_all.25 = bf16[64,2,1408]{2,1,0:T(2,128)(2,1)S(1)} all-to-all(bf16[64,2,1408]{2,1,0:T(2,128)(2,1)S(1)} %bitcast.30), channel_id=1, replica_groups=mesh['zh'=4,'zl'=2,'x'=4,'c'=2,'pool'=8] {'zh','zl','x','c'}, dimensions={0} | all-to-all | bytes 720896 | tf_op jit(solution)/shard_map/all_to_all | solution.py:223
  40.0 0.9 all_gather_reshape.3
  41.4 0.2 concatenate.7
  41.6 1.9 %all_gather.13 = bf16[44,2,384]{2,1,0:T(2,128)(2,1)S(1)} all-gather(bf16[22,2,384]{2,1,0:T(2,128)(2,1)S(1)} %concatenate.7), channel_id=1, replica_groups=mesh['zh'=4,'zl'=2,'x'=4,'c'=2,'pool'=8] {'c'}, dimensions={0}, use_global_device_ids=true | all-gather | bytes 101376 | tf_op jit(solution)/shard_map/all_gather | solution.py:241
  43.6 10.7 %all_to_all.26 = bf16[4,44,384]{2,1,0:T(8,128)(2,1)S(1)} all-to-all(bf16[4,44,384]{2,1,0:T(8,128)(2,1)S(1)} %broadcast_in_dim.24), channel_id=1, replica_groups=mesh['zh'=4,'zl'=2,'x'=4,'c'=2,'pool'=8] {'zh'}, dimensions={0} | all-to-all | bytes 270336 | tf_op jit(solution)/shard_map/all_to_all | solution.py:34
  54.4 16.4 %all_to_all.27.source_ref = bf16[8,176,384]{2,1,0:T(8,128)(2,1)S(1)} all-to-all(bf16[8,176,384]{2,1,0:T(8,128)(2,1)S(1)} %broadcast_in_dim.26), channel_id=1, replica_groups=mesh['zh'=4,'zl'=2,'x'=4,'c'=2,'pool'=8] {'zl','x'}, dimensions={0} | all-to-all | bytes 2162688 | tf_op jit(solution)/shard_map/all_to_all | solution.py:34
  70.9 1.2 order.1
  72.1 5.8 %collective-permute-start = (bf16[1408,384]{1,0:T(8,128)(2,1)S(1)}, bf16[1408,384]{1,0:T(8,128)(2,1)S(1)}, u32[]{:S(2)}, u32[]{:S(2)}) collective-permute-start(bf16[1408,384]{1,0:T(8,128)(2,1)S(1)} %get-tuple-element.4.own_ref), channel_id=1, source_target_pairs={{0,8},{8,0},{1,9},{9,1},{2,10},{10,2},{3,11},{11,3},{4,12},{12,4},... | collective-permute-start | bytes 3244040 | tf_op jit(solution)/shard_map/ppermute | solution.py:255
  77.9 2.3 %collective-permute-done.other_ref = bf16[1408,384]{1,0:T(8,128)(2,1)S(1)} collective-permute-done((bf16[1408,384]{1,0:T(8,128)(2,1)S(1)}, bf16[1408,384]{1,0:T(8,128)(2,1)S(1)}, u32[]{:S(2)}, u32[]{:S(2)}) %collective-permute-start) | collective-permute-done | bytes 1081376 | tf_op jit(solution)/shard_map/ppermute | solution.py:255
  80.2 1.1 all-gather.4.cloned.1.call-done.tokens_ref
  81.3 8.1 %track.1 = bf16[16,2,2,3,8,128]{5,4,3,2,1,0:T(8,128)(2,1)} custom-call(s32[1]{0:T(128)} %bitcast.2.core_ref, bf16[8,128,1408]{2,1,0:T(8,128)(2,1)} %all-gather.4.cloned.1.call-done.tokens_ref, bf16[1408,384]{1,0:T(8,128)(2,1)} %copy-done.3, bf16[1408,384]{1,0:T(8,128)(2,1)} %copy-done.5), custom_call_target="tpu_custom_call" | custom-call | tf_op jit(solution)/shard_map/track/pallas_call | solution.py:258
  89.4 28.4 %all_to_all.28 = bf16[64,3,8,128]{3,2,1,0:T(8,128)(2,1)S(1)} all-to-all(bf16[64,3,8,128]{3,2,1,0:T(8,128)(2,1)} %bitcast.29), channel_id=1, replica_groups=mesh['zh'=4,'zl'=2,'x'=4,'c'=2,'pool'=8] {'zh','zl','x','c'}, dimensions={0} | all-to-all | bytes 786432 | tf_op jit(solution)/shard_map/all_to_all | solution.py:274
  117.8 1.1 pack.1
  118.9 0.9 copy-done.2
  119.8 4.2 %all-to-all-start.4 = ((bf16[8,2,24,8,128]{4,3,2,1,0:T(8,128)(2,1)}), bf16[8,2,24,8,128]{4,3,2,1,0:T(8,128)(2,1)}, u32[]{:S(2)}, u32[]{:S(2)}) async-start(bf16[8,2,24,8,128]{4,3,2,1,0:T(8,128)(2,1)} %copy-done.2), calls=%async_computation.4 | async-start | bytes 1572864 | tf_op jit(solution)/shard_map/all_to_all | solution.py:287
  124.1 0.6 select_reduce_fusion
  124.7 0.6 reduce_or.9
  126.0 0.7 pad_add_fusion.pick_ref
  126.7 19.6 %all-to-all-done.4.y_ref = bf16[8,2,24,8,128]{4,3,2,1,0:T(8,128)(2,1)} async-done(((bf16[8,2,24,8,128]{4,3,2,1,0:T(8,128)(2,1)}), bf16[8,2,24,8,128]{4,3,2,1,0:T(8,128)(2,1)}, u32[]{:S(2)}, u32[]{:S(2)}) %all-to-all-start.4) | async-done | bytes 786464 | tf_op jit(solution)/shard_map/all_to_all | solution.py:287
  146.3 2.2 %copy-done.1 = bf16[1536,1408]{1,0:T(8,128)(2,1)S(1)} copy-done((bf16[1536,1408]{1,0:T(8,128)(2,1)S(1)}, bf16[1536,1408]{1,0:T(8,128)(2,1)}, u32[]{:S(2)}) %copy-start.1) | copy-done | bytes 4325400
  148.6 4.1 %deliver.1 = (bf16[1,256,1408]{2,1,0:T(8,128)(2,1)}, bf16[1,11,256]{2,1,0:T(8,128)(2,1)}) custom-call(s32[2]{0:T(128)S(1)} %pad_add_fusion.pick_ref, bf16[4,256,1408]{2,1,0:T(8,128)(2,1)S(1)} %copy-done, bf16[8,2,24,8,128]{4,3,2,1,0:T(8,128)(2,1)} %all-to-all-done.4.y_ref, bf16[16,96,1408]{2,1,0:T(8,128)(2,1)S(1)} %bitcast.27), custom_call_target="tpu_custom_call" | custom-call | tf_op jit(solution)/shard_map/deliver/pallas_call | solution.py:293
  (37 shorter events, 1.2 us)
Async XLA Ops:
  7.2 74.2 %all-gather.4.cloned.1.call-start = ((), (), s32[]{:S(2)}) async-start(), calls=%async_computation.5 | async-start | bytes 3244032 | tf_op jit(solution)/shard_map/all_gather | solution.py:224
  9.8 31.1 %copy-start.6 = (bf16[22,3,176]{2,0,1:T(8,128)(2,1)S(1)}, bf16[22,3,176]{2,0,1:T(8,128)(2,1)}, u32[]{:S(2)}) copy-start(bf16[22,3,176]{2,0,1:T(8,128)(2,1)} %param.6) | copy-start | bytes 69700
  9.8 31.2 %copy-start.7 = (bf16[176,22]{0,1:T(8,128)(2,1)S(1)}, bf16[176,22]{0,1:T(8,128)(2,1)}, u32[]{:S(2)}) copy-start(bf16[176,22]{0,1:T(8,128)(2,1)} %param.7) | copy-start | bytes 23236
  40.9 105.5 %all-gather.6.cloned.1.call-start = ((), (), s32[]{:S(2)}) async-start(), calls=%async_computation.6 | async-start | bytes 4595712 | tf_op jit(solution)/shard_map/all_gather | solution.py:256
  72.0 9.3 %copy-start.3 = (bf16[1408,384]{1,0:T(8,128)(2,1)}, bf16[1408,384]{1,0:T(8,128)(2,1)S(1)}, u32[]{:S(2)}) copy-start(bf16[1408,384]{1,0:T(8,128)(2,1)S(1)} %get-tuple-element.4.own_ref) | copy-start | bytes 3244036
  72.1 8.1 %collective-permute-start = (bf16[1408,384]{1,0:T(8,128)(2,1)S(1)}, bf16[1408,384]{1,0:T(8,128)(2,1)S(1)}, u32[]{:S(2)}, u32[]{:S(2)}) collective-permute-start(bf16[1408,384]{1,0:T(8,128)(2,1)S(1)} %get-tuple-element.4.own_ref), channel_id=1, source_target_pairs={{0,8},{8,0},{1,9},{9,1},{2,10},{10,2},{3,11},{11,3},{4,12},{12,4},... | collective-permute-start | bytes 3244040 | tf_op jit(solution)/shard_map/ppermute | solution.py:255
  80.2 1.1 copy-start.5
  81.3 36.5 %copy-start.4 = (s32[4]{0:T(128)S(1)}, s32[4]{0:T(128)}, u32[]{:S(2)}) copy-start(s32[4]{0:T(128)} %owner_ref.1) | copy-start | bytes 52
  89.4 34.7 %copy-start.8 = (s32[4]{0:T(128)S(1)}, s32[4]{0:T(128)}, u32[]{:S(2)}) copy-start(s32[4]{0:T(128)} %param.9) | copy-start | bytes 52
  89.4 56.9 %copy-start = (bf16[4,256,1408]{2,1,0:T(8,128)(2,1)S(1)}, bf16[4,256,1408]{2,1,0:T(8,128)(2,1)}, u32[]{:S(2)}) copy-start(bf16[4,256,1408]{2,1,0:T(8,128)(2,1)} %frame_ref.1) | copy-start | bytes 8650756
  118.9 0.9 copy-start.2
  119.8 26.5 %all-to-all-start.4 = ((bf16[8,2,24,8,128]{4,3,2,1,0:T(8,128)(2,1)}), bf16[8,2,24,8,128]{4,3,2,1,0:T(8,128)(2,1)}, u32[]{:S(2)}, u32[]{:S(2)}) async-start(bf16[8,2,24,8,128]{4,3,2,1,0:T(8,128)(2,1)} %copy-done.2), calls=%async_computation.4 | async-start | bytes 1572864 | tf_op jit(solution)/shard_map/all_to_all | solution.py:287
  146.3 2.2 %copy-start.1 = (bf16[1536,1408]{1,0:T(8,128)(2,1)S(1)}, bf16[1536,1408]{1,0:T(8,128)(2,1)}, u32[]{:S(2)}) copy-start(bf16[1536,1408]{1,0:T(8,128)(2,1)} %all-gather.6.cloned.1.call-done) | copy-start | bytes 12976132
Sparse Core Ops, SparseCore 0:
  41.0 40.2 all-gather.3
  83.4 45.9 all-gather.5

commit v6 on v1

--- a/solution.py
+++ b/solution.py
@@ -11,10 +11,11 @@
 GROUP = 128
 MAIN = 64
 SLOT = 32
+NORMALISE, ORDER, PROJECT = 57, 30, 57
+ATTEND, PACK, DELIVER = 40, 40, 30
 FACTOR = 1.0 / HEAD_DIM**0.5
 CHIP = ("zh", "zl", "x")
 FRAME = CHIP + ("c",)
-VMEM_LIMIT = 40 * 1024 * 1024
 F32 = jnp.float32
 BF16 = jnp.bfloat16
 
@@ -36,6 +37,29 @@
     return lax.all_to_all(copies, axis, 0, 0, tiled=True)
 
 
+def normalise_kernel(own_ref, other_ref, own_out, other_out, mark_ref):
+    for source, target in ((own_ref, own_out), (other_ref, other_out)):
+        rows = source[0].astype(F32)
+        mean = jnp.mean(rows, axis=-1, keepdims=True)
+        centred = rows - mean
+        var = jnp.mean(centred * centred, axis=-1, keepdims=True)
+        target[0] = (centred * lax.rsqrt(var + 1e-06)).astype(BF16)
+    mark_ref[...] = jnp.zeros_like(mark_ref)
+
+
+def order_kernel(source_ref, mark_ref, right_ref, back_ref, order_ref):
+    inner, height = source_ref.shape[:2]
+    outer = 4
+    rows = height // outer
+    for low in range(inner):
+        block = source_ref[low].astype(F32)
+        for high in range(outer):
+            start = (high * inner + low) * rows
+            order_ref[start : start + rows, :] = block[high * rows : (high + 1) * rows]
+    right_ref[...] = order_ref[...].astype(BF16)
+    back_ref[...] = order_ref[:, 256:384].T[32:].astype(BF16)
+
+
 def project_kernel(core_ref, own_ref, other_ref, weight_ref, out_ref, rest_ref):
     step = pl.program_id(0)
     core = core_ref[0]
@@ -48,11 +72,11 @@
     lane = lanes_of(rest_ref.shape)
     for which, ref in enumerate((own_ref, other_ref)):
         frame = (core if which == 0 else 1 - core) * 4 + step
-        rows = jnp.dot(ref[0], weight_ref[...], preferred_element_type=F32)
+        out = jnp.dot(ref[0], weight_ref[...], preferred_element_type=F32)
         for tile in range(2):
-            block = rows[:, tile * 128 : (tile + 1) * 128].astype(BF16)
+            block = out[:, tile * 128 : (tile + 1) * 128].astype(BF16)
             out_ref[:, 2 * frame + tile] = block.reshape(chips, 8, 128)
-        rest = jnp.where(lane < 8, rows[:, 256:384], 0.0)
+        rest = jnp.where(lane < 8, out[:, 256:384], 0.0)
         rest_ref[...] += pltpu.roll(rest, 8 * frame, 1)
 
     @pl.when(step == pl.num_programs(0) - 1)
@@ -175,8 +199,8 @@
     scale_ref[0] = scales[: width // GROUP].astype(BF16)
 
 
-def params():
-    return pltpu.CompilerParams(vmem_limit_bytes=VMEM_LIMIT)
+def params(mebibytes):
+    return pltpu.CompilerParams(vmem_limit_bytes=mebibytes * 1024 * 1024)
 
 
 def local(frames_in, qkv_weight, out_weight, owners, slots):
@@ -188,12 +212,21 @@
     sources = 2 * lax.axis_size("pool")
     swap = [(0, 1), (1, 0)]
 
-    xf = frames_in.astype(F32)
-    mean = jnp.mean(xf, axis=-1, keepdims=True)
-    centred = xf - mean
-    var = jnp.mean(centred * centred, axis=-1, keepdims=True)
-    normed = (centred * lax.rsqrt(var + 1e-06)).astype(BF16)
-    normed_other = lax.ppermute(normed, "c", swap)
+    frames_other = lax.ppermute(frames_in, "c", swap)
+    frame_spec = pl.BlockSpec((1, patch_count, width), lambda j: (j, 0, 0))
+    normed, normed_other, mark = pl.pallas_call(
+        normalise_kernel,
+        grid=(fr_count,),
+        in_specs=[frame_spec, frame_spec],
+        out_specs=[frame_spec, frame_spec, pl.BlockSpec((8, 128), lambda j: (0, 0))],
+        out_shape=[
+            jax.ShapeDtypeStruct(frames_in.shape, BF16),
+            jax.ShapeDtypeStruct(frames_in.shape, BF16),
+            jax.ShapeDtypeStruct((8, 128), F32),
+        ],
+        compiler_params=params(NORMALISE),
+        name="normalise",
+    )(frames_in, frames_other)
     owners_other = lax.ppermute(owners, "c", swap)
 
     parts = qkv_weight.reshape(rows_here, 3, 2, HEAD_DIM)
@@ -217,32 +250,40 @@
     mine = lax.dynamic_index_in_dim(both, core, 1, keepdims=False)
     mine = spread(mine, "zh").reshape(-1, mine.shape[-1])
     mine = spread(mine, ("zl", "x"))
-    mine = mine.reshape(8, 4, 2 * rows_here, -1).transpose(1, 0, 2, 3).reshape(width, -1)
-
+    mine, back = pl.pallas_call(
+        order_kernel,
+        out_shape=[
+            jax.ShapeDtypeStruct((width, 384), BF16),
+            jax.ShapeDtypeStruct((96, width), BF16),
+        ],
+        scratch_shapes=[pltpu.VMEM((width, 384), F32)],
+        compiler_params=params(ORDER),
+        name="order",
+    )(mine, mark)
     projected = pl.pallas_call(
         project_kernel,
         grid=(fr_count,),
         in_specs=[
             pl.BlockSpec(memory_space=pltpu.SMEM),
-            pl.BlockSpec((1, patch_count, width), lambda j: (j, 0, 0)),
-            pl.BlockSpec((1, patch_count, width), lambda j: (j, 0, 0)),
-            pl.BlockSpec((width, 384), lambda j: (0, 0)),
+            frame_spec,
+            frame_spec,
+            pl.BlockSpec(mine.shape, lambda j: (0, 0)),
         ],
         out_specs=pl.BlockSpec((chips, 17, 8, 128), lambda j: (0, 0, 0, 0)),
         out_shape=jax.ShapeDtypeStruct((chips, 17, 8, 128), BF16),
         scratch_shapes=[pltpu.VMEM((patch_count, 128), F32)],
-        compiler_params=params(),
+        compiler_params=params(PROJECT),
         name="project",
     )(core.reshape(1), normed, normed_other, mine)
     tracks = lax.all_to_all(projected, CHIP, 0, 0, tiled=True)
 
-    out_rows = lax.all_gather(mine[:, 288:].T, ("c", "pool"), axis=0, tiled=False)
+    out_rows = lax.all_gather(back, ("c", "pool"), axis=0, tiled=False)
 
     attended = pl.pallas_call(
         attend_kernel,
         out_shape=jax.ShapeDtypeStruct((chips, 6, 8, 128), BF16),
         scratch_shapes=[pltpu.VMEM((chips, 64, 128), F32)] * 4,
-        compiler_params=params(),
+        compiler_params=params(ATTEND),
         name="attend",
     )(tracks)
     returned = lax.all_to_all(attended, CHIP, 0, 0, tiled=True)
@@ -260,7 +301,7 @@
         ],
         out_specs=pl.BlockSpec(memory_space=pltpu.VMEM),
         out_shape=jax.ShapeDtypeStruct((sources, 3 * chips // 4, 8, 128), BF16),
-        compiler_params=params(),
+        compiler_params=params(PACK),
         name="pack",
     )(pair, returned)
     gathered = lax.all_to_all(packed, ("c", "pool"), 0, 0, tiled=True)
@@ -288,7 +329,7 @@
             jax.ShapeDtypeStruct((1, patch_count, width), BF16),
             jax.ShapeDtypeStruct((1, groups, patch_count), BF16),
         ],
-        compiler_params=params(),
+        compiler_params=params(DELIVER),
         name="deliver",
     )(pick, frames_in, gathered, out_rows)
 

time: 174 us -> 168 us (0.966)
  Pallas kernels: 11.5 us -> 22.4 us
  waiting for transfers between devices: 42.9 us -> 32 us
  local copies, waits for them, and re-layouts: 14.2 us -> 8.82 us
  starting transfers between devices: 29.9 us -> 32.4 us
  other arithmetic: 4.17 us -> 2.06 us
    pallas_call x0 -> x2, Pallas kernels: none -> 7.81 us  [the longest x1 6.9 us: local(): pl.pallas_call(normalise_kernel, grid=(fr_count,), in_specs=[frame_spec,...]
    all_to_all x1, waiting for transfers between devices: 10.2 us -> 4.3 us  [spread(): return lax.all_to_all(copies, axis, 0, 0, tiled=True)]
    all_gather x1, blocking collectives: 8.39 us -> 2.84 us  [local(): both = lax.all_gather(payload, 'c', axis=0, tiled=True)]
    ppermute x1, waiting for transfers between devices: 4.89 us -> 0.01 us  [local(): frames_other = lax.ppermute(frames_in, 'c', swap)]
    all_to_all x1, blocking collectives: 35.1 us -> 39.6 us  [local(): tracks = lax.all_to_all(projected, CHIP, 0, 0, tiled=True)]
    transpose x3 -> x0, local copies, waits for them, and re-layouts: 3.24 us -> none  [the longest x2 2.04 us: local(): mine[:, 288:]]
    pallas_call x1, Pallas kernels: 4.12 us -> 7.19 us  [local(): pl.pallas_call(project_kernel, grid=(fr_count,), in_specs=[pl.BlockSpec(m...]
    ppermute x1, starting transfers between devices: 6.47 us -> 8.79 us  [local(): frames_other = lax.ppermute(frames_in, 'c', swap)]
  transfers between devices with their start and end apart: 6 -> 6, of which waited for: 5 -> 4; matrix products, arithmetic and copies ran while one was open for 2% -> 3% of each run, Pallas kernels for 4% -> 10%
where the time goes in v6:
time: 168 us; the launch traced here: 167 us
  blocking collectives  54.3 us (32%)
  starting transfers between devices  32.4 us (19%)
  waiting for transfers between devices  32 us (19%)
  Pallas kernels  22.4 us (13%)
  between operations  14.8 us (9%)
  local copies, waits for them, and re-layouts  8.82 us (5%)
  other arithmetic  2.06 us (1%)
    all_to_all x1, blocking collectives, local(): tracks = lax.all_to_all(projected, CHIP, 0, 0, tiled=True)  39.6 us
    all_to_all x1, waiting for transfers between devices, local(): gathered = lax.all_to_all(packed, ('c', 'pool'), 0, 0, tiled=True)  18.7 us
    all_to_all x1, blocking collectives, spread(): return lax.all_to_all(copies, axis, 0, 0, tiled=True)  11.9 us
    all_to_all x1, starting transfers between devices, local(): gathered = lax.all_to_all(packed, ('c', 'pool'), 0, 0, tiled=True)  10.4 us
    ppermute x1, starting transfers between devices, local(): frames_other = lax.ppermute(frames_in, 'c', swap)  8.79 us
    all_to_all x1, waiting for transfers between devices, local(): returned = lax.all_to_all(attended, CHIP, 0, 0, tiled=True)  8.18 us
    pallas_call x1, Pallas kernels, local(): pl.pallas_call(project_kernel, grid=(fr_count,), in_specs=[pl.BlockSpec(m...  7.19 us
    pallas_call x1, Pallas kernels, local(): pl.pallas_call(normalise_kernel, grid=(fr_count,), in_specs=[frame_spec,...  6.9 us
  transfers between devices with their start and end apart: 6, of which 4 were waited for; matrix products, arithmetic and copies ran while one was open for 3% of the time, Pallas kernels for 10%

profile of v6, /device:TPU:1, one launch (start us, length us, event | category | flops | bytes accessed | tf_op | source)
XLA Modules:
  0.0 166.8 jit_solution(2450364152588911116)
XLA Ops:
  7.2 8.8 %collective-permute-start.1 = (bf16[4,256,1408]{2,1,0:T(8,128)(2,1)}, bf16[4,256,1408]{2,1,0:T(8,128)(2,1)}, u32[]{:S(2)}, u32[]{:S(2)}) collective-permute-start(bf16[4,256,1408]{2,1,0:T(8,128)(2,1)} %frame_ref.1), channel_id=1, source_target_pairs={{0,8},{8,0},{1,9},{9,1},{2,10},{10,2},{3,11},{11,3},{4,12},{12,4},... | collective-permute-start | bytes 8650760 | tf_op jit(solution)/shard_map/ppermute | solution.py:215
  16.0 0.9 reshape.17
  17.0 0.8 reshape.18
  18.1 2.8 %all_gather.9 = bf16[44,2,384]{2,1,0:T(2,128)(2,1)S(1)} all-gather(bf16[22,2,384]{2,1,0:T(2,128)(2,1)S(1)} %concatenate.12), channel_id=1, replica_groups=mesh['zh'=4,'zl'=2,'x'=4,'c'=2,'pool'=8] {'c'}, dimensions={0}, use_global_device_ids=true | all-gather | bytes 101376 | tf_op jit(solution)/shard_map/all_gather | solution.py:249
  21.0 11.9 %all_to_all.25 = bf16[4,44,384]{2,1,0:T(8,128)(2,1)S(1)} all-to-all(bf16[4,44,384]{2,1,0:T(8,128)(2,1)S(1)} %broadcast_in_dim.26), channel_id=1, replica_groups=mesh['zh'=4,'zl'=2,'x'=4,'c'=2,'pool'=8] {'zh'}, dimensions={0} | all-to-all | bytes 270336 | tf_op jit(solution)/shard_map/all_to_all | solution.py:37
  32.9 1.1 broadcast_in_dim.28
  34.0 4.9 %all-to-all-start.1 = ((bf16[8,176,384]{2,1,0:T(8,128)(2,1)}), bf16[8,176,384]{2,1,0:T(8,128)(2,1)S(1)}, u32[]{:S(2)}, u32[]{:S(2)}) async-start(bf16[8,176,384]{2,1,0:T(8,128)(2,1)} %broadcast_in_dim.28), calls=%async_computation.1 | async-start | bytes 2162688 | tf_op jit(solution)/shard_map/all_to_all | solution.py:37
  39.0 6.9 %normalise.1 = (bf16[4,256,1408]{2,1,0:T(8,128)(2,1)}, bf16[4,256,1408]{2,1,0:T(8,128)(2,1)}, f32[8,128]{1,0:T(8,128)}) custom-call(bf16[4,256,1408]{2,1,0:T(8,128)(2,1)} %frame_ref.1, bf16[4,256,1408]{2,1,0:T(8,128)(2,1)} %collective-permute-done.1.other_ref), custom_call_target="tpu_custom_call" | custom-call | tf_op jit(solution)/shard_map/normalise/pallas_call | solution.py:217
  45.9 4.3 %all-to-all-done.1.source_ref = bf16[8,176,384]{2,1,0:T(8,128)(2,1)S(1)} async-done(((bf16[8,176,384]{2,1,0:T(8,128)(2,1)}), bf16[8,176,384]{2,1,0:T(8,128)(2,1)S(1)}, u32[]{:S(2)}, u32[]{:S(2)}) %all-to-all-start.1) | async-done | bytes 1081376 | tf_op jit(solution)/shard_map/all_to_all | solution.py:37
  50.8 0.9 order.1
  51.8 1.0 copy-done.4
  52.8 7.2 %project.1 = bf16[32,17,8,128]{3,2,1,0:T(8,128)(2,1)} custom-call(s32[1]{0:T(128)} %bitcast.2.core_ref, bf16[4,256,1408]{2,1,0:T(8,128)(2,1)} %get-tuple-element.7.own_ref, bf16[4,256,1408]{2,1,0:T(8,128)(2,1)} %get-tuple-element.8.other_ref, bf16[1408,384]{1,0:T(8,128)(2,1)} %copy-done.4), custom_call_target="tpu_custom_call" | custom-call | tf_op jit(solution)/shard_map/project/pallas_call | solution.py:263
  60.0 39.6 %all_to_all.26.x_ref = bf16[32,17,8,128]{3,2,1,0:T(8,128)(2,1)S(1)} all-to-all(bf16[32,17,8,128]{3,2,1,0:T(8,128)(2,1)} %project.1), channel_id=1, replica_groups=mesh['zh'=4,'zl'=2,'x'=4,'c'=2,'pool'=8] {'zh','zl','x'}, dimensions={0} | all-to-all | bytes 2228224 | tf_op jit(solution)/shard_map/all_to_all | solution.py:278
  99.6 2.3 %attend.1 = bf16[32,6,8,128]{3,2,1,0:T(8,128)(2,1)S(1)} custom-call(bf16[32,17,8,128]{3,2,1,0:T(8,128)(2,1)S(1)} %all_to_all.26.x_ref), custom_call_target="tpu_custom_call" | custom-call | tf_op jit(solution)/shard_map/attend/pallas_call | solution.py:282
  102.6 4.4 %all-to-all-start.3 = ((bf16[32,6,8,128]{3,2,1,0:T(8,128)(2,1)}), bf16[32,6,8,128]{3,2,1,0:T(8,128)(2,1)S(1)}, u32[]{:S(2)}, u32[]{:S(2)}) async-start(bf16[32,6,8,128]{3,2,1,0:T(8,128)(2,1)} %copy-done.3), calls=%async_computation.3 | async-start | bytes 786432 | tf_op jit(solution)/shard_map/all_to_all | solution.py:289
  107.1 3.8 %collective-permute-start = (s32[4]{0:T(128)S(1)}, s32[4]{0:T(128)S(1)}, u32[]{:S(2)}, u32[]{:S(2)}) collective-permute-start(s32[4]{0:T(128)S(1)} %copy-done.6), channel_id=1, source_target_pairs={{0,8},{8,0},{1,9},{9,1},{2,10},{10,2},{3,11},{11,3},{4,12},{12,4},... | collective-permute-start | bytes 56 | tf_op jit(solution)/shard_map/ppermute | solution.py:230
  110.9 0.8 collective-permute-done
  111.8 8.2 %all-to-all-done.3.x_ref = bf16[32,6,8,128]{3,2,1,0:T(8,128)(2,1)S(1)} async-done(((bf16[32,6,8,128]{3,2,1,0:T(8,128)(2,1)}), bf16[32,6,8,128]{3,2,1,0:T(8,128)(2,1)S(1)}, u32[]{:S(2)}, u32[]{:S(2)}) %all-to-all-start.3) | async-done | bytes 393248 | tf_op jit(solution)/shard_map/all_to_all | solution.py:289
  120.0 0.9 pack.1
  120.8 0.9 copy-done.2
  121.7 10.4 %all-to-all-start.4 = ((bf16[16,24,8,128]{3,2,1,0:T(8,128)(2,1)}), bf16[16,24,8,128]{3,2,1,0:T(8,128)(2,1)}, u32[]{:S(2)}, u32[]{:S(2)}) async-start(bf16[16,24,8,128]{3,2,1,0:T(8,128)(2,1)} %copy-done.2), calls=%async_computation.4 | async-start | bytes 1572864 | tf_op jit(solution)/shard_map/all_to_all | solution.py:307
  134.8 18.7 %all-to-all-done.4.y_ref = bf16[16,24,8,128]{3,2,1,0:T(8,128)(2,1)} async-done(((bf16[16,24,8,128]{3,2,1,0:T(8,128)(2,1)}), bf16[16,24,8,128]{3,2,1,0:T(8,128)(2,1)}, u32[]{:S(2)}, u32[]{:S(2)}) %all-to-all-start.4) | async-done | bytes 786464 | tf_op jit(solution)/shard_map/all_to_all | solution.py:307
  153.5 2.2 %copy-done.1 = bf16[1536,1408]{1,0:T(8,128)(2,1)S(1)} copy-done((bf16[1536,1408]{1,0:T(8,128)(2,1)S(1)}, bf16[1536,1408]{1,0:T(8,128)(2,1)}, u32[]{:S(2)}) %copy-start.1) | copy-done | bytes 4325400
  155.8 4.2 %deliver.1 = (bf16[1,256,1408]{2,1,0:T(8,128)(2,1)}, bf16[1,11,256]{2,1,0:T(8,128)(2,1)}) custom-call(s32[2]{0:T(128)S(1)} %pad_add_fusion.pick_ref, bf16[4,256,1408]{2,1,0:T(8,128)(2,1)S(1)} %copy-done, bf16[16,24,8,128]{3,2,1,0:T(8,128)(2,1)} %all-to-all-done.4.y_ref, bf16[16,96,1408]{2,1,0:T(8,128)(2,1)S(1)} %bitcast.17), custom_call_target="tpu_custom_call" | custom-call | tf_op jit(solution)/shard_map/deliver/pallas_call | solution.py:313
  (30 shorter events, 4.1 us)
Async XLA Ops:
  7.2 31.8 %collective-permute-start.1 = (bf16[4,256,1408]{2,1,0:T(8,128)(2,1)}, bf16[4,256,1408]{2,1,0:T(8,128)(2,1)}, u32[]{:S(2)}, u32[]{:S(2)}) collective-permute-start(bf16[4,256,1408]{2,1,0:T(8,128)(2,1)} %frame_ref.1), channel_id=1, source_target_pairs={{0,8},{8,0},{1,9},{9,1},{2,10},{10,2},{3,11},{11,3},{4,12},{12,4},... | collective-permute-start | bytes 8650760 | tf_op jit(solution)/shard_map/ppermute | solution.py:215
  34.0 16.1 %all-to-all-start.1 = ((bf16[8,176,384]{2,1,0:T(8,128)(2,1)}), bf16[8,176,384]{2,1,0:T(8,128)(2,1)S(1)}, u32[]{:S(2)}, u32[]{:S(2)}) async-start(bf16[8,176,384]{2,1,0:T(8,128)(2,1)} %broadcast_in_dim.28), calls=%async_computation.1 | async-start | bytes 2162688 | tf_op jit(solution)/shard_map/all_to_all | solution.py:37
  38.9 114.6 %all-gather.3.cloned.1.call-start = ((), (), s32[]{:S(2)}) async-start(), calls=%async_computation.5 | async-start | bytes 4595712 | tf_op jit(solution)/shard_map/all_gather | solution.py:280
  50.2 0.7 copy-start.5
  51.8 1.0 copy-start.4
  60.0 47.1 %copy-start.6 = (s32[4]{0:T(128)S(1)}, s32[4]{0:T(128)}, u32[]{:S(2)}) copy-start(s32[4]{0:T(128)} %param.8) | copy-start | bytes 52
  99.6 32.6 %copy-start.7 = (s32[4]{0:T(128)S(1)}, s32[4]{0:T(128)}, u32[]{:S(2)}) copy-start(s32[4]{0:T(128)} %param.9) | copy-start | bytes 52
  99.6 54.0 %copy-start = (bf16[4,256,1408]{2,1,0:T(8,128)(2,1)S(1)}, bf16[4,256,1408]{2,1,0:T(8,128)(2,1)}, u32[]{:S(2)}) copy-start(bf16[4,256,1408]{2,1,0:T(8,128)(2,1)} %frame_ref.1) | copy-start | bytes 8650756
  101.9 0.7 copy-start.3
  102.6 17.3 %all-to-all-start.3 = ((bf16[32,6,8,128]{3,2,1,0:T(8,128)(2,1)}), bf16[32,6,8,128]{3,2,1,0:T(8,128)(2,1)S(1)}, u32[]{:S(2)}, u32[]{:S(2)}) async-start(bf16[32,6,8,128]{3,2,1,0:T(8,128)(2,1)} %copy-done.3), calls=%async_computation.3 | async-start | bytes 786432 | tf_op jit(solution)/shard_map/all_to_all | solution.py:289
  107.1 4.6 %collective-permute-start = (s32[4]{0:T(128)S(1)}, s32[4]{0:T(128)S(1)}, u32[]{:S(2)}, u32[]{:S(2)}) collective-permute-start(s32[4]{0:T(128)S(1)} %copy-done.6), channel_id=1, source_target_pairs={{0,8},{8,0},{1,9},{9,1},{2,10},{10,2},{3,11},{11,3},{4,12},{12,4},... | collective-permute-start | bytes 56 | tf_op jit(solution)/shard_map/ppermute | solution.py:230
  120.8 0.9 copy-start.2
  121.7 31.8 %all-to-all-start.4 = ((bf16[16,24,8,128]{3,2,1,0:T(8,128)(2,1)}), bf16[16,24,8,128]{3,2,1,0:T(8,128)(2,1)}, u32[]{:S(2)}, u32[]{:S(2)}) async-start(bf16[16,24,8,128]{3,2,1,0:T(8,128)(2,1)} %copy-done.2), calls=%async_computation.4 | async-start | bytes 1572864 | tf_op jit(solution)/shard_map/all_to_all | solution.py:307
  153.5 2.2 %copy-start.1 = (bf16[1536,1408]{1,0:T(8,128)(2,1)S(1)}, bf16[1536,1408]{1,0:T(8,128)(2,1)}, u32[]{:S(2)}) copy-start(bf16[1536,1408]{1,0:T(8,128)(2,1)} %all-gather.3.cloned.1.call-done) | copy-start | bytes 12976132
Sparse Core Ops, SparseCore 0:
  52.9 45.9 all-gather.2

commit v7 on v4

--- a/solution.py
+++ b/solution.py
@@ -9,8 +9,8 @@
 GROUP = 128
 MAIN = 64
 SLOT = 32
-ORDER, TRACK, PACK, DELIVER = 30, 40, 40, 30
-FACTOR = 1.0 / HEAD_DIM**0.5
+ORDER, TRACK, PACK, DELIVER = 30, 57, 40, 30
+FACTOR = 1.4426950408889634 / HEAD_DIM**0.5
 CHIP = ("zh", "zl", "x")
 FRAME = CHIP + ("c",)
 F32 = jnp.float32
@@ -56,18 +56,19 @@
     tokens = tokens_ref[...].reshape(frames, tokens_ref.shape[2])
     right = jnp.concatenate([own_ref[...], other_ref[...]], axis=1)
     both = jnp.dot(tokens, right, preferred_element_type=F32)
+    ones = jnp.where(lane == 127, 1.0, 0.0)
     for which in range(2):
         head = core if which == 0 else 1 - core
         out = both[:, which * 384 : which * 384 + 384]
-        query = jnp.where(lane < HEAD_DIM, out[:, :128], 0.0).astype(BF16)
+        query = jnp.where(lane < HEAD_DIM, out[:, :128] * FACTOR, 0.0).astype(BF16)
         key = out[:, 128:256].astype(BF16)
-        value = jnp.where(lane < HEAD_DIM, out[:, 256:], 0.0).astype(BF16)
+        value = jnp.where(lane < HEAD_DIM, out[:, 256:], ones).astype(BF16)
         scores = lax.dot_general(query, key, (((1,), (1,)), ((), ())), preferred_element_type=F32)
         top = jnp.max(scores, axis=-1, keepdims=True)
-        expo = jnp.exp((scores - top) * FACTOR)
-        total = jnp.sum(expo, axis=-1, keepdims=True)
-        mixed = jnp.dot(expo.astype(BF16), value, preferred_element_type=F32)
-        mixed = (mixed * (1.0 / total)).reshape(frames // 8, 8, 128)
+        expo = jnp.exp2(scores - top).astype(BF16)
+        mixed = jnp.dot(expo, value, preferred_element_type=F32)
+        mixed = jnp.where(lane < HEAD_DIM, mixed * (1.0 / mixed[:, 127:]), 0.0)
+        mixed = mixed.reshape(frames // 8, 8, 128)
         o_ref[:, pl.ds(head * 4 + step, 8, stride=8), :] = mixed
 
     @pl.when(step == pl.num_programs(0) - 1)
@@ -209,10 +210,15 @@
     sources = 2 * lax.axis_size("pool")
     swap = [(0, 1), (1, 0)]
 
-    share = lax.dynamic_slice_in_dim(frames_in, (position % 2) * 2, 2, 0)
-    share = share.reshape(2, chips, 8, width)
+    grid = frames_in.reshape(2, 2, chips, 8, width)
     share = jnp.concatenate(
-        [lax.dynamic_slice_in_dim(share, position // 2 + at, 1, 2) for at in (0, 4)], axis=2
+        [
+            lax.dynamic_slice(
+                grid, (position % 2, 0, 0, position // 2 + at, 0), (1, 2, chips, 1, width)
+            )[0]
+            for at in (0, 4)
+        ],
+        axis=2,
     )
     share = normalise(share).transpose(1, 2, 0, 3).reshape(2 * chips, 2, width)
     share = lax.all_to_all(share, FRAME, 0, 0, tiled=True).reshape(4 * chips, width)

time: 160 us -> 159 us (level)
  Pallas kernels: 12.6 us -> 14.7 us
    pallas_call x1, Pallas kernels: 6.25 us -> 8.37 us  [local(): pl.pallas_call(track_kernel, grid=(4,), in_specs=[pl.BlockSpec(memory_spa...]
    reshape x2 -> x0, local copies, waits for them, and re-layouts: 1.85 us -> none  [the longest x1 1.47 us: local(): share = share.reshape(2, chips, 8, width)]
    dynamic_slice x1, local copies, waits for them, and re-layouts: 0.75 us -> 2.55 us  [local(): lax.dynamic_slice(grid, (position % 2, 0, 0, position // 2 + at, 0), (1,...]
    unnamed x17 -> x20, local copies, waits for them, and re-layouts: 4.98 us -> 3.21 us
  transfers between devices with their start and end apart: 6 -> 6, of which waited for: 5 -> 5; matrix products, arithmetic and copies ran while one was open for 2% -> 2% of each run, Pallas kernels for 5% -> 7%
where the time goes in v7:
time: 159 us; the launch traced here: 158 us
  blocking collectives  58.2 us (37%)
  starting transfers between devices  30.8 us (19%)
  waiting for transfers between devices  29.2 us (18%)
  between operations  14.9 us (9%)
  Pallas kernels  14.7 us (9%)
  local copies, waits for them, and re-layouts  7.77 us (5%)
  other arithmetic  2.69 us (2%)
    all_to_all x1, blocking collectives, local(): lax.all_to_all(share, FRAME, 0, 0, tiled=True).reshape(4 * chips, width)  29.2 us
    all_to_all x2, blocking collectives, spread(): return lax.all_to_all(copies, axis, 0, 0, tiled=True)  27.2 us
    all_to_all x1, waiting for transfers between devices, local(): gathered = lax.all_to_all(packed, ('c', 'pool'), 0, 0, tiled=True)  19.2 us
    all_to_all x1, starting transfers between devices, local(): returned = lax.all_to_all(attended, CHIP, 0, 0, tiled=True)  10.1 us
    all_to_all x1, starting transfers between devices, local(): gathered = lax.all_to_all(packed, ('c', 'pool'), 0, 0, tiled=True)  9.81 us
    pallas_call x1, Pallas kernels, local(): pl.pallas_call(track_kernel, grid=(4,), in_specs=[pl.BlockSpec(memory_spa...  8.37 us
    ppermute x1, starting transfers between devices, local(): mine_other = lax.ppermute(mine, 'c', swap)  5.79 us
    all_to_all x1, waiting for transfers between devices, local(): returned = lax.all_to_all(attended, CHIP, 0, 0, tiled=True)  5.62 us
  transfers between devices with their start and end apart: 6, of which 5 were waited for; matrix products, arithmetic and copies ran while one was open for 2% of the time, Pallas kernels for 7%

profile of v7, /device:TPU:1, one launch (start us, length us, event | category | flops | bytes accessed | tf_op | source)
XLA Modules:
  0.0 158.2 jit_solution(6540379331444678473)
XLA Ops:
  7.2 2.5 %constant_dynamic-slice_fusion.2 = (bf16[1,2,32,1,1408]{4,3,2,1,0:T(2,128)(2,1)S(1)}, bf16[1,2,32,1,1408]{4,3,2,1,0:T(2,128)(2,1)S(1)}) fusion(bf16[2,2,32,8,1408]{4,3,2,1,0:T(8,128)(2,1)} %bitcast.26, s32[]{:T(128)S(6)} %select_n.44, s32[]{:T(128)S(6)} %select_n.46, s32[]{:T(128)S(6)} %select_n.47), kind=kLoop, calls=%fused_computation.20 | loop fusion | bytes 720908 | tf_op jit(solution)/shard_map/dynamic_slice | solution.py:216
  10.8 29.2 %all_to_all.25 = bf16[64,2,1408]{2,1,0:T(2,128)(2,1)S(1)} all-to-all(bf16[64,2,1408]{2,1,0:T(2,128)(2,1)S(1)} %bitcast.30), channel_id=1, replica_groups=mesh['zh'=4,'zl'=2,'x'=4,'c'=2,'pool'=8] {'zh','zl','x','c'}, dimensions={0} | all-to-all | bytes 720896 | tf_op jit(solution)/shard_map/all_to_all | solution.py:224
  40.0 0.9 all_gather_reshape.3
  41.6 1.9 %all_gather.13 = bf16[44,2,384]{2,1,0:T(2,128)(2,1)S(1)} all-gather(bf16[22,2,384]{2,1,0:T(2,128)(2,1)S(1)} %concatenate.15), channel_id=1, replica_groups=mesh['zh'=4,'zl'=2,'x'=4,'c'=2,'pool'=8] {'c'}, dimensions={0}, use_global_device_ids=true | all-gather | bytes 101376 | tf_op jit(solution)/shard_map/all_gather | solution.py:243
  43.6 10.7 %all_to_all.26 = bf16[4,44,384]{2,1,0:T(8,128)(2,1)S(1)} all-to-all(bf16[4,44,384]{2,1,0:T(8,128)(2,1)S(1)} %broadcast_in_dim.24), channel_id=1, replica_groups=mesh['zh'=4,'zl'=2,'x'=4,'c'=2,'pool'=8] {'zh'}, dimensions={0} | all-to-all | bytes 270336 | tf_op jit(solution)/shard_map/all_to_all | solution.py:34
  54.4 16.4 %all_to_all.27.source_ref = bf16[8,176,384]{2,1,0:T(8,128)(2,1)S(1)} all-to-all(bf16[8,176,384]{2,1,0:T(8,128)(2,1)S(1)} %broadcast_in_dim.26), channel_id=1, replica_groups=mesh['zh'=4,'zl'=2,'x'=4,'c'=2,'pool'=8] {'zl','x'}, dimensions={0} | all-to-all | bytes 2162688 | tf_op jit(solution)/shard_map/all_to_all | solution.py:34
  70.9 1.2 order.1
  72.1 5.8 %collective-permute-start.1 = (bf16[1408,384]{1,0:T(8,128)(2,1)S(1)}, bf16[1408,384]{1,0:T(8,128)(2,1)S(1)}, u32[]{:S(2)}, u32[]{:S(2)}) collective-permute-start(bf16[1408,384]{1,0:T(8,128)(2,1)S(1)} %get-tuple-element.4.own_ref), channel_id=1, source_target_pairs={{0,8},{8,0},{1,9},{9,1},{2,10},{10,2},{3,11},{11,3},{4,12},{12,4},... | collective-permute-start | bytes 3244040 | tf_op jit(solution)/shard_map/ppermute | solution.py:257
  77.9 2.3 %collective-permute-done.1.other_ref = bf16[1408,384]{1,0:T(8,128)(2,1)S(1)} collective-permute-done((bf16[1408,384]{1,0:T(8,128)(2,1)S(1)}, bf16[1408,384]{1,0:T(8,128)(2,1)S(1)}, u32[]{:S(2)}, u32[]{:S(2)}) %collective-permute-start.1) | collective-permute-done | bytes 1081376 | tf_op jit(solution)/shard_map/ppermute | solution.py:257
  80.2 1.1 all-gather.4.cloned.1.call-done.tokens_ref
  81.3 8.4 %track.1 = bf16[16,2,6,8,128]{4,3,2,1,0:T(8,128)(2,1)} custom-call(s32[1]{0:T(128)} %bitcast.2.core_ref, bf16[8,128,1408]{2,1,0:T(8,128)(2,1)} %all-gather.4.cloned.1.call-done.tokens_ref, bf16[1408,384]{1,0:T(8,128)(2,1)} %copy-done.3, bf16[1408,384]{1,0:T(8,128)(2,1)} %copy-done.4), custom_call_target="tpu_custom_call" | custom-call | tf_op jit(solution)/shard_map/track/pallas_call | solution.py:260
  89.7 10.1 %all-to-all-start.3 = ((bf16[32,6,8,128]{3,2,1,0:T(8,128)(2,1)}), bf16[32,6,8,128]{3,2,1,0:T(8,128)(2,1)S(1)}, u32[]{:S(2)}, u32[]{:S(2)}) async-start(bf16[32,6,8,128]{3,2,1,0:T(8,128)(2,1)} %bitcast.29), calls=%async_computation.3 | async-start | bytes 786432 | tf_op jit(solution)/shard_map/all_to_all | solution.py:276
  99.9 4.9 %collective-permute-start = (s32[4]{0:T(128)S(1)}, s32[4]{0:T(128)S(1)}, u32[]{:S(2)}, u32[]{:S(2)}) collective-permute-start(s32[4]{0:T(128)S(1)} %copy-done.7), channel_id=1, source_target_pairs={{0,8},{8,0},{1,9},{9,1},{2,10},{10,2},{3,11},{11,3},{4,12},{12,4},... | collective-permute-start | bytes 56 | tf_op jit(solution)/shard_map/ppermute | solution.py:226
  104.8 0.8 collective-permute-done
  105.7 5.6 %all-to-all-done.3 = bf16[32,6,8,128]{3,2,1,0:T(8,128)(2,1)S(1)} async-done(((bf16[32,6,8,128]{3,2,1,0:T(8,128)(2,1)}), bf16[32,6,8,128]{3,2,1,0:T(8,128)(2,1)S(1)}, u32[]{:S(2)}, u32[]{:S(2)}) %all-to-all-start.3) | async-done | bytes 393248 | tf_op jit(solution)/shard_map/all_to_all | solution.py:276
  111.3 1.1 pack.1
  112.4 0.9 copy-done.2
  113.3 9.8 %all-to-all-start.4 = ((bf16[16,24,8,128]{3,2,1,0:T(8,128)(2,1)}), bf16[16,24,8,128]{3,2,1,0:T(8,128)(2,1)}, u32[]{:S(2)}, u32[]{:S(2)}) async-start(bf16[16,24,8,128]{3,2,1,0:T(8,128)(2,1)} %copy-done.2), calls=%async_computation.4 | async-start | bytes 1572864 | tf_op jit(solution)/shard_map/all_to_all | solution.py:294
  123.1 0.6 select_reduce_fusion
  123.7 0.6 reduce_or.9
  125.0 0.7 pad_add_fusion.pick_ref
  125.7 19.2 %all-to-all-done.4.y_ref = bf16[16,24,8,128]{3,2,1,0:T(8,128)(2,1)} async-done(((bf16[16,24,8,128]{3,2,1,0:T(8,128)(2,1)}), bf16[16,24,8,128]{3,2,1,0:T(8,128)(2,1)}, u32[]{:S(2)}, u32[]{:S(2)}) %all-to-all-start.4) | async-done | bytes 786464 | tf_op jit(solution)/shard_map/all_to_all | solution.py:294
  145.0 2.2 %copy-done.1 = bf16[1536,1408]{1,0:T(8,128)(2,1)S(1)} copy-done((bf16[1536,1408]{1,0:T(8,128)(2,1)S(1)}, bf16[1536,1408]{1,0:T(8,128)(2,1)}, u32[]{:S(2)}) %copy-start.1) | copy-done | bytes 4325400
  147.2 4.1 %deliver.1 = (bf16[1,256,1408]{2,1,0:T(8,128)(2,1)}, bf16[1,11,256]{2,1,0:T(8,128)(2,1)}) custom-call(s32[2]{0:T(128)S(1)} %pad_add_fusion.pick_ref, bf16[4,256,1408]{2,1,0:T(8,128)(2,1)S(1)} %copy-done, bf16[16,24,8,128]{3,2,1,0:T(8,128)(2,1)} %all-to-all-done.4.y_ref, bf16[16,96,1408]{2,1,0:T(8,128)(2,1)S(1)} %bitcast.27), custom_call_target="tpu_custom_call" | custom-call | tf_op jit(solution)/shard_map/deliver/pallas_call | solution.py:300
  (41 shorter events, 2.0 us)
Async XLA Ops:
  7.2 74.2 %all-gather.4.cloned.1.call-start = ((), (), s32[]{:S(2)}) async-start(), calls=%async_computation.5 | async-start | bytes 3244032 | tf_op jit(solution)/shard_map/all_gather | solution.py:225
  9.8 31.1 %copy-start.5 = (bf16[22,3,176]{2,0,1:T(8,128)(2,1)S(1)}, bf16[22,3,176]{2,0,1:T(8,128)(2,1)}, u32[]{:S(2)}) copy-start(bf16[22,3,176]{2,0,1:T(8,128)(2,1)} %param.6) | copy-start | bytes 69700
  9.8 31.2 %copy-start.6 = (bf16[176,22]{0,1:T(8,128)(2,1)S(1)}, bf16[176,22]{0,1:T(8,128)(2,1)}, u32[]{:S(2)}) copy-start(bf16[176,22]{0,1:T(8,128)(2,1)} %param.7) | copy-start | bytes 23236
  40.9 104.1 %all-gather.6.cloned.1.call-start = ((), (), s32[]{:S(2)}) async-start(), calls=%async_computation.6 | async-start | bytes 4595712 | tf_op jit(solution)/shard_map/all_gather | solution.py:258
  72.0 9.3 %copy-start.3 = (bf16[1408,384]{1,0:T(8,128)(2,1)}, bf16[1408,384]{1,0:T(8,128)(2,1)S(1)}, u32[]{:S(2)}) copy-start(bf16[1408,384]{1,0:T(8,128)(2,1)S(1)} %get-tuple-element.4.own_ref) | copy-start | bytes 3244036
  72.1 8.1 %collective-permute-start.1 = (bf16[1408,384]{1,0:T(8,128)(2,1)S(1)}, bf16[1408,384]{1,0:T(8,128)(2,1)S(1)}, u32[]{:S(2)}, u32[]{:S(2)}) collective-permute-start(bf16[1408,384]{1,0:T(8,128)(2,1)S(1)} %get-tuple-element.4.own_ref), channel_id=1, source_target_pairs={{0,8},{8,0},{1,9},{9,1},{2,10},{10,2},{3,11},{11,3},{4,12},{12,4},... | collective-permute-start | bytes 3244040 | tf_op jit(solution)/shard_map/ppermute | solution.py:257
  80.2 1.2 copy-start.4
  81.3 18.5 %copy-start.7 = (s32[4]{0:T(128)S(1)}, s32[4]{0:T(128)}, u32[]{:S(2)}) copy-start(s32[4]{0:T(128)} %param.8) | copy-start | bytes 52
  89.7 33.4 %copy-start.8 = (s32[4]{0:T(128)S(1)}, s32[4]{0:T(128)}, u32[]{:S(2)}) copy-start(s32[4]{0:T(128)} %param.9) | copy-start | bytes 52
  89.7 55.3 %copy-start = (bf16[4,256,1408]{2,1,0:T(8,128)(2,1)S(1)}, bf16[4,256,1408]{2,1,0:T(8,128)(2,1)}, u32[]{:S(2)}) copy-start(bf16[4,256,1408]{2,1,0:T(8,128)(2,1)} %frame_ref.1) | copy-start | bytes 8650756
  89.7 21.6 %all-to-all-start.3 = ((bf16[32,6,8,128]{3,2,1,0:T(8,128)(2,1)}), bf16[32,6,8,128]{3,2,1,0:T(8,128)(2,1)S(1)}, u32[]{:S(2)}, u32[]{:S(2)}) async-start(bf16[32,6,8,128]{3,2,1,0:T(8,128)(2,1)} %bitcast.29), calls=%async_computation.3 | async-start | bytes 786432 | tf_op jit(solution)/shard_map/all_to_all | solution.py:276
  99.9 5.7 %collective-permute-start = (s32[4]{0:T(128)S(1)}, s32[4]{0:T(128)S(1)}, u32[]{:S(2)}, u32[]{:S(2)}) collective-permute-start(s32[4]{0:T(128)S(1)} %copy-done.7), channel_id=1, source_target_pairs={{0,8},{8,0},{1,9},{9,1},{2,10},{10,2},{3,11},{11,3},{4,12},{12,4},... | collective-permute-start | bytes 56 | tf_op jit(solution)/shard_map/ppermute | solution.py:226
  112.4 0.9 copy-start.2
  113.3 31.7 %all-to-all-start.4 = ((bf16[16,24,8,128]{3,2,1,0:T(8,128)(2,1)}), bf16[16,24,8,128]{3,2,1,0:T(8,128)(2,1)}, u32[]{:S(2)}, u32[]{:S(2)}) async-start(bf16[16,24,8,128]{3,2,1,0:T(8,128)(2,1)} %copy-done.2), calls=%async_computation.4 | async-start | bytes 1572864 | tf_op jit(solution)/shard_map/all_to_all | solution.py:294
  145.0 2.2 %copy-start.1 = (bf16[1536,1408]{1,0:T(8,128)(2,1)S(1)}, bf16[1536,1408]{1,0:T(8,128)(2,1)}, u32[]{:S(2)}) copy-start(bf16[1536,1408]{1,0:T(8,128)(2,1)} %all-gather.6.cloned.1.call-done) | copy-start | bytes 12976132
Sparse Core Ops, SparseCore 0:
  41.0 40.2 all-gather.3
  83.4 49.4 all-gather.5

commit v8 on v7

--- a/solution.py
+++ b/solution.py
@@ -9,7 +9,7 @@
 GROUP = 128
 MAIN = 64
 SLOT = 32
-ORDER, TRACK, PACK, DELIVER = 30, 57, 40, 30
+ORDER, TRACK, PACK, DELIVER = 30, 50, 40, 30
 FACTOR = 1.4426950408889634 / HEAD_DIM**0.5
 CHIP = ("zh", "zl", "x")
 FRAME = CHIP + ("c",)
@@ -51,9 +51,9 @@
 def track_kernel(core_ref, tokens_ref, own_ref, other_ref, out_ref, o_ref):
     step = pl.program_id(0)
     core = core_ref[0]
-    frames = 2 * tokens_ref.shape[1]
+    frames = 2 * tokens_ref.shape[2]
     lane = lanes_of((frames, 128))
-    tokens = tokens_ref[...].reshape(frames, tokens_ref.shape[2])
+    tokens = tokens_ref[...].reshape(frames, tokens_ref.shape[3])
     right = jnp.concatenate([own_ref[...], other_ref[...]], axis=1)
     both = jnp.dot(tokens, right, preferred_element_type=F32)
     ones = jnp.where(lane == 127, 1.0, 0.0)
@@ -77,8 +77,8 @@
         lane_o = lanes_of((pairs, 8, 128))
 
         def piece_of(side, owner, late, odd):
-            start = (side * 4 + owner * 2 + odd) * 8
-            return o_ref[late * pairs : (late + 1) * pairs, start : start + 8, :]
+            start = (side * 4 + late * 2 + odd) * 8
+            return o_ref[owner * pairs : (owner + 1) * pairs, start : start + 8, :]
 
         for side in range(2):
             for owner in range(2):
@@ -207,22 +207,16 @@
     core = lax.axis_index("c")
     position = lax.axis_index("pool")
     chips = lax.axis_size("zh") * lax.axis_size("zl") * lax.axis_size("x")
-    sources = 2 * lax.axis_size("pool")
+    pool = lax.axis_size("pool")
+    sources = 2 * pool
     swap = [(0, 1), (1, 0)]
 
-    grid = frames_in.reshape(2, 2, chips, 8, width)
-    share = jnp.concatenate(
-        [
-            lax.dynamic_slice(
-                grid, (position % 2, 0, 0, position // 2 + at, 0), (1, 2, chips, 1, width)
-            )[0]
-            for at in (0, 4)
-        ],
-        axis=2,
-    )
-    share = normalise(share).transpose(1, 2, 0, 3).reshape(2 * chips, 2, width)
-    share = lax.all_to_all(share, FRAME, 0, 0, tiled=True).reshape(4 * chips, width)
-    tracks = lax.all_gather(share, "pool", axis=0, tiled=False)
+    share = frames_in.reshape(fr_count, chips, 8, width)
+    share = lax.dynamic_index_in_dim(share, position, 2, keepdims=False)
+    share = normalise(share).transpose(1, 0, 2)
+    share = lax.all_to_all(share, CHIP, 0, 0, tiled=True).reshape(chips * fr_count, width)
+    tracks = lax.all_gather(share, ("c", "pool"), axis=0, tiled=False)
+    tracks = tracks.reshape(2, pool, chips * fr_count, width)
     owners_other = lax.ppermute(owners, "c", swap)
 
     parts = qkv_weight.reshape(rows_here, 3, 2, HEAD_DIM)
@@ -259,16 +253,20 @@
 
     attended = pl.pallas_call(
         track_kernel,
-        grid=(4,),
-        in_specs=[
-            pl.BlockSpec(memory_space=pltpu.SMEM),
-            pl.BlockSpec((2, 4 * chips, width), lambda p: (p, 0, 0)),
-            pl.BlockSpec(mine.shape, lambda p: (0, 0)),
-            pl.BlockSpec(mine.shape, lambda p: (0, 0)),
-        ],
-        out_specs=pl.BlockSpec((chips // 2, 2, 6, 8, 128), lambda p: (0, 0, 0, 0, 0)),
+        grid_spec=pltpu.PrefetchScalarGridSpec(
+            num_scalar_prefetch=1,
+            grid=(4,),
+            in_specs=[
+                pl.BlockSpec(
+                    (2, 1, chips * fr_count, width), lambda p, core: (0, 4 * core[0] + p, 0, 0)
+                ),
+                pl.BlockSpec(mine.shape, lambda p, core: (0, 0)),
+                pl.BlockSpec(mine.shape, lambda p, core: (0, 0)),
+            ],
+            out_specs=pl.BlockSpec((chips // 2, 2, 6, 8, 128), lambda p, core: (0, 0, 0, 0, 0)),
+            scratch_shapes=[pltpu.VMEM((chips, 64, 128), F32)],
+        ),
         out_shape=jax.ShapeDtypeStruct((chips // 2, 2, 6, 8, 128), BF16),
-        scratch_shapes=[pltpu.VMEM((chips, 64, 128), F32)],
         compiler_params=params(TRACK),
         name="track",
     )(core.reshape(1), tracks, mine, mine_other)

time: 159 us -> 159 us (level)
  waiting for transfers between devices: 29.2 us -> 37.6 us
  starting transfers between devices: 30.8 us -> 25.1 us
  local copies, waits for them, and re-layouts: 7.77 us -> 5.01 us
  other arithmetic: 2.69 us -> 5.41 us
  blocking collectives: 58.2 us -> 56.5 us
    all_to_all x1, waiting for transfers between devices: 5.62 us -> 10.7 us  [local(): returned = lax.all_to_all(attended, CHIP, 0, 0, tiled=True)]
    all_gather x1, waiting for transfers between devices: 1.14 us -> 5.14 us  [local(): tracks = lax.all_gather(share, ('c', 'pool'), axis=0, tiled=False)]
    all_to_all x1, starting transfers between devices: 9.81 us -> 6.39 us  [local(): gathered = lax.all_to_all(packed, ('c', 'pool'), 0, 0, tiled=True)]
    all_to_all x1, waiting for transfers between devices: 19.2 us -> 16 us  [local(): gathered = lax.all_to_all(packed, ('c', 'pool'), 0, 0, tiled=True)]
    reduce_sum x1, other arithmetic: 0.13 us -> 2.96 us  [normalise(): mean = jnp.mean(xf, axis=-1, keepdims=True)]
    all_gather x1, waiting for transfers between devices: 0.01 us -> 2.67 us  [local(): out_rows = lax.all_gather(back_rows, ('c', 'pool'), axis=0, tiled=False)]
    dynamic_slice x1 -> x0, local copies, waits for them, and re-layouts: 2.55 us -> none  [local(): lax.dynamic_slice(grid, (position % 2, 0, 0, position // 2 + at, 0), (1,...]
    ppermute x1, starting transfers between devices: 4.94 us -> 2.46 us  [local(): owners_other = lax.ppermute(owners, 'c', swap)]
  transfers between devices with their start and end apart: 6 -> 6, of which waited for: 5 -> 6; matrix products, arithmetic and copies ran while one was open for 2% -> 2% of each run, Pallas kernels for 7% -> 6%
where the time goes in v8:
time: 159 us
  blocking collectives  56.5 us (36%)
  waiting for transfers between devices  37.6 us (24%)
  starting transfers between devices  25.1 us (16%)
  between operations  14.9 us (9%)
  Pallas kernels  14.1 us (9%)
  other arithmetic  5.41 us (3%)
  local copies, waits for them, and re-layouts  5.01 us (3%)
    all_to_all x1, blocking collectives, local(): lax.all_to_all(share, CHIP, 0, 0, tiled=True)  26.9 us
    all_to_all x2, blocking collectives, spread(): return lax.all_to_all(copies, axis, 0, 0, tiled=True)  26 us
    all_to_all x1, waiting for transfers between devices, local(): gathered = lax.all_to_all(packed, ('c', 'pool'), 0, 0, tiled=True)  16 us
    all_to_all x1, waiting for transfers between devices, local(): returned = lax.all_to_all(attended, CHIP, 0, 0, tiled=True)  10.7 us
    all_to_all x1, starting transfers between devices, local(): returned = lax.all_to_all(attended, CHIP, 0, 0, tiled=True)  10.2 us
    pallas_call x1, Pallas kernels, local(): pl.pallas_call(track_kernel, grid_spec=pltpu.PrefetchScalarGridSpec(num_s...  7.7 us
    all_to_all x1, starting transfers between devices, local(): gathered = lax.all_to_all(packed, ('c', 'pool'), 0, 0, tiled=True)  6.39 us
    ppermute x1, starting transfers between devices, local(): mine_other = lax.ppermute(mine, 'c', swap)  6.01 us
  transfers between devices with their start and end apart: 6, of which 6 were waited for; matrix products, arithmetic and copies ran while one was open for 2% of the time, Pallas kernels for 6%

profile of v8, /device:TPU:1, one launch (start us, length us, event | category | flops | bytes accessed | tf_op | source)
XLA Modules:
  0.0 158.7 jit_solution(3324029326810063491)
XLA Ops:
  7.2 3.0 %fusion.1 = (f32[4,32]{1,0:T(4,128)S(1)}, f32[4,32,1,1408]{3,2,1,0:T(1,128)S(1)}) fusion(bf16[4,32,8,1408]{3,2,1,0:T(8,128)(2,1)} %bitcast.30, s32[]{:T(128)S(6)} %select_n.23), kind=kLoop, calls=%fused_computation.16 | loop fusion | flops 360320 | bytes 1081860 | tf_op jit(solution)/shard_map/reduce_sum | solution.py:194
  10.8 26.9 %all_to_all.25 = bf16[32,4,1408]{2,1,0:T(4,128)(2,1)S(1)} all-to-all(bf16[32,4,1408]{2,1,0:T(4,128)(2,1)S(1)} %copy.11), channel_id=1, replica_groups=mesh['zh'=4,'zl'=2,'x'=4,'c'=2,'pool'=8] {'zh','zl','x'}, dimensions={0} | all-to-all | bytes 720896 | tf_op jit(solution)/shard_map/all_to_all | solution.py:217
  37.7 0.8 all_gather_reshape.3
  39.3 3.7 %all_gather.13 = bf16[44,2,384]{2,1,0:T(2,128)(2,1)S(1)} all-gather(bf16[22,2,384]{2,1,0:T(2,128)(2,1)S(1)} %concatenate.11), channel_id=1, replica_groups=mesh['zh'=4,'zl'=2,'x'=4,'c'=2,'pool'=8] {'c'}, dimensions={0}, use_global_device_ids=true | all-gather | bytes 101376 | tf_op jit(solution)/shard_map/all_gather | solution.py:237
  43.1 9.8 %all_to_all.26 = bf16[4,44,384]{2,1,0:T(8,128)(2,1)S(1)} all-to-all(bf16[4,44,384]{2,1,0:T(8,128)(2,1)S(1)} %broadcast_in_dim.24), channel_id=1, replica_groups=mesh['zh'=4,'zl'=2,'x'=4,'c'=2,'pool'=8] {'zh'}, dimensions={0} | all-to-all | bytes 270336 | tf_op jit(solution)/shard_map/all_to_all | solution.py:34
  53.0 16.2 %all_to_all.27.source_ref = bf16[8,176,384]{2,1,0:T(8,128)(2,1)S(1)} all-to-all(bf16[8,176,384]{2,1,0:T(8,128)(2,1)S(1)} %broadcast_in_dim.26), channel_id=1, replica_groups=mesh['zh'=4,'zl'=2,'x'=4,'c'=2,'pool'=8] {'zl','x'}, dimensions={0} | all-to-all | bytes 2162688 | tf_op jit(solution)/shard_map/all_to_all | solution.py:34
  69.2 1.2 order.1
  70.4 6.0 %collective-permute-start.1 = (bf16[1408,384]{1,0:T(8,128)(2,1)S(1)}, bf16[1408,384]{1,0:T(8,128)(2,1)S(1)}, u32[]{:S(2)}, u32[]{:S(2)}) collective-permute-start(bf16[1408,384]{1,0:T(8,128)(2,1)S(1)} %get-tuple-element.4.own_ref), channel_id=1, source_target_pairs={{0,8},{8,0},{1,9},{9,1},{2,10},{10,2},{3,11},{11,3},{4,12},{12,4},... | collective-permute-start | bytes 3244040 | tf_op jit(solution)/shard_map/ppermute | solution.py:251
  76.4 2.3 %collective-permute-done.1.other_ref = bf16[1408,384]{1,0:T(8,128)(2,1)S(1)} collective-permute-done((bf16[1408,384]{1,0:T(8,128)(2,1)S(1)}, bf16[1408,384]{1,0:T(8,128)(2,1)S(1)}, u32[]{:S(2)}, u32[]{:S(2)}) %collective-permute-start.1) | collective-permute-done | bytes 1081376 | tf_op jit(solution)/shard_map/ppermute | solution.py:251
  78.7 5.1 %all-gather.4.cloned.1.call-done = bf16[16,128,1408]{2,1,0:T(8,128)(2,1)} async-done(((bf16[1,128,1408]{2,1,0:T(8,128)(2,1)}), bf16[16,128,1408]{2,1,0:T(8,128)(2,1)}) %all-gather.4.cloned.1.call-update) | async-done | bytes 5767184 | tf_op jit(solution)/shard_map/all_gather | solution.py:218
  83.8 7.7 %track.1 = bf16[16,2,6,8,128]{4,3,2,1,0:T(8,128)(2,1)} custom-call(s32[1]{0:T(128)} %bitcast.2.core_ref, bf16[2,8,128,1408]{3,2,1,0:T(8,128)(2,1)} %bitcast.33, bf16[1408,384]{1,0:T(8,128)(2,1)S(1)} %get-tuple-element.4.own_ref, bf16[1408,384]{1,0:T(8,128)(2,1)S(1)} %collective-permute-done.1.other_ref), custom_call_target="tpu_custom_call" | custom-call | tf_op jit(solution)/shard_map/track/pallas_call | solution.py:254
  91.5 10.2 %all-to-all-start.3 = ((bf16[32,6,8,128]{3,2,1,0:T(8,128)(2,1)}), bf16[32,6,8,128]{3,2,1,0:T(8,128)(2,1)S(1)}, u32[]{:S(2)}, u32[]{:S(2)}) async-start(bf16[32,6,8,128]{3,2,1,0:T(8,128)(2,1)} %bitcast.11), calls=%async_computation.3 | async-start | bytes 786432 | tf_op jit(solution)/shard_map/all_to_all | solution.py:274
  101.7 2.5 %collective-permute-start = (s32[4]{0:T(128)S(1)}, s32[4]{0:T(128)S(1)}, u32[]{:S(2)}, u32[]{:S(2)}) collective-permute-start(s32[4]{0:T(128)S(1)} %copy-done.5), channel_id=1, source_target_pairs={{0,8},{8,0},{1,9},{9,1},{2,10},{10,2},{3,11},{11,3},{4,12},{12,4},... | collective-permute-start | bytes 56 | tf_op jit(solution)/shard_map/ppermute | solution.py:220
  104.2 0.8 collective-permute-done
  105.1 10.7 %all-to-all-done.3 = bf16[32,6,8,128]{3,2,1,0:T(8,128)(2,1)S(1)} async-done(((bf16[32,6,8,128]{3,2,1,0:T(8,128)(2,1)}), bf16[32,6,8,128]{3,2,1,0:T(8,128)(2,1)S(1)}, u32[]{:S(2)}, u32[]{:S(2)}) %all-to-all-start.3) | async-done | bytes 393248 | tf_op jit(solution)/shard_map/all_to_all | solution.py:274
  115.8 1.1 pack.1
  116.9 0.9 copy-done.2
  117.8 6.4 %all-to-all-start.4 = ((bf16[16,24,8,128]{3,2,1,0:T(8,128)(2,1)}), bf16[16,24,8,128]{3,2,1,0:T(8,128)(2,1)}, u32[]{:S(2)}, u32[]{:S(2)}) async-start(bf16[16,24,8,128]{3,2,1,0:T(8,128)(2,1)} %copy-done.2), calls=%async_computation.4 | async-start | bytes 1572864 | tf_op jit(solution)/shard_map/all_to_all | solution.py:292
  124.2 0.6 select_reduce_fusion
  126.1 0.7 pad_add_fusion.pick_ref
  126.8 2.7 %all-gather.6.cloned.1.call-done = bf16[1536,1408]{1,0:T(8,128)(2,1)} async-done(((bf16[96,1408]{1,0:T(8,128)(2,1)}), bf16[1536,1408]{1,0:T(8,128)(2,1)}) %all-gather.6.cloned.1.call-update) | async-done | bytes 4325392 | tf_op jit(solution)/shard_map/all_gather | solution.py:252
  129.5 16.0 %all-to-all-done.4.y_ref = bf16[16,24,8,128]{3,2,1,0:T(8,128)(2,1)} async-done(((bf16[16,24,8,128]{3,2,1,0:T(8,128)(2,1)}), bf16[16,24,8,128]{3,2,1,0:T(8,128)(2,1)}, u32[]{:S(2)}, u32[]{:S(2)}) %all-to-all-start.4) | async-done | bytes 786464 | tf_op jit(solution)/shard_map/all_to_all | solution.py:292
  145.5 2.2 %copy-done.1 = bf16[1536,1408]{1,0:T(8,128)(2,1)S(1)} copy-done((bf16[1536,1408]{1,0:T(8,128)(2,1)S(1)}, bf16[1536,1408]{1,0:T(8,128)(2,1)}, u32[]{:S(2)}) %copy-start.1) | copy-done | bytes 4325400
  147.7 4.1 %deliver.1 = (bf16[1,256,1408]{2,1,0:T(8,128)(2,1)}, bf16[1,11,256]{2,1,0:T(8,128)(2,1)}) custom-call(s32[2]{0:T(128)S(1)} %pad_add_fusion.pick_ref, bf16[4,256,1408]{2,1,0:T(8,128)(2,1)S(1)} %copy-done, bf16[16,24,8,128]{3,2,1,0:T(8,128)(2,1)} %all-to-all-done.4.y_ref, bf16[16,96,1408]{2,1,0:T(8,128)(2,1)S(1)} %bitcast.31), custom_call_target="tpu_custom_call" | custom-call | tf_op jit(solution)/shard_map/deliver/pallas_call | solution.py:298
  (35 shorter events, 2.3 us)
Async XLA Ops:
  7.2 76.7 %all-gather.4.cloned.1.call-start = ((), (), s32[]{:S(2)}) async-start(), calls=%async_computation.5 | async-start | bytes 6127616 | tf_op jit(solution)/shard_map/all_gather | solution.py:218
  7.2 31.4 %copy-start.3 = (bf16[22,3,176]{2,0,1:T(8,128)(2,1)S(1)}, bf16[22,3,176]{2,0,1:T(8,128)(2,1)}, u32[]{:S(2)}) copy-start(bf16[22,3,176]{2,0,1:T(8,128)(2,1)} %param.6) | copy-start | bytes 69700
  7.2 31.5 %copy-start.4 = (bf16[176,22]{0,1:T(8,128)(2,1)S(1)}, bf16[176,22]{0,1:T(8,128)(2,1)}, u32[]{:S(2)}) copy-start(bf16[176,22]{0,1:T(8,128)(2,1)} %param.7) | copy-start | bytes 23236
  38.5 91.0 %all-gather.6.cloned.1.call-start = ((), (), s32[]{:S(2)}) async-start(), calls=%async_computation.6 | async-start | bytes 4595712 | tf_op jit(solution)/shard_map/all_gather | solution.py:252
  70.4 8.3 %collective-permute-start.1 = (bf16[1408,384]{1,0:T(8,128)(2,1)S(1)}, bf16[1408,384]{1,0:T(8,128)(2,1)S(1)}, u32[]{:S(2)}, u32[]{:S(2)}) collective-permute-start(bf16[1408,384]{1,0:T(8,128)(2,1)S(1)} %get-tuple-element.4.own_ref), channel_id=1, source_target_pairs={{0,8},{8,0},{1,9},{9,1},{2,10},{10,2},{3,11},{11,3},{4,12},{12,4},... | collective-permute-start | bytes 3244040 | tf_op jit(solution)/shard_map/ppermute | solution.py:251
  83.8 17.9 %copy-start.5 = (s32[4]{0:T(128)S(1)}, s32[4]{0:T(128)}, u32[]{:S(2)}) copy-start(s32[4]{0:T(128)} %param.8) | copy-start | bytes 52
  91.5 32.6 %copy-start.6 = (s32[4]{0:T(128)S(1)}, s32[4]{0:T(128)}, u32[]{:S(2)}) copy-start(s32[4]{0:T(128)} %param.9) | copy-start | bytes 52
  91.5 53.9 %copy-start = (bf16[4,256,1408]{2,1,0:T(8,128)(2,1)S(1)}, bf16[4,256,1408]{2,1,0:T(8,128)(2,1)}, u32[]{:S(2)}) copy-start(bf16[4,256,1408]{2,1,0:T(8,128)(2,1)} %frame_ref.1) | copy-start | bytes 8650756
  91.5 24.3 %all-to-all-start.3 = ((bf16[32,6,8,128]{3,2,1,0:T(8,128)(2,1)}), bf16[32,6,8,128]{3,2,1,0:T(8,128)(2,1)S(1)}, u32[]{:S(2)}, u32[]{:S(2)}) async-start(bf16[32,6,8,128]{3,2,1,0:T(8,128)(2,1)} %bitcast.11), calls=%async_computation.3 | async-start | bytes 786432 | tf_op jit(solution)/shard_map/all_to_all | solution.py:274
  101.7 3.3 %collective-permute-start = (s32[4]{0:T(128)S(1)}, s32[4]{0:T(128)S(1)}, u32[]{:S(2)}, u32[]{:S(2)}) collective-permute-start(s32[4]{0:T(128)S(1)} %copy-done.5), channel_id=1, source_target_pairs={{0,8},{8,0},{1,9},{9,1},{2,10},{10,2},{3,11},{11,3},{4,12},{12,4},... | collective-permute-start | bytes 56 | tf_op jit(solution)/shard_map/ppermute | solution.py:220
  116.9 0.9 copy-start.2
  117.8 27.7 %all-to-all-start.4 = ((bf16[16,24,8,128]{3,2,1,0:T(8,128)(2,1)}), bf16[16,24,8,128]{3,2,1,0:T(8,128)(2,1)}, u32[]{:S(2)}, u32[]{:S(2)}) async-start(bf16[16,24,8,128]{3,2,1,0:T(8,128)(2,1)} %copy-done.2), calls=%async_computation.4 | async-start | bytes 1572864 | tf_op jit(solution)/shard_map/all_to_all | solution.py:292
  145.5 2.2 %copy-start.1 = (bf16[1536,1408]{1,0:T(8,128)(2,1)S(1)}, bf16[1536,1408]{1,0:T(8,128)(2,1)}, u32[]{:S(2)}) copy-start(bf16[1536,1408]{1,0:T(8,128)(2,1)} %all-gather.6.cloned.1.call-done) | copy-start | bytes 12976132
Sparse Core Ops, SparseCore 0:
  38.6 45.1 all-gather.3
  85.9 43.5 all-gather.5

commit v9 on v7

--- a/solution.py
+++ b/solution.py
@@ -9,7 +9,7 @@
 GROUP = 128
 MAIN = 64
 SLOT = 32
-ORDER, TRACK, PACK, DELIVER = 30, 57, 40, 30
+ORDER, TRACK, PACK, DELIVER = 30, 50, 40, 30
 FACTOR = 1.4426950408889634 / HEAD_DIM**0.5
 CHIP = ("zh", "zl", "x")
 FRAME = CHIP + ("c",)
@@ -182,7 +182,7 @@
             part = total[:, at : at + GROUP]
             top = jnp.max(jnp.abs(part), axis=-1, keepdims=True)
             scale = (top + 1e-06).astype(BF16).astype(F32)
-            coded = jnp.where(valid, part / scale, 0.0).astype(BF16)
+            coded = jnp.where(valid, part * (1.0 / scale), 0.0).astype(BF16)
             out_ref[0, :, start + at : start + at + GROUP] = coded
             scales = jnp.where(lane_p == (start + at) // GROUP, scale, scales)
     scales = jnp.where(valid, scales, 0.0).T

time: 159 us -> 159 us (level)
    unnamed x20 -> x16, local copies, waits for them, and re-layouts: 3.21 us -> 3.21 us
  transfers between devices with their start and end apart: 6 -> 6, of which waited for: 5 -> 5; matrix products, arithmetic and copies ran while one was open for 2% -> 2% of each run, Pallas kernels for 7% -> 6%
where the time goes in v9:
time: 159 us; the launch traced here: 158 us
  blocking collectives  58.2 us (37%)
  starting transfers between devices  30.8 us (19%)
  waiting for transfers between devices  29.6 us (19%)
  between operations  14.9 us (9%)
  Pallas kernels  14 us (9%)
  local copies, waits for them, and re-layouts  7.77 us (5%)
  other arithmetic  2.69 us (2%)
    all_to_all x1, blocking collectives, local(): lax.all_to_all(share, FRAME, 0, 0, tiled=True).reshape(4 * chips, width)  29.2 us
    all_to_all x2, blocking collectives, spread(): return lax.all_to_all(copies, axis, 0, 0, tiled=True)  27.2 us
    all_to_all x1, waiting for transfers between devices, local(): gathered = lax.all_to_all(packed, ('c', 'pool'), 0, 0, tiled=True)  19.7 us
    all_to_all x1, starting transfers between devices, local(): returned = lax.all_to_all(attended, CHIP, 0, 0, tiled=True)  10.1 us
    all_to_all x1, starting transfers between devices, local(): gathered = lax.all_to_all(packed, ('c', 'pool'), 0, 0, tiled=True)  9.81 us
    pallas_call x1, Pallas kernels, local(): pl.pallas_call(track_kernel, grid=(4,), in_specs=[pl.BlockSpec(memory_spa...  7.69 us
    ppermute x1, starting transfers between devices, local(): mine_other = lax.ppermute(mine, 'c', swap)  5.79 us
    all_to_all x1, waiting for transfers between devices, local(): returned = lax.all_to_all(attended, CHIP, 0, 0, tiled=True)  5.62 us
  transfers between devices with their start and end apart: 6, of which 5 were waited for; matrix products, arithmetic and copies ran while one was open for 2% of the time, Pallas kernels for 6%

profile of v9, /device:TPU:1, one launch (start us, length us, event | category | flops | bytes accessed | tf_op | source)
XLA Modules:
  0.0 158.0 jit_solution(17663449864382580979)
XLA Ops:
  7.2 2.5 %constant_dynamic-slice_fusion.2 = (bf16[1,2,32,1,1408]{4,3,2,1,0:T(2,128)(2,1)S(1)}, bf16[1,2,32,1,1408]{4,3,2,1,0:T(2,128)(2,1)S(1)}) fusion(bf16[2,2,32,8,1408]{4,3,2,1,0:T(8,128)(2,1)} %bitcast.26, s32[]{:T(128)S(6)} %select_n.44, s32[]{:T(128)S(6)} %select_n.46, s32[]{:T(128)S(6)} %select_n.47), kind=kLoop, calls=%fused_computation.20 | loop fusion | bytes 720908 | tf_op jit(solution)/shard_map/dynamic_slice | solution.py:216
  10.8 29.2 %all_to_all.25 = bf16[64,2,1408]{2,1,0:T(2,128)(2,1)S(1)} all-to-all(bf16[64,2,1408]{2,1,0:T(2,128)(2,1)S(1)} %bitcast.29), channel_id=1, replica_groups=mesh['zh'=4,'zl'=2,'x'=4,'c'=2,'pool'=8] {'zh','zl','x','c'}, dimensions={0} | all-to-all | bytes 720896 | tf_op jit(solution)/shard_map/all_to_all | solution.py:224
  40.0 0.9 all_gather_reshape.3
  41.6 1.9 %all_gather.13 = bf16[44,2,384]{2,1,0:T(2,128)(2,1)S(1)} all-gather(bf16[22,2,384]{2,1,0:T(2,128)(2,1)S(1)} %concatenate.15), channel_id=1, replica_groups=mesh['zh'=4,'zl'=2,'x'=4,'c'=2,'pool'=8] {'c'}, dimensions={0}, use_global_device_ids=true | all-gather | bytes 101376 | tf_op jit(solution)/shard_map/all_gather | solution.py:243
  43.6 10.7 %all_to_all.26 = bf16[4,44,384]{2,1,0:T(8,128)(2,1)S(1)} all-to-all(bf16[4,44,384]{2,1,0:T(8,128)(2,1)S(1)} %broadcast_in_dim.24), channel_id=1, replica_groups=mesh['zh'=4,'zl'=2,'x'=4,'c'=2,'pool'=8] {'zh'}, dimensions={0} | all-to-all | bytes 270336 | tf_op jit(solution)/shard_map/all_to_all | solution.py:34
  54.4 16.4 %all_to_all.27.source_ref = bf16[8,176,384]{2,1,0:T(8,128)(2,1)S(1)} all-to-all(bf16[8,176,384]{2,1,0:T(8,128)(2,1)S(1)} %broadcast_in_dim.26), channel_id=1, replica_groups=mesh['zh'=4,'zl'=2,'x'=4,'c'=2,'pool'=8] {'zl','x'}, dimensions={0} | all-to-all | bytes 2162688 | tf_op jit(solution)/shard_map/all_to_all | solution.py:34
  70.9 1.2 order.1
  72.1 5.8 %collective-permute-start.1 = (bf16[1408,384]{1,0:T(8,128)(2,1)S(1)}, bf16[1408,384]{1,0:T(8,128)(2,1)S(1)}, u32[]{:S(2)}, u32[]{:S(2)}) collective-permute-start(bf16[1408,384]{1,0:T(8,128)(2,1)S(1)} %get-tuple-element.4.own_ref), channel_id=1, source_target_pairs={{0,8},{8,0},{1,9},{9,1},{2,10},{10,2},{3,11},{11,3},{4,12},{12,4},... | collective-permute-start | bytes 3244040 | tf_op jit(solution)/shard_map/ppermute | solution.py:257
  77.9 2.3 %collective-permute-done.1.other_ref = bf16[1408,384]{1,0:T(8,128)(2,1)S(1)} collective-permute-done((bf16[1408,384]{1,0:T(8,128)(2,1)S(1)}, bf16[1408,384]{1,0:T(8,128)(2,1)S(1)}, u32[]{:S(2)}, u32[]{:S(2)}) %collective-permute-start.1) | collective-permute-done | bytes 1081376 | tf_op jit(solution)/shard_map/ppermute | solution.py:257
  80.2 1.1 all-gather.4.cloned.1.call-done.tokens_ref
  81.3 7.7 %track.1 = bf16[16,2,6,8,128]{4,3,2,1,0:T(8,128)(2,1)} custom-call(s32[1]{0:T(128)} %bitcast.2.core_ref, bf16[8,128,1408]{2,1,0:T(8,128)(2,1)} %all-gather.4.cloned.1.call-done.tokens_ref, bf16[1408,384]{1,0:T(8,128)(2,1)S(1)} %get-tuple-element.4.own_ref, bf16[1408,384]{1,0:T(8,128)(2,1)S(1)} %collective-permute-done.1.other_ref), custom_call_target="tpu_custom_call" | custom-call | tf_op jit(solution)/shard_map/track/pallas_call | solution.py:260
  89.0 10.1 %all-to-all-start.3 = ((bf16[32,6,8,128]{3,2,1,0:T(8,128)(2,1)}), bf16[32,6,8,128]{3,2,1,0:T(8,128)(2,1)S(1)}, u32[]{:S(2)}, u32[]{:S(2)}) async-start(bf16[32,6,8,128]{3,2,1,0:T(8,128)(2,1)} %bitcast.11), calls=%async_computation.3 | async-start | bytes 786432 | tf_op jit(solution)/shard_map/all_to_all | solution.py:276
  99.2 4.9 %collective-permute-start = (s32[4]{0:T(128)S(1)}, s32[4]{0:T(128)S(1)}, u32[]{:S(2)}, u32[]{:S(2)}) collective-permute-start(s32[4]{0:T(128)S(1)} %copy-done.5), channel_id=1, source_target_pairs={{0,8},{8,0},{1,9},{9,1},{2,10},{10,2},{3,11},{11,3},{4,12},{12,4},... | collective-permute-start | bytes 56 | tf_op jit(solution)/shard_map/ppermute | solution.py:226
  104.1 0.8 collective-permute-done
  105.0 5.6 %all-to-all-done.3 = bf16[32,6,8,128]{3,2,1,0:T(8,128)(2,1)S(1)} async-done(((bf16[32,6,8,128]{3,2,1,0:T(8,128)(2,1)}), bf16[32,6,8,128]{3,2,1,0:T(8,128)(2,1)S(1)}, u32[]{:S(2)}, u32[]{:S(2)}) %all-to-all-start.3) | async-done | bytes 393248 | tf_op jit(solution)/shard_map/all_to_all | solution.py:276
  110.6 1.1 pack.1
  111.7 0.9 copy-done.2
  112.6 9.8 %all-to-all-start.4 = ((bf16[16,24,8,128]{3,2,1,0:T(8,128)(2,1)}), bf16[16,24,8,128]{3,2,1,0:T(8,128)(2,1)}, u32[]{:S(2)}, u32[]{:S(2)}) async-start(bf16[16,24,8,128]{3,2,1,0:T(8,128)(2,1)} %copy-done.2), calls=%async_computation.4 | async-start | bytes 1572864 | tf_op jit(solution)/shard_map/all_to_all | solution.py:294
  122.4 0.6 select_reduce_fusion
  123.1 0.6 reduce_or.9
  124.3 0.7 pad_add_fusion.pick_ref
  125.1 19.7 %all-to-all-done.4.y_ref = bf16[16,24,8,128]{3,2,1,0:T(8,128)(2,1)} async-done(((bf16[16,24,8,128]{3,2,1,0:T(8,128)(2,1)}), bf16[16,24,8,128]{3,2,1,0:T(8,128)(2,1)}, u32[]{:S(2)}, u32[]{:S(2)}) %all-to-all-start.4) | async-done | bytes 786464 | tf_op jit(solution)/shard_map/all_to_all | solution.py:294
  144.8 2.2 %copy-done.1 = bf16[1536,1408]{1,0:T(8,128)(2,1)S(1)} copy-done((bf16[1536,1408]{1,0:T(8,128)(2,1)S(1)}, bf16[1536,1408]{1,0:T(8,128)(2,1)}, u32[]{:S(2)}) %copy-start.1) | copy-done | bytes 4325400
  147.0 4.1 %deliver.1 = (bf16[1,256,1408]{2,1,0:T(8,128)(2,1)}, bf16[1,11,256]{2,1,0:T(8,128)(2,1)}) custom-call(s32[2]{0:T(128)S(1)} %pad_add_fusion.pick_ref, bf16[4,256,1408]{2,1,0:T(8,128)(2,1)S(1)} %copy-done, bf16[16,24,8,128]{3,2,1,0:T(8,128)(2,1)} %all-to-all-done.4.y_ref, bf16[16,96,1408]{2,1,0:T(8,128)(2,1)S(1)} %bitcast.27), custom_call_target="tpu_custom_call" | custom-call | tf_op jit(solution)/shard_map/deliver/pallas_call | solution.py:300
  (37 shorter events, 2.0 us)
Async XLA Ops:
  7.2 74.2 %all-gather.4.cloned.1.call-start = ((), (), s32[]{:S(2)}) async-start(), calls=%async_computation.5 | async-start | bytes 3244032 | tf_op jit(solution)/shard_map/all_gather | solution.py:225
  9.8 31.1 %copy-start.3 = (bf16[22,3,176]{2,0,1:T(8,128)(2,1)S(1)}, bf16[22,3,176]{2,0,1:T(8,128)(2,1)}, u32[]{:S(2)}) copy-start(bf16[22,3,176]{2,0,1:T(8,128)(2,1)} %param.6) | copy-start | bytes 69700
  9.8 31.2 %copy-start.4 = (bf16[176,22]{0,1:T(8,128)(2,1)S(1)}, bf16[176,22]{0,1:T(8,128)(2,1)}, u32[]{:S(2)}) copy-start(bf16[176,22]{0,1:T(8,128)(2,1)} %param.7) | copy-start | bytes 23236
  40.9 103.9 %all-gather.6.cloned.1.call-start = ((), (), s32[]{:S(2)}) async-start(), calls=%async_computation.6 | async-start | bytes 4595712 | tf_op jit(solution)/shard_map/all_gather | solution.py:258
  72.1 8.1 %collective-permute-start.1 = (bf16[1408,384]{1,0:T(8,128)(2,1)S(1)}, bf16[1408,384]{1,0:T(8,128)(2,1)S(1)}, u32[]{:S(2)}, u32[]{:S(2)}) collective-permute-start(bf16[1408,384]{1,0:T(8,128)(2,1)S(1)} %get-tuple-element.4.own_ref), channel_id=1, source_target_pairs={{0,8},{8,0},{1,9},{9,1},{2,10},{10,2},{3,11},{11,3},{4,12},{12,4},... | collective-permute-start | bytes 3244040 | tf_op jit(solution)/shard_map/ppermute | solution.py:257
  81.3 17.8 %copy-start.5 = (s32[4]{0:T(128)S(1)}, s32[4]{0:T(128)}, u32[]{:S(2)}) copy-start(s32[4]{0:T(128)} %param.8) | copy-start | bytes 52
  89.0 33.4 %copy-start.6 = (s32[4]{0:T(128)S(1)}, s32[4]{0:T(128)}, u32[]{:S(2)}) copy-start(s32[4]{0:T(128)} %param.9) | copy-start | bytes 52
  89.0 55.7 %copy-start = (bf16[4,256,1408]{2,1,0:T(8,128)(2,1)S(1)}, bf16[4,256,1408]{2,1,0:T(8,128)(2,1)}, u32[]{:S(2)}) copy-start(bf16[4,256,1408]{2,1,0:T(8,128)(2,1)} %frame_ref.1) | copy-start | bytes 8650756
  89.0 21.6 %all-to-all-start.3 = ((bf16[32,6,8,128]{3,2,1,0:T(8,128)(2,1)}), bf16[32,6,8,128]{3,2,1,0:T(8,128)(2,1)S(1)}, u32[]{:S(2)}, u32[]{:S(2)}) async-start(bf16[32,6,8,128]{3,2,1,0:T(8,128)(2,1)} %bitcast.11), calls=%async_computation.3 | async-start | bytes 786432 | tf_op jit(solution)/shard_map/all_to_all | solution.py:276
  99.2 5.7 %collective-permute-start = (s32[4]{0:T(128)S(1)}, s32[4]{0:T(128)S(1)}, u32[]{:S(2)}, u32[]{:S(2)}) collective-permute-start(s32[4]{0:T(128)S(1)} %copy-done.5), channel_id=1, source_target_pairs={{0,8},{8,0},{1,9},{9,1},{2,10},{10,2},{3,11},{11,3},{4,12},{12,4},... | collective-permute-start | bytes 56 | tf_op jit(solution)/shard_map/ppermute | solution.py:226
  111.7 0.9 copy-start.2
  112.6 32.1 %all-to-all-start.4 = ((bf16[16,24,8,128]{3,2,1,0:T(8,128)(2,1)}), bf16[16,24,8,128]{3,2,1,0:T(8,128)(2,1)}, u32[]{:S(2)}, u32[]{:S(2)}) async-start(bf16[16,24,8,128]{3,2,1,0:T(8,128)(2,1)} %copy-done.2), calls=%async_computation.4 | async-start | bytes 1572864 | tf_op jit(solution)/shard_map/all_to_all | solution.py:294
  144.7 2.2 %copy-start.1 = (bf16[1536,1408]{1,0:T(8,128)(2,1)S(1)}, bf16[1536,1408]{1,0:T(8,128)(2,1)}, u32[]{:S(2)}) copy-start(bf16[1536,1408]{1,0:T(8,128)(2,1)} %all-gather.6.cloned.1.call-done) | copy-start | bytes 12976132
Sparse Core Ops, SparseCore 0:
  41.0 40.2 all-gather.3
  83.4 49.9 all-gather.5

commit v10 on v9

--- a/solution.py
+++ b/solution.py
@@ -9,7 +9,7 @@
 GROUP = 128
 MAIN = 64
 SLOT = 32
-ORDER, TRACK, PACK, DELIVER = 30, 50, 40, 30
+SHARE, ORDER, TRACK, PACK, DELIVER = 58, 30, 50, 40, 30
 FACTOR = 1.4426950408889634 / HEAD_DIM**0.5
 CHIP = ("zh", "zl", "x")
 FRAME = CHIP + ("c",)
@@ -32,6 +32,22 @@
     count = lax.axis_size(axis)
     copies = jnp.broadcast_to(value[None], (count,) + value.shape)
     return lax.all_to_all(copies, axis, 0, 0, tiled=True)
+
+
+def share_kernel(at_ref, frames_ref, out_ref):
+    count, patches, width = frames_ref.shape
+    rows = out_ref.shape[0] * out_ref.shape[1]
+    row = lax.broadcasted_iota(jnp.int32, (rows, count * patches), 0)
+    column = lax.broadcasted_iota(jnp.int32, (rows, count * patches), 1)
+    wanted = (row & 1) * patches + (row >> 2) * 8 + ((row >> 1) & 1) * 4 + (at_ref[0] >> 1)
+    pick = jnp.where(column == wanted, 1.0, 0.0).astype(BF16)
+    tokens = frames_ref[...].reshape(count * patches, width)
+    xf = jnp.dot(pick, tokens, preferred_element_type=F32)
+    mean = jnp.mean(xf, axis=-1, keepdims=True)
+    centred = xf - mean
+    var = jnp.mean(centred * centred, axis=-1, keepdims=True)
+    normed = centred * lax.rsqrt(var + 1e-06)
+    out_ref[...] = normed.reshape(out_ref.shape).astype(BF16)
 
 
 def order_kernel(source_ref, right_ref, back_ref, order_ref):
@@ -189,14 +205,6 @@
     scale_ref[0] = scales[: width // GROUP].astype(BF16)
 
 
-def normalise(frames):
-    xf = frames.astype(F32)
-    mean = jnp.mean(xf, axis=-1, keepdims=True)
-    centred = xf - mean
-    var = jnp.mean(centred * centred, axis=-1, keepdims=True)
-    return (centred * lax.rsqrt(var + 1e-06)).astype(BF16)
-
-
 def params(mebibytes):
     return pltpu.CompilerParams(vmem_limit_bytes=mebibytes * 1024 * 1024)
 
@@ -210,17 +218,18 @@
     sources = 2 * lax.axis_size("pool")
     swap = [(0, 1), (1, 0)]
 
-    grid = frames_in.reshape(2, 2, chips, 8, width)
-    share = jnp.concatenate(
-        [
-            lax.dynamic_slice(
-                grid, (position % 2, 0, 0, position // 2 + at, 0), (1, 2, chips, 1, width)
-            )[0]
-            for at in (0, 4)
-        ],
-        axis=2,
-    )
-    share = normalise(share).transpose(1, 2, 0, 3).reshape(2 * chips, 2, width)
+    share = pl.pallas_call(
+        share_kernel,
+        grid_spec=pltpu.PrefetchScalarGridSpec(
+            num_scalar_prefetch=1,
+            grid=(1,),
+            in_specs=[pl.BlockSpec((2, patch_count, width), lambda g, at: (at[0] & 1, 0, 0))],
+            out_specs=pl.BlockSpec((2 * chips, 2, width), lambda g, at: (0, 0, 0)),
+        ),
+        out_shape=jax.ShapeDtypeStruct((2 * chips, 2, width), BF16),
+        compiler_params=params(SHARE),
+        name="share",
+    )(position.reshape(1), frames_in)
     share = lax.all_to_all(share, FRAME, 0, 0, tiled=True).reshape(4 * chips, width)
     tracks = lax.all_gather(share, "pool", axis=0, tiled=False)
     owners_other = lax.ppermute(owners, "c", swap)

time: 159 us -> 159 us (level)
  Pallas kernels: 14 us -> 17 us
  local copies, waits for them, and re-layouts: 7.77 us -> 4.89 us
    pallas_call x0 -> x1, Pallas kernels: none -> 3.01 us  [local(): pl.pallas_call(share_kernel, grid_spec=pltpu.PrefetchScalarGridSpec(num_s...]
    dynamic_slice x1 -> x0, local copies, waits for them, and re-layouts: 2.55 us -> none  [local(): lax.dynamic_slice(grid, (position % 2, 0, 0, position // 2 + at, 0), (1,...]
    unnamed x16 -> x15, local copies, waits for them, and re-layouts: 3.21 us -> 3.16 us
where the time goes in v10:
time: 159 us; the launch traced here: 158 us
  blocking collectives  58.5 us (37%)
  starting transfers between devices  30.9 us (19%)
  waiting for transfers between devices  29.6 us (19%)
  Pallas kernels  17 us (11%)
  between operations  14.8 us (9%)
  local copies, waits for them, and re-layouts  4.89 us (3%)
  other arithmetic  2.07 us (1%)
    all_to_all x1, blocking collectives, local(): lax.all_to_all(share, FRAME, 0, 0, tiled=True).reshape(4 * chips, width)  29.5 us
    all_to_all x2, blocking collectives, spread(): return lax.all_to_all(copies, axis, 0, 0, tiled=True)  27.2 us
    all_to_all x1, waiting for transfers between devices, local(): gathered = lax.all_to_all(packed, ('c', 'pool'), 0, 0, tiled=True)  19.7 us
    all_to_all x1, starting transfers between devices, local(): returned = lax.all_to_all(attended, CHIP, 0, 0, tiled=True)  10.2 us
    all_to_all x1, starting transfers between devices, local(): gathered = lax.all_to_all(packed, ('c', 'pool'), 0, 0, tiled=True)  9.94 us
    pallas_call x1, Pallas kernels, local(): pl.pallas_call(track_kernel, grid=(4,), in_specs=[pl.BlockSpec(memory_spa...  7.69 us
    ppermute x1, starting transfers between devices, local(): mine_other = lax.ppermute(mine, 'c', swap)  5.79 us
    all_to_all x1, waiting for transfers between devices, local(): returned = lax.all_to_all(attended, CHIP, 0, 0, tiled=True)  5.62 us
  transfers between devices with their start and end apart: 6, of which 5 were waited for; matrix products, arithmetic and copies ran while one was open for 2% of the time, Pallas kernels for 6%

profile of v10, /device:TPU:1, one launch (start us, length us, event | category | flops | bytes accessed | tf_op | source)
XLA Modules:
  0.0 157.8 jit_solution(15899449208334689275)
XLA Ops:
  7.2 3.0 %share.1 = bf16[64,2,1408]{2,1,0:T(2,128)(2,1)} custom-call(s32[1]{0:T(128)} %bitcast.3.at_ref, bf16[4,256,1408]{2,1,0:T(8,128)(2,1)} %frame_ref.1), custom_call_target="tpu_custom_call" | custom-call | tf_op jit(solution)/shard_map/share/pallas_call | solution.py:221
  10.2 29.5 %all_to_all.25 = bf16[64,2,1408]{2,1,0:T(2,128)(2,1)S(1)} all-to-all(bf16[64,2,1408]{2,1,0:T(2,128)(2,1)} %share.1), channel_id=1, replica_groups=mesh['zh'=4,'zl'=2,'x'=4,'c'=2,'pool'=8] {'zh','zl','x','c'}, dimensions={0} | all-to-all | bytes 720896 | tf_op jit(solution)/shard_map/all_to_all | solution.py:233
  39.7 0.9 all_gather_reshape.3
  41.4 1.9 %all_gather.13 = bf16[44,2,384]{2,1,0:T(2,128)(2,1)S(1)} all-gather(bf16[22,2,384]{2,1,0:T(2,128)(2,1)S(1)} %concatenate.11), channel_id=1, replica_groups=mesh['zh'=4,'zl'=2,'x'=4,'c'=2,'pool'=8] {'c'}, dimensions={0}, use_global_device_ids=true | all-gather | bytes 101376 | tf_op jit(solution)/shard_map/all_gather | solution.py:252
  43.3 10.7 %all_to_all.26 = bf16[4,44,384]{2,1,0:T(8,128)(2,1)S(1)} all-to-all(bf16[4,44,384]{2,1,0:T(8,128)(2,1)S(1)} %broadcast_in_dim.22), channel_id=1, replica_groups=mesh['zh'=4,'zl'=2,'x'=4,'c'=2,'pool'=8] {'zh'}, dimensions={0} | all-to-all | bytes 270336 | tf_op jit(solution)/shard_map/all_to_all | solution.py:34
  54.2 16.4 %all_to_all.27.source_ref = bf16[8,176,384]{2,1,0:T(8,128)(2,1)S(1)} all-to-all(bf16[8,176,384]{2,1,0:T(8,128)(2,1)S(1)} %broadcast_in_dim.24), channel_id=1, replica_groups=mesh['zh'=4,'zl'=2,'x'=4,'c'=2,'pool'=8] {'zl','x'}, dimensions={0} | all-to-all | bytes 2162688 | tf_op jit(solution)/shard_map/all_to_all | solution.py:34
  70.6 1.1 order.1
  71.8 5.8 %collective-permute-start.1 = (bf16[1408,384]{1,0:T(8,128)(2,1)S(1)}, bf16[1408,384]{1,0:T(8,128)(2,1)S(1)}, u32[]{:S(2)}, u32[]{:S(2)}) collective-permute-start(bf16[1408,384]{1,0:T(8,128)(2,1)S(1)} %get-tuple-element.4.own_ref), channel_id=1, source_target_pairs={{0,8},{8,0},{1,9},{9,1},{2,10},{10,2},{3,11},{11,3},{4,12},{12,4},... | collective-permute-start | bytes 3244040 | tf_op jit(solution)/shard_map/ppermute | solution.py:266
  77.6 2.3 %collective-permute-done.1.other_ref = bf16[1408,384]{1,0:T(8,128)(2,1)S(1)} collective-permute-done((bf16[1408,384]{1,0:T(8,128)(2,1)S(1)}, bf16[1408,384]{1,0:T(8,128)(2,1)S(1)}, u32[]{:S(2)}, u32[]{:S(2)}) %collective-permute-start.1) | collective-permute-done | bytes 1081376 | tf_op jit(solution)/shard_map/ppermute | solution.py:266
  79.9 1.1 all-gather.4.cloned.1.call-done.tokens_ref
  81.1 7.7 %track.1 = bf16[16,2,6,8,128]{4,3,2,1,0:T(8,128)(2,1)} custom-call(s32[1]{0:T(128)} %bitcast.2.core_ref, bf16[8,128,1408]{2,1,0:T(8,128)(2,1)} %all-gather.4.cloned.1.call-done.tokens_ref, bf16[1408,384]{1,0:T(8,128)(2,1)S(1)} %get-tuple-element.4.own_ref, bf16[1408,384]{1,0:T(8,128)(2,1)S(1)} %collective-permute-done.1.other_ref), custom_call_target="tpu_custom_call" | custom-call | tf_op jit(solution)/shard_map/track/pallas_call | solution.py:269
  88.8 10.2 %all-to-all-start.3 = ((bf16[32,6,8,128]{3,2,1,0:T(8,128)(2,1)}), bf16[32,6,8,128]{3,2,1,0:T(8,128)(2,1)S(1)}, u32[]{:S(2)}, u32[]{:S(2)}) async-start(bf16[32,6,8,128]{3,2,1,0:T(8,128)(2,1)} %bitcast.9), calls=%async_computation.3 | async-start | bytes 786432 | tf_op jit(solution)/shard_map/all_to_all | solution.py:285
  98.9 4.9 %collective-permute-start = (s32[4]{0:T(128)S(1)}, s32[4]{0:T(128)S(1)}, u32[]{:S(2)}, u32[]{:S(2)}) collective-permute-start(s32[4]{0:T(128)S(1)} %copy-done.5), channel_id=1, source_target_pairs={{0,8},{8,0},{1,9},{9,1},{2,10},{10,2},{3,11},{11,3},{4,12},{12,4},... | collective-permute-start | bytes 56 | tf_op jit(solution)/shard_map/ppermute | solution.py:235
  103.9 0.8 collective-permute-done
  104.7 5.6 %all-to-all-done.3 = bf16[32,6,8,128]{3,2,1,0:T(8,128)(2,1)S(1)} async-done(((bf16[32,6,8,128]{3,2,1,0:T(8,128)(2,1)}), bf16[32,6,8,128]{3,2,1,0:T(8,128)(2,1)S(1)}, u32[]{:S(2)}, u32[]{:S(2)}) %all-to-all-start.3) | async-done | bytes 393248 | tf_op jit(solution)/shard_map/all_to_all | solution.py:285
  110.4 1.1 pack.1
  111.5 0.9 copy-done.2
  112.4 9.9 %all-to-all-start.4 = ((bf16[16,24,8,128]{3,2,1,0:T(8,128)(2,1)}), bf16[16,24,8,128]{3,2,1,0:T(8,128)(2,1)}, u32[]{:S(2)}, u32[]{:S(2)}) async-start(bf16[16,24,8,128]{3,2,1,0:T(8,128)(2,1)} %copy-done.2), calls=%async_computation.4 | async-start | bytes 1572864 | tf_op jit(solution)/shard_map/all_to_all | solution.py:303
  122.3 0.6 select_reduce_fusion
  122.9 0.6 reduce_or.9
  124.2 0.7 pad_add_fusion.pick_ref
  125.0 19.7 %all-to-all-done.4.y_ref = bf16[16,24,8,128]{3,2,1,0:T(8,128)(2,1)} async-done(((bf16[16,24,8,128]{3,2,1,0:T(8,128)(2,1)}), bf16[16,24,8,128]{3,2,1,0:T(8,128)(2,1)}, u32[]{:S(2)}, u32[]{:S(2)}) %all-to-all-start.4) | async-done | bytes 786464 | tf_op jit(solution)/shard_map/all_to_all | solution.py:303
  144.6 2.2 %copy-done.1 = bf16[1536,1408]{1,0:T(8,128)(2,1)S(1)} copy-done((bf16[1536,1408]{1,0:T(8,128)(2,1)S(1)}, bf16[1536,1408]{1,0:T(8,128)(2,1)}, u32[]{:S(2)}) %copy-start.1) | copy-done | bytes 4325400
  146.9 4.1 %deliver.1 = (bf16[1,256,1408]{2,1,0:T(8,128)(2,1)}, bf16[1,11,256]{2,1,0:T(8,128)(2,1)}) custom-call(s32[2]{0:T(128)S(1)} %pad_add_fusion.pick_ref, bf16[4,256,1408]{2,1,0:T(8,128)(2,1)S(1)} %copy-done, bf16[16,24,8,128]{3,2,1,0:T(8,128)(2,1)} %all-to-all-done.4.y_ref, bf16[16,96,1408]{2,1,0:T(8,128)(2,1)S(1)} %bitcast.19), custom_call_target="tpu_custom_call" | custom-call | tf_op jit(solution)/shard_map/deliver/pallas_call | solution.py:309
  (30 shorter events, 1.1 us)
Async XLA Ops:
  7.2 73.9 %all-gather.4.cloned.1.call-start = ((), (), s32[]{:S(2)}) async-start(), calls=%async_computation.5 | async-start | bytes 3244032 | tf_op jit(solution)/shard_map/all_gather | solution.py:234
  10.2 30.4 %copy-start.3 = (bf16[22,3,176]{2,0,1:T(8,128)(2,1)S(1)}, bf16[22,3,176]{2,0,1:T(8,128)(2,1)}, u32[]{:S(2)}) copy-start(bf16[22,3,176]{2,0,1:T(8,128)(2,1)} %param.6) | copy-start | bytes 69700
  10.2 30.6 %copy-start.4 = (bf16[176,22]{0,1:T(8,128)(2,1)S(1)}, bf16[176,22]{0,1:T(8,128)(2,1)}, u32[]{:S(2)}) copy-start(bf16[176,22]{0,1:T(8,128)(2,1)} %param.7) | copy-start | bytes 23236
  40.6 104.0 %all-gather.6.cloned.1.call-start = ((), (), s32[]{:S(2)}) async-start(), calls=%async_computation.6 | async-start | bytes 4595712 | tf_op jit(solution)/shard_map/all_gather | solution.py:267
  71.8 8.1 %collective-permute-start.1 = (bf16[1408,384]{1,0:T(8,128)(2,1)S(1)}, bf16[1408,384]{1,0:T(8,128)(2,1)S(1)}, u32[]{:S(2)}, u32[]{:S(2)}) collective-permute-start(bf16[1408,384]{1,0:T(8,128)(2,1)S(1)} %get-tuple-element.4.own_ref), channel_id=1, source_target_pairs={{0,8},{8,0},{1,9},{9,1},{2,10},{10,2},{3,11},{11,3},{4,12},{12,4},... | collective-permute-start | bytes 3244040 | tf_op jit(solution)/shard_map/ppermute | solution.py:266
  81.1 17.9 %copy-start.5 = (s32[4]{0:T(128)S(1)}, s32[4]{0:T(128)}, u32[]{:S(2)}) copy-start(s32[4]{0:T(128)} %param.8) | copy-start | bytes 52
  88.7 55.9 %copy-start = (bf16[4,256,1408]{2,1,0:T(8,128)(2,1)S(1)}, bf16[4,256,1408]{2,1,0:T(8,128)(2,1)}, u32[]{:S(2)}) copy-start(bf16[4,256,1408]{2,1,0:T(8,128)(2,1)} %frame_ref.1) | copy-start | bytes 8650756
  88.8 21.6 %all-to-all-start.3 = ((bf16[32,6,8,128]{3,2,1,0:T(8,128)(2,1)}), bf16[32,6,8,128]{3,2,1,0:T(8,128)(2,1)S(1)}, u32[]{:S(2)}, u32[]{:S(2)}) async-start(bf16[32,6,8,128]{3,2,1,0:T(8,128)(2,1)} %bitcast.9), calls=%async_computation.3 | async-start | bytes 786432 | tf_op jit(solution)/shard_map/all_to_all | solution.py:285
  98.9 5.7 %collective-permute-start = (s32[4]{0:T(128)S(1)}, s32[4]{0:T(128)S(1)}, u32[]{:S(2)}, u32[]{:S(2)}) collective-permute-start(s32[4]{0:T(128)S(1)} %copy-done.5), channel_id=1, source_target_pairs={{0,8},{8,0},{1,9},{9,1},{2,10},{10,2},{3,11},{11,3},{4,12},{12,4},... | collective-permute-start | bytes 56 | tf_op jit(solution)/shard_map/ppermute | solution.py:235
  111.4 0.9 copy-start.2
  112.4 9.9 %copy-start.6 = (s32[4]{0:T(128)S(1)}, s32[4]{0:T(128)}, u32[]{:S(2)}) copy-start(s32[4]{0:T(128)} %param.9) | copy-start | bytes 52
  112.4 32.3 %all-to-all-start.4 = ((bf16[16,24,8,128]{3,2,1,0:T(8,128)(2,1)}), bf16[16,24,8,128]{3,2,1,0:T(8,128)(2,1)}, u32[]{:S(2)}, u32[]{:S(2)}) async-start(bf16[16,24,8,128]{3,2,1,0:T(8,128)(2,1)} %copy-done.2), calls=%async_computation.4 | async-start | bytes 1572864 | tf_op jit(solution)/shard_map/all_to_all | solution.py:303
  144.6 2.2 %copy-start.1 = (bf16[1536,1408]{1,0:T(8,128)(2,1)S(1)}, bf16[1536,1408]{1,0:T(8,128)(2,1)}, u32[]{:S(2)}) copy-start(bf16[1536,1408]{1,0:T(8,128)(2,1)} %all-gather.6.cloned.1.call-done) | copy-start | bytes 12976132
Sparse Core Ops, SparseCore 0:
  40.7 40.2 all-gather.3
  83.2 50.4 all-gather.5

commit v11 on v10

--- a/solution.py
+++ b/solution.py
@@ -9,7 +9,8 @@
 GROUP = 128
 MAIN = 64
 SLOT = 32
-SHARE, ORDER, TRACK, PACK, DELIVER = 58, 30, 50, 40, 30
+STEP = 4
+SHARE, ORDER, TRACK, PACK, DELIVER = 58, 30, 40, 40, 52
 FACTOR = 1.4426950408889634 / HEAD_DIM**0.5
 CHIP = ("zh", "zl", "x")
 FRAME = CHIP + ("c",)
@@ -67,25 +68,29 @@
 def track_kernel(core_ref, tokens_ref, own_ref, other_ref, out_ref, o_ref):
     step = pl.program_id(0)
     core = core_ref[0]
+    here = tokens_ref.shape[0] // 2
     frames = 2 * tokens_ref.shape[1]
     lane = lanes_of((frames, 128))
-    tokens = tokens_ref[...].reshape(frames, tokens_ref.shape[2])
     right = jnp.concatenate([own_ref[...], other_ref[...]], axis=1)
-    both = jnp.dot(tokens, right, preferred_element_type=F32)
     ones = jnp.where(lane == 127, 1.0, 0.0)
-    for which in range(2):
-        head = core if which == 0 else 1 - core
-        out = both[:, which * 384 : which * 384 + 384]
-        query = jnp.where(lane < HEAD_DIM, out[:, :128] * FACTOR, 0.0).astype(BF16)
-        key = out[:, 128:256].astype(BF16)
-        value = jnp.where(lane < HEAD_DIM, out[:, 256:], ones).astype(BF16)
-        scores = lax.dot_general(query, key, (((1,), (1,)), ((), ())), preferred_element_type=F32)
-        top = jnp.max(scores, axis=-1, keepdims=True)
-        expo = jnp.exp2(scores - top).astype(BF16)
-        mixed = jnp.dot(expo, value, preferred_element_type=F32)
-        mixed = jnp.where(lane < HEAD_DIM, mixed * (1.0 / mixed[:, 127:]), 0.0)
-        mixed = mixed.reshape(frames // 8, 8, 128)
-        o_ref[:, pl.ds(head * 4 + step, 8, stride=8), :] = mixed
+    for track in range(here):
+        tokens = tokens_ref[2 * track : 2 * track + 2].reshape(frames, tokens_ref.shape[2])
+        both = jnp.dot(tokens, right, preferred_element_type=F32)
+        for which in range(2):
+            head = core if which == 0 else 1 - core
+            out = both[:, which * 384 : which * 384 + 384]
+            query = jnp.where(lane < HEAD_DIM, out[:, :128] * FACTOR, 0.0).astype(BF16)
+            key = out[:, 128:256].astype(BF16)
+            value = jnp.where(lane < HEAD_DIM, out[:, 256:], ones).astype(BF16)
+            scores = lax.dot_general(
+                query, key, (((1,), (1,)), ((), ())), preferred_element_type=F32
+            )
+            top = jnp.max(scores, axis=-1, keepdims=True)
+            expo = jnp.exp2(scores - top).astype(BF16)
+            mixed = jnp.dot(expo, value, preferred_element_type=F32)
+            mixed = jnp.where(lane < HEAD_DIM, mixed * (1.0 / mixed[:, 127:]), 0.0)
+            mixed = mixed.reshape(frames // 8, 8, 128)
+            o_ref[:, pl.ds(head * 4 + step * here + track, 8, stride=8), :] = mixed
 
     @pl.when(step == pl.num_programs(0) - 1)
     def _():
@@ -268,10 +273,10 @@
 
     attended = pl.pallas_call(
         track_kernel,
-        grid=(4,),
+        grid=(4 // STEP,),
         in_specs=[
             pl.BlockSpec(memory_space=pltpu.SMEM),
-            pl.BlockSpec((2, 4 * chips, width), lambda p: (p, 0, 0)),
+            pl.BlockSpec((2 * STEP, 4 * chips, width), lambda p: (p, 0, 0)),
             pl.BlockSpec(mine.shape, lambda p: (0, 0)),
             pl.BlockSpec(mine.shape, lambda p: (0, 0)),
         ],

time: 159 us -> 157 us (0.987)
  no operation moved by 1% of the time
where the time goes in v11:
time: 157 us
  blocking collectives  58.5 us (37%)
  starting transfers between devices  30.6 us (19%)
  waiting for transfers between devices  29.5 us (19%)
  Pallas kernels  17.6 us (11%)
  between operations  14.8 us (9%)
  local copies, waits for them, and re-layouts  3.57 us (2%)
  other arithmetic  2.07 us (1%)
    all_to_all x1, blocking collectives, local(): lax.all_to_all(share, FRAME, 0, 0, tiled=True).reshape(4 * chips, width)  29.5 us
    all_to_all x2, blocking collectives, spread(): return lax.all_to_all(copies, axis, 0, 0, tiled=True)  27.2 us
    all_to_all x1, waiting for transfers between devices, local(): gathered = lax.all_to_all(packed, ('c', 'pool'), 0, 0, tiled=True)  19.6 us
    all_to_all x1, starting transfers between devices, local(): gathered = lax.all_to_all(packed, ('c', 'pool'), 0, 0, tiled=True)  9.94 us
    all_to_all x1, starting transfers between devices, local(): returned = lax.all_to_all(attended, CHIP, 0, 0, tiled=True)  9.89 us
    pallas_call x1, Pallas kernels, local(): pl.pallas_call(track_kernel, grid=(4 // STEP,), in_specs=[pl.BlockSpec(me...  6.13 us
    ppermute x1, starting transfers between devices, local(): mine_other = lax.ppermute(mine, 'c', swap)  5.79 us
    all_to_all x1, waiting for transfers between devices, local(): returned = lax.all_to_all(attended, CHIP, 0, 0, tiled=True)  5.63 us
  transfers between devices with their start and end apart: 6, of which 5 were waited for; matrix products, arithmetic and copies ran while one was open for 2% of the time, Pallas kernels for 6%

profile of v11, /device:TPU:1, one launch (start us, length us, event | category | flops | bytes accessed | tf_op | source)
XLA Modules:
  0.0 156.7 jit_solution(2766517526368149731)
XLA Ops:
  7.2 3.0 %share.1 = bf16[64,2,1408]{2,1,0:T(2,128)(2,1)} custom-call(s32[1]{0:T(128)} %bitcast.3.at_ref, bf16[4,256,1408]{2,1,0:T(8,128)(2,1)} %frame_ref.1), custom_call_target="tpu_custom_call" | custom-call | tf_op jit(solution)/shard_map/share/pallas_call | solution.py:226
  10.2 29.5 %all_to_all.25 = bf16[64,2,1408]{2,1,0:T(2,128)(2,1)S(1)} all-to-all(bf16[64,2,1408]{2,1,0:T(2,128)(2,1)} %share.1), channel_id=1, replica_groups=mesh['zh'=4,'zl'=2,'x'=4,'c'=2,'pool'=8] {'zh','zl','x','c'}, dimensions={0} | all-to-all | bytes 720896 | tf_op jit(solution)/shard_map/all_to_all | solution.py:238
  39.7 0.9 all_gather_reshape.3
  41.1 0.2 concatenate.11
  41.4 1.9 %all_gather.13 = bf16[44,2,384]{2,1,0:T(2,128)(2,1)S(1)} all-gather(bf16[22,2,384]{2,1,0:T(2,128)(2,1)S(1)} %concatenate.11), channel_id=1, replica_groups=mesh['zh'=4,'zl'=2,'x'=4,'c'=2,'pool'=8] {'c'}, dimensions={0}, use_global_device_ids=true | all-gather | bytes 101376 | tf_op jit(solution)/shard_map/all_gather | solution.py:257
  43.3 10.7 %all_to_all.26 = bf16[4,44,384]{2,1,0:T(8,128)(2,1)S(1)} all-to-all(bf16[4,44,384]{2,1,0:T(8,128)(2,1)S(1)} %broadcast_in_dim.22), channel_id=1, replica_groups=mesh['zh'=4,'zl'=2,'x'=4,'c'=2,'pool'=8] {'zh'}, dimensions={0} | all-to-all | bytes 270336 | tf_op jit(solution)/shard_map/all_to_all | solution.py:35
  54.2 16.4 %all_to_all.27.source_ref = bf16[8,176,384]{2,1,0:T(8,128)(2,1)S(1)} all-to-all(bf16[8,176,384]{2,1,0:T(8,128)(2,1)S(1)} %broadcast_in_dim.24), channel_id=1, replica_groups=mesh['zh'=4,'zl'=2,'x'=4,'c'=2,'pool'=8] {'zl','x'}, dimensions={0} | all-to-all | bytes 2162688 | tf_op jit(solution)/shard_map/all_to_all | solution.py:35
  70.6 1.2 order.1
  71.8 5.8 %collective-permute-start.1 = (bf16[1408,384]{1,0:T(8,128)(2,1)S(1)}, bf16[1408,384]{1,0:T(8,128)(2,1)S(1)}, u32[]{:S(2)}, u32[]{:S(2)}) collective-permute-start(bf16[1408,384]{1,0:T(8,128)(2,1)S(1)} %get-tuple-element.4.own_ref), channel_id=1, source_target_pairs={{0,8},{8,0},{1,9},{9,1},{2,10},{10,2},{3,11},{11,3},{4,12},{12,4},... | collective-permute-start | bytes 3244040 | tf_op jit(solution)/shard_map/ppermute | solution.py:271
  77.6 2.3 %collective-permute-done.1.other_ref = bf16[1408,384]{1,0:T(8,128)(2,1)S(1)} collective-permute-done((bf16[1408,384]{1,0:T(8,128)(2,1)S(1)}, bf16[1408,384]{1,0:T(8,128)(2,1)S(1)}, u32[]{:S(2)}, u32[]{:S(2)}) %collective-permute-start.1) | collective-permute-done | bytes 1081376 | tf_op jit(solution)/shard_map/ppermute | solution.py:271
  79.9 1.1 all-gather.4.cloned.1.call-done.tokens_ref
  81.1 1.8 %copy-done = bf16[8,128,1408]{2,1,0:T(8,128)(2,1)S(1)} copy-done((bf16[8,128,1408]{2,1,0:T(8,128)(2,1)S(1)}, bf16[8,128,1408]{2,1,0:T(8,128)(2,1)}, u32[]{:S(2)}) %copy-start) | copy-done | bytes 2883608
  82.9 6.1 %track.1 = bf16[16,2,6,8,128]{4,3,2,1,0:T(8,128)(2,1)} custom-call(s32[1]{0:T(128)} %bitcast.2.core_ref, bf16[8,128,1408]{2,1,0:T(8,128)(2,1)S(1)} %copy-done, bf16[1408,384]{1,0:T(8,128)(2,1)S(1)} %get-tuple-element.4.own_ref, bf16[1408,384]{1,0:T(8,128)(2,1)S(1)} %collective-permute-done.1.other_ref), custom_call_target="tpu_custom_call" | custom-call | tf_op jit(solution)/shard_map/track/pallas_call | solution.py:274
  89.0 9.9 %all-to-all-start.3 = ((bf16[32,6,8,128]{3,2,1,0:T(8,128)(2,1)}), bf16[32,6,8,128]{3,2,1,0:T(8,128)(2,1)S(1)}, u32[]{:S(2)}, u32[]{:S(2)}) async-start(bf16[32,6,8,128]{3,2,1,0:T(8,128)(2,1)} %bitcast.9), calls=%async_computation.3 | async-start | bytes 786432 | tf_op jit(solution)/shard_map/all_to_all | solution.py:290
  98.9 4.9 %collective-permute-start = (s32[4]{0:T(128)S(1)}, s32[4]{0:T(128)S(1)}, u32[]{:S(2)}, u32[]{:S(2)}) collective-permute-start(s32[4]{0:T(128)S(1)} %copy-done.3), channel_id=1, source_target_pairs={{0,8},{8,0},{1,9},{9,1},{2,10},{10,2},{3,11},{11,3},{4,12},{12,4},... | collective-permute-start | bytes 56 | tf_op jit(solution)/shard_map/ppermute | solution.py:240
  103.9 0.8 collective-permute-done
  104.7 5.6 %all-to-all-done.3 = bf16[32,6,8,128]{3,2,1,0:T(8,128)(2,1)S(1)} async-done(((bf16[32,6,8,128]{3,2,1,0:T(8,128)(2,1)}), bf16[32,6,8,128]{3,2,1,0:T(8,128)(2,1)S(1)}, u32[]{:S(2)}, u32[]{:S(2)}) %all-to-all-start.3) | async-done | bytes 393248 | tf_op jit(solution)/shard_map/all_to_all | solution.py:290
  110.4 1.9 %pack.1 = bf16[16,24,8,128]{3,2,1,0:T(8,128)(2,1)} custom-call(s32[8]{0:T(128)S(1)} %broadcast_select_fusion.owner_ref, bf16[16,2,6,8,128]{4,3,2,1,0:T(8,128)(2,1)S(1)} %bitcast.19), custom_call_target="tpu_custom_call" | custom-call | tf_op jit(solution)/shard_map/pack/pallas_call | solution.py:297
  112.3 9.9 %all-to-all-start.4 = ((bf16[16,24,8,128]{3,2,1,0:T(8,128)(2,1)}), bf16[16,24,8,128]{3,2,1,0:T(8,128)(2,1)S(1)}, u32[]{:S(2)}, u32[]{:S(2)}) async-start(bf16[16,24,8,128]{3,2,1,0:T(8,128)(2,1)} %pack.1), calls=%async_computation.4 | async-start | bytes 1572864 | tf_op jit(solution)/shard_map/all_to_all | solution.py:308
  122.2 0.6 select_reduce_fusion
  122.9 0.6 reduce_or.9
  124.2 0.7 pad_add_fusion.pick_ref
  124.9 19.6 %all-to-all-done.4.y_ref = bf16[16,24,8,128]{3,2,1,0:T(8,128)(2,1)S(1)} async-done(((bf16[16,24,8,128]{3,2,1,0:T(8,128)(2,1)}), bf16[16,24,8,128]{3,2,1,0:T(8,128)(2,1)S(1)}, u32[]{:S(2)}, u32[]{:S(2)}) %all-to-all-start.4) | async-done | bytes 786464 | tf_op jit(solution)/shard_map/all_to_all | solution.py:308
  144.5 5.4 %deliver.1 = (bf16[1,256,1408]{2,1,0:T(8,128)(2,1)}, bf16[1,11,256]{2,1,0:T(8,128)(2,1)}) custom-call(s32[2]{0:T(128)S(1)} %pad_add_fusion.pick_ref, bf16[4,256,1408]{2,1,0:T(8,128)(2,1)} %frame_ref.1, bf16[16,24,8,128]{3,2,1,0:T(8,128)(2,1)S(1)} %all-to-all-done.4.y_ref, bf16[16,96,1408]{2,1,0:T(8,128)(2,1)} %bitcast.20), custom_call_target="tpu_custom_call" | custom-call | tf_op jit(solution)/shard_map/deliver/pallas_call | solution.py:314
  (26 shorter events, 0.8 us)
Async XLA Ops:
  7.2 73.9 %all-gather.4.cloned.1.call-start = ((), (), s32[]{:S(2)}) async-start(), calls=%async_computation.5 | async-start | bytes 3244032 | tf_op jit(solution)/shard_map/all_gather | solution.py:239
  10.2 30.4 %copy-start.1 = (bf16[22,3,176]{2,0,1:T(8,128)(2,1)S(1)}, bf16[22,3,176]{2,0,1:T(8,128)(2,1)}, u32[]{:S(2)}) copy-start(bf16[22,3,176]{2,0,1:T(8,128)(2,1)} %param.6) | copy-start | bytes 69700
  10.2 30.6 %copy-start.2 = (bf16[176,22]{0,1:T(8,128)(2,1)S(1)}, bf16[176,22]{0,1:T(8,128)(2,1)}, u32[]{:S(2)}) copy-start(bf16[176,22]{0,1:T(8,128)(2,1)} %param.7) | copy-start | bytes 23236
  40.6 103.8 %all-gather.6.cloned.1.call-start = ((), (), s32[]{:S(2)}) async-start(), calls=%async_computation.6 | async-start | bytes 4595712 | tf_op jit(solution)/shard_map/all_gather | solution.py:272
  71.8 8.1 %collective-permute-start.1 = (bf16[1408,384]{1,0:T(8,128)(2,1)S(1)}, bf16[1408,384]{1,0:T(8,128)(2,1)S(1)}, u32[]{:S(2)}, u32[]{:S(2)}) collective-permute-start(bf16[1408,384]{1,0:T(8,128)(2,1)S(1)} %get-tuple-element.4.own_ref), channel_id=1, source_target_pairs={{0,8},{8,0},{1,9},{9,1},{2,10},{10,2},{3,11},{11,3},{4,12},{12,4},... | collective-permute-start | bytes 3244040 | tf_op jit(solution)/shard_map/ppermute | solution.py:271
  81.1 1.8 %copy-start = (bf16[8,128,1408]{2,1,0:T(8,128)(2,1)S(1)}, bf16[8,128,1408]{2,1,0:T(8,128)(2,1)}, u32[]{:S(2)}) copy-start(bf16[8,128,1408]{2,1,0:T(8,128)(2,1)} %all-gather.4.cloned.1.call-done.tokens_ref) | copy-start | bytes 8650756
  82.9 16.0 %copy-start.3 = (s32[4]{0:T(128)S(1)}, s32[4]{0:T(128)}, u32[]{:S(2)}) copy-start(s32[4]{0:T(128)} %param.8) | copy-start | bytes 52
  89.0 21.4 %all-to-all-start.3 = ((bf16[32,6,8,128]{3,2,1,0:T(8,128)(2,1)}), bf16[32,6,8,128]{3,2,1,0:T(8,128)(2,1)S(1)}, u32[]{:S(2)}, u32[]{:S(2)}) async-start(bf16[32,6,8,128]{3,2,1,0:T(8,128)(2,1)} %bitcast.9), calls=%async_computation.3 | async-start | bytes 786432 | tf_op jit(solution)/shard_map/all_to_all | solution.py:290
  98.9 5.7 %collective-permute-start = (s32[4]{0:T(128)S(1)}, s32[4]{0:T(128)S(1)}, u32[]{:S(2)}, u32[]{:S(2)}) collective-permute-start(s32[4]{0:T(128)S(1)} %copy-done.3), channel_id=1, source_target_pairs={{0,8},{8,0},{1,9},{9,1},{2,10},{10,2},{3,11},{11,3},{4,12},{12,4},... | collective-permute-start | bytes 56 | tf_op jit(solution)/shard_map/ppermute | solution.py:240
  112.3 9.9 %copy-start.4 = (s32[4]{0:T(128)S(1)}, s32[4]{0:T(128)}, u32[]{:S(2)}) copy-start(s32[4]{0:T(128)} %param.9) | copy-start | bytes 52
  112.3 32.2 %all-to-all-start.4 = ((bf16[16,24,8,128]{3,2,1,0:T(8,128)(2,1)}), bf16[16,24,8,128]{3,2,1,0:T(8,128)(2,1)S(1)}, u32[]{:S(2)}, u32[]{:S(2)}) async-start(bf16[16,24,8,128]{3,2,1,0:T(8,128)(2,1)} %pack.1), calls=%async_computation.4 | async-start | bytes 1572864 | tf_op jit(solution)/shard_map/all_to_all | solution.py:308
Sparse Core Ops, SparseCore 0:
  40.7 40.2 all-gather.3
  83.2 50.1 all-gather.5

commit v12 on v11

--- a/solution.py
+++ b/solution.py
@@ -9,8 +9,8 @@
 GROUP = 128
 MAIN = 64
 SLOT = 32
-STEP = 4
-SHARE, ORDER, TRACK, PACK, DELIVER = 58, 30, 40, 40, 52
+STEP = 1
+SHARE, ORDER, TRACK, PACK, DELIVER = 58, 30, 50, 40, 52
 FACTOR = 1.4426950408889634 / HEAD_DIM**0.5
 CHIP = ("zh", "zl", "x")
 FRAME = CHIP + ("c",)

time: 157 us -> 157 us (level)
  local copies, waits for them, and re-layouts: 3.57 us -> 1.75 us
  Pallas kernels: 17.6 us -> 19.2 us
    unnamed x11 -> x9, local copies, waits for them, and re-layouts: 1.84 us -> 0.02 us
  transfers between devices with their start and end apart: 6 -> 6, of which waited for: 5 -> 5; matrix products, arithmetic and copies ran while one was open for 2% -> 2% of each run, Pallas kernels for 6% -> 7%
where the time goes in v12:
time: 157 us; the launch traced here: 156 us
  blocking collectives  58.5 us (37%)
  starting transfers between devices  30.6 us (19%)
  waiting for transfers between devices  29.4 us (19%)
  Pallas kernels  19.2 us (12%)
  between operations  14.8 us (9%)
  other arithmetic  2.07 us (1%)
  local copies, waits for them, and re-layouts  1.75 us (1%)
    all_to_all x1, blocking collectives, local(): lax.all_to_all(share, FRAME, 0, 0, tiled=True).reshape(4 * chips, width)  29.5 us
    all_to_all x2, blocking collectives, spread(): return lax.all_to_all(copies, axis, 0, 0, tiled=True)  27.2 us
    all_to_all x1, waiting for transfers between devices, local(): gathered = lax.all_to_all(packed, ('c', 'pool'), 0, 0, tiled=True)  19.5 us
    all_to_all x1, starting transfers between devices, local(): gathered = lax.all_to_all(packed, ('c', 'pool'), 0, 0, tiled=True)  9.93 us
    all_to_all x1, starting transfers between devices, local(): returned = lax.all_to_all(attended, CHIP, 0, 0, tiled=True)  9.89 us
    pallas_call x1, Pallas kernels, local(): pl.pallas_call(track_kernel, grid=(4 // STEP,), in_specs=[pl.BlockSpec(me...  7.69 us
    ppermute x1, starting transfers between devices, local(): mine_other = lax.ppermute(mine, 'c', swap)  5.79 us
    all_to_all x1, waiting for transfers between devices, local(): returned = lax.all_to_all(attended, CHIP, 0, 0, tiled=True)  5.63 us
  transfers between devices with their start and end apart: 6, of which 5 were waited for; matrix products, arithmetic and copies ran while one was open for 2% of the time, Pallas kernels for 7%

profile of v12, /device:TPU:1, one launch (start us, length us, event | category | flops | bytes accessed | tf_op | source)
XLA Modules:
  0.0 156.4 jit_solution(7054637548424045333)
XLA Ops:
  7.2 3.0 %share.1 = bf16[64,2,1408]{2,1,0:T(2,128)(2,1)} custom-call(s32[1]{0:T(128)} %bitcast.3.at_ref, bf16[4,256,1408]{2,1,0:T(8,128)(2,1)} %frame_ref.1), custom_call_target="tpu_custom_call" | custom-call | tf_op jit(solution)/shard_map/share/pallas_call | solution.py:226
  10.2 29.5 %all_to_all.25 = bf16[64,2,1408]{2,1,0:T(2,128)(2,1)S(1)} all-to-all(bf16[64,2,1408]{2,1,0:T(2,128)(2,1)} %share.1), channel_id=1, replica_groups=mesh['zh'=4,'zl'=2,'x'=4,'c'=2,'pool'=8] {'zh','zl','x','c'}, dimensions={0} | all-to-all | bytes 720896 | tf_op jit(solution)/shard_map/all_to_all | solution.py:238
  39.7 0.9 all_gather_reshape.3
  40.7 0.1 reshape.27
  41.1 0.2 concatenate.11
  41.4 1.9 %all_gather.13 = bf16[44,2,384]{2,1,0:T(2,128)(2,1)S(1)} all-gather(bf16[22,2,384]{2,1,0:T(2,128)(2,1)S(1)} %concatenate.11), channel_id=1, replica_groups=mesh['zh'=4,'zl'=2,'x'=4,'c'=2,'pool'=8] {'c'}, dimensions={0}, use_global_device_ids=true | all-gather | bytes 101376 | tf_op jit(solution)/shard_map/all_gather | solution.py:257
  43.3 10.7 %all_to_all.26 = bf16[4,44,384]{2,1,0:T(8,128)(2,1)S(1)} all-to-all(bf16[4,44,384]{2,1,0:T(8,128)(2,1)S(1)} %broadcast_in_dim.22), channel_id=1, replica_groups=mesh['zh'=4,'zl'=2,'x'=4,'c'=2,'pool'=8] {'zh'}, dimensions={0} | all-to-all | bytes 270336 | tf_op jit(solution)/shard_map/all_to_all | solution.py:35
  54.2 16.4 %all_to_all.27.source_ref = bf16[8,176,384]{2,1,0:T(8,128)(2,1)S(1)} all-to-all(bf16[8,176,384]{2,1,0:T(8,128)(2,1)S(1)} %broadcast_in_dim.24), channel_id=1, replica_groups=mesh['zh'=4,'zl'=2,'x'=4,'c'=2,'pool'=8] {'zl','x'}, dimensions={0} | all-to-all | bytes 2162688 | tf_op jit(solution)/shard_map/all_to_all | solution.py:35
  70.6 1.2 order.1
  71.8 5.8 %collective-permute-start.1 = (bf16[1408,384]{1,0:T(8,128)(2,1)S(1)}, bf16[1408,384]{1,0:T(8,128)(2,1)S(1)}, u32[]{:S(2)}, u32[]{:S(2)}) collective-permute-start(bf16[1408,384]{1,0:T(8,128)(2,1)S(1)} %get-tuple-element.4.own_ref), channel_id=1, source_target_pairs={{0,8},{8,0},{1,9},{9,1},{2,10},{10,2},{3,11},{11,3},{4,12},{12,4},... | collective-permute-start | bytes 3244040 | tf_op jit(solution)/shard_map/ppermute | solution.py:271
  77.6 2.3 %collective-permute-done.1.other_ref = bf16[1408,384]{1,0:T(8,128)(2,1)S(1)} collective-permute-done((bf16[1408,384]{1,0:T(8,128)(2,1)S(1)}, bf16[1408,384]{1,0:T(8,128)(2,1)S(1)}, u32[]{:S(2)}, u32[]{:S(2)}) %collective-permute-start.1) | collective-permute-done | bytes 1081376 | tf_op jit(solution)/shard_map/ppermute | solution.py:271
  79.9 1.1 all-gather.4.cloned.1.call-done.tokens_ref
  81.1 7.7 %track.1 = bf16[16,2,6,8,128]{4,3,2,1,0:T(8,128)(2,1)} custom-call(s32[1]{0:T(128)} %bitcast.2.core_ref, bf16[8,128,1408]{2,1,0:T(8,128)(2,1)} %all-gather.4.cloned.1.call-done.tokens_ref, bf16[1408,384]{1,0:T(8,128)(2,1)S(1)} %get-tuple-element.4.own_ref, bf16[1408,384]{1,0:T(8,128)(2,1)S(1)} %collective-permute-done.1.other_ref), custom_call_target="tpu_custom_call" | custom-call | tf_op jit(solution)/shard_map/track/pallas_call | solution.py:274
  88.7 9.9 %all-to-all-start.3 = ((bf16[32,6,8,128]{3,2,1,0:T(8,128)(2,1)}), bf16[32,6,8,128]{3,2,1,0:T(8,128)(2,1)S(1)}, u32[]{:S(2)}, u32[]{:S(2)}) async-start(bf16[32,6,8,128]{3,2,1,0:T(8,128)(2,1)} %bitcast.9), calls=%async_computation.3 | async-start | bytes 786432 | tf_op jit(solution)/shard_map/all_to_all | solution.py:290
  98.7 4.9 %collective-permute-start = (s32[4]{0:T(128)S(1)}, s32[4]{0:T(128)S(1)}, u32[]{:S(2)}, u32[]{:S(2)}) collective-permute-start(s32[4]{0:T(128)S(1)} %copy-done.2), channel_id=1, source_target_pairs={{0,8},{8,0},{1,9},{9,1},{2,10},{10,2},{3,11},{11,3},{4,12},{12,4},... | collective-permute-start | bytes 56 | tf_op jit(solution)/shard_map/ppermute | solution.py:240
  103.6 0.8 collective-permute-done
  104.5 5.6 %all-to-all-done.3 = bf16[32,6,8,128]{3,2,1,0:T(8,128)(2,1)S(1)} async-done(((bf16[32,6,8,128]{3,2,1,0:T(8,128)(2,1)}), bf16[32,6,8,128]{3,2,1,0:T(8,128)(2,1)S(1)}, u32[]{:S(2)}, u32[]{:S(2)}) %all-to-all-start.3) | async-done | bytes 393248 | tf_op jit(solution)/shard_map/all_to_all | solution.py:290
  110.1 1.9 %pack.1 = bf16[16,24,8,128]{3,2,1,0:T(8,128)(2,1)} custom-call(s32[8]{0:T(128)S(1)} %broadcast_select_fusion.owner_ref, bf16[16,2,6,8,128]{4,3,2,1,0:T(8,128)(2,1)S(1)} %bitcast.19), custom_call_target="tpu_custom_call" | custom-call | tf_op jit(solution)/shard_map/pack/pallas_call | solution.py:297
  112.0 9.9 %all-to-all-start.4 = ((bf16[16,24,8,128]{3,2,1,0:T(8,128)(2,1)}), bf16[16,24,8,128]{3,2,1,0:T(8,128)(2,1)S(1)}, u32[]{:S(2)}, u32[]{:S(2)}) async-start(bf16[16,24,8,128]{3,2,1,0:T(8,128)(2,1)} %pack.1), calls=%async_computation.4 | async-start | bytes 1572864 | tf_op jit(solution)/shard_map/all_to_all | solution.py:308
  122.0 0.6 select_reduce_fusion
  122.6 0.6 reduce_or.9
  123.9 0.7 pad_add_fusion.pick_ref
  124.6 19.5 %all-to-all-done.4.y_ref = bf16[16,24,8,128]{3,2,1,0:T(8,128)(2,1)S(1)} async-done(((bf16[16,24,8,128]{3,2,1,0:T(8,128)(2,1)}), bf16[16,24,8,128]{3,2,1,0:T(8,128)(2,1)S(1)}, u32[]{:S(2)}, u32[]{:S(2)}) %all-to-all-start.4) | async-done | bytes 786464 | tf_op jit(solution)/shard_map/all_to_all | solution.py:308
  144.2 5.4 %deliver.1 = (bf16[1,256,1408]{2,1,0:T(8,128)(2,1)}, bf16[1,11,256]{2,1,0:T(8,128)(2,1)}) custom-call(s32[2]{0:T(128)S(1)} %pad_add_fusion.pick_ref, bf16[4,256,1408]{2,1,0:T(8,128)(2,1)} %frame_ref.1, bf16[16,24,8,128]{3,2,1,0:T(8,128)(2,1)S(1)} %all-to-all-done.4.y_ref, bf16[16,96,1408]{2,1,0:T(8,128)(2,1)} %bitcast.20), custom_call_target="tpu_custom_call" | custom-call | tf_op jit(solution)/shard_map/deliver/pallas_call | solution.py:314
  (24 shorter events, 0.7 us)
Async XLA Ops:
  7.2 73.9 %all-gather.4.cloned.1.call-start = ((), (), s32[]{:S(2)}) async-start(), calls=%async_computation.5 | async-start | bytes 3244032 | tf_op jit(solution)/shard_map/all_gather | solution.py:239
  10.2 30.4 %copy-start = (bf16[22,3,176]{2,0,1:T(8,128)(2,1)S(1)}, bf16[22,3,176]{2,0,1:T(8,128)(2,1)}, u32[]{:S(2)}) copy-start(bf16[22,3,176]{2,0,1:T(8,128)(2,1)} %param.6) | copy-start | bytes 69700
  10.2 30.6 %copy-start.1 = (bf16[176,22]{0,1:T(8,128)(2,1)S(1)}, bf16[176,22]{0,1:T(8,128)(2,1)}, u32[]{:S(2)}) copy-start(bf16[176,22]{0,1:T(8,128)(2,1)} %param.7) | copy-start | bytes 23236
  40.6 103.5 %all-gather.6.cloned.1.call-start = ((), (), s32[]{:S(2)}) async-start(), calls=%async_computation.6 | async-start | bytes 4595712 | tf_op jit(solution)/shard_map/all_gather | solution.py:272
  71.8 8.1 %collective-permute-start.1 = (bf16[1408,384]{1,0:T(8,128)(2,1)S(1)}, bf16[1408,384]{1,0:T(8,128)(2,1)S(1)}, u32[]{:S(2)}, u32[]{:S(2)}) collective-permute-start(bf16[1408,384]{1,0:T(8,128)(2,1)S(1)} %get-tuple-element.4.own_ref), channel_id=1, source_target_pairs={{0,8},{8,0},{1,9},{9,1},{2,10},{10,2},{3,11},{11,3},{4,12},{12,4},... | collective-permute-start | bytes 3244040 | tf_op jit(solution)/shard_map/ppermute | solution.py:271
  81.1 17.6 %copy-start.2 = (s32[4]{0:T(128)S(1)}, s32[4]{0:T(128)}, u32[]{:S(2)}) copy-start(s32[4]{0:T(128)} %param.8) | copy-start | bytes 52
  88.7 21.4 %all-to-all-start.3 = ((bf16[32,6,8,128]{3,2,1,0:T(8,128)(2,1)}), bf16[32,6,8,128]{3,2,1,0:T(8,128)(2,1)S(1)}, u32[]{:S(2)}, u32[]{:S(2)}) async-start(bf16[32,6,8,128]{3,2,1,0:T(8,128)(2,1)} %bitcast.9), calls=%async_computation.3 | async-start | bytes 786432 | tf_op jit(solution)/shard_map/all_to_all | solution.py:290
  98.7 5.7 %collective-permute-start = (s32[4]{0:T(128)S(1)}, s32[4]{0:T(128)S(1)}, u32[]{:S(2)}, u32[]{:S(2)}) collective-permute-start(s32[4]{0:T(128)S(1)} %copy-done.2), channel_id=1, source_target_pairs={{0,8},{8,0},{1,9},{9,1},{2,10},{10,2},{3,11},{11,3},{4,12},{12,4},... | collective-permute-start | bytes 56 | tf_op jit(solution)/shard_map/ppermute | solution.py:240
  112.0 9.9 %copy-start.3 = (s32[4]{0:T(128)S(1)}, s32[4]{0:T(128)}, u32[]{:S(2)}) copy-start(s32[4]{0:T(128)} %param.9) | copy-start | bytes 52
  112.0 32.1 %all-to-all-start.4 = ((bf16[16,24,8,128]{3,2,1,0:T(8,128)(2,1)}), bf16[16,24,8,128]{3,2,1,0:T(8,128)(2,1)S(1)}, u32[]{:S(2)}, u32[]{:S(2)}) async-start(bf16[16,24,8,128]{3,2,1,0:T(8,128)(2,1)} %pack.1), calls=%async_computation.4 | async-start | bytes 1572864 | tf_op jit(solution)/shard_map/all_to_all | solution.py:308
Sparse Core Ops, SparseCore 0:
  40.7 40.2 all-gather.3
  83.2 50.2 all-gather.5

commit v13 on v12

--- a/solution.py
+++ b/solution.py
@@ -132,20 +132,21 @@
 
     lane = lanes_of((pairs, 8, 128))
     lane_h = lanes_of((pairs // 2, 8, 128))
-    for fr in range(8):
-        place = (fr // 4) * 8 + owner_ref[fr]
-        tiles = [x_ref[:, side, fr // 2].astype(F32) for side in range(2)]
+    core = pl.program_id(0)
+    for fr in range(4):
+        place = owner_ref[core * 4 + fr]
+        tiles = [x_ref[:, side, 2 * core + fr // 2].astype(F32) for side in range(2)]
         even, odd = (
             [turn(tile, MAIN * head - MAIN * (fr % 2)) for head in range(2)] for tile in tiles
         )
         out_ref[place, :pairs] = join(even, odd, lane, MAIN).astype(BF16)
-        tiles = [x_ref[:, side, 4 + fr // 4].astype(F32) for side in range(2)]
+        tiles = [x_ref[:, side, 4 + core].astype(F32) for side in range(2)]
         rests = []
         for half in range(2):
             rows = slice(half * (pairs // 2), (half + 1) * (pairs // 2))
             even, odd = (
                 [
-                    turn(tile[rows], 2 * SLOT * half + SLOT * head - SLOT * (fr % 4))
+                    turn(tile[rows], 2 * SLOT * half + SLOT * head - SLOT * fr)
                     for head in range(2)
                 ]
                 for tile in tiles
@@ -296,11 +297,12 @@
     )
     packed = pl.pallas_call(
         pack_kernel,
+        grid=(2,),
         in_specs=[
             pl.BlockSpec(memory_space=pltpu.SMEM),
-            pl.BlockSpec(memory_space=pltpu.VMEM),
-        ],
-        out_specs=pl.BlockSpec(memory_space=pltpu.VMEM),
+            pl.BlockSpec((chips // 2, 2, 6, 8, 128), lambda c: (0, 0, 0, 0, 0)),
+        ],
+        out_specs=pl.BlockSpec((sources // 2, 3 * chips // 4, 8, 128), lambda c: (c, 0, 0, 0)),
         out_shape=jax.ShapeDtypeStruct((sources, 3 * chips // 4, 8, 128), BF16),
         compiler_params=params(PACK),
         name="pack",

time: 157 us -> 157 us (level)
  no operation moved by 1% of the time
where the time goes in v13:
time: 157 us; the launch traced here: 156 us
  blocking collectives  58.5 us (37%)
  starting transfers between devices  30.6 us (19%)
  waiting for transfers between devices  29.5 us (19%)
  Pallas kernels  19.1 us (12%)
  between operations  14.8 us (9%)
  other arithmetic  2.07 us (1%)
  local copies, waits for them, and re-layouts  1.75 us (1%)
    all_to_all x1, blocking collectives, local(): lax.all_to_all(share, FRAME, 0, 0, tiled=True).reshape(4 * chips, width)  29.5 us
    all_to_all x2, blocking collectives, spread(): return lax.all_to_all(copies, axis, 0, 0, tiled=True)  27.2 us
    all_to_all x1, waiting for transfers between devices, local(): gathered = lax.all_to_all(packed, ('c', 'pool'), 0, 0, tiled=True)  19.6 us
    all_to_all x1, starting transfers between devices, local(): gathered = lax.all_to_all(packed, ('c', 'pool'), 0, 0, tiled=True)  9.93 us
    all_to_all x1, starting transfers between devices, local(): returned = lax.all_to_all(attended, CHIP, 0, 0, tiled=True)  9.89 us
    pallas_call x1, Pallas kernels, local(): pl.pallas_call(track_kernel, grid=(4 // STEP,), in_specs=[pl.BlockSpec(me...  7.69 us
    ppermute x1, starting transfers between devices, local(): mine_other = lax.ppermute(mine, 'c', swap)  5.79 us
    all_to_all x1, waiting for transfers between devices, local(): returned = lax.all_to_all(attended, CHIP, 0, 0, tiled=True)  5.63 us
  transfers between devices with their start and end apart: 6, of which 5 were waited for; matrix products, arithmetic and copies ran while one was open for 2% of the time, Pallas kernels for 7%

profile of v13, /device:TPU:1, one launch (start us, length us, event | category | flops | bytes accessed | tf_op | source)
XLA Modules:
  0.0 156.4 jit_solution(17746676097303096315)
XLA Ops:
  7.2 3.0 %share.1 = bf16[64,2,1408]{2,1,0:T(2,128)(2,1)} custom-call(s32[1]{0:T(128)} %bitcast.3.at_ref, bf16[4,256,1408]{2,1,0:T(8,128)(2,1)} %frame_ref.1), custom_call_target="tpu_custom_call" | custom-call | tf_op jit(solution)/shard_map/share/pallas_call | solution.py:227
  10.2 29.5 %all_to_all.25 = bf16[64,2,1408]{2,1,0:T(2,128)(2,1)S(1)} all-to-all(bf16[64,2,1408]{2,1,0:T(2,128)(2,1)} %share.1), channel_id=1, replica_groups=mesh['zh'=4,'zl'=2,'x'=4,'c'=2,'pool'=8] {'zh','zl','x','c'}, dimensions={0} | all-to-all | bytes 720896 | tf_op jit(solution)/shard_map/all_to_all | solution.py:239
  39.7 0.9 all_gather_reshape.3
  40.7 0.1 reshape.27
  41.1 0.2 concatenate.11
  41.4 1.9 %all_gather.13 = bf16[44,2,384]{2,1,0:T(2,128)(2,1)S(1)} all-gather(bf16[22,2,384]{2,1,0:T(2,128)(2,1)S(1)} %concatenate.11), channel_id=1, replica_groups=mesh['zh'=4,'zl'=2,'x'=4,'c'=2,'pool'=8] {'c'}, dimensions={0}, use_global_device_ids=true | all-gather | bytes 101376 | tf_op jit(solution)/shard_map/all_gather | solution.py:258
  43.3 10.7 %all_to_all.26 = bf16[4,44,384]{2,1,0:T(8,128)(2,1)S(1)} all-to-all(bf16[4,44,384]{2,1,0:T(8,128)(2,1)S(1)} %broadcast_in_dim.22), channel_id=1, replica_groups=mesh['zh'=4,'zl'=2,'x'=4,'c'=2,'pool'=8] {'zh'}, dimensions={0} | all-to-all | bytes 270336 | tf_op jit(solution)/shard_map/all_to_all | solution.py:35
  54.2 16.4 %all_to_all.27.source_ref = bf16[8,176,384]{2,1,0:T(8,128)(2,1)S(1)} all-to-all(bf16[8,176,384]{2,1,0:T(8,128)(2,1)S(1)} %broadcast_in_dim.24), channel_id=1, replica_groups=mesh['zh'=4,'zl'=2,'x'=4,'c'=2,'pool'=8] {'zl','x'}, dimensions={0} | all-to-all | bytes 2162688 | tf_op jit(solution)/shard_map/all_to_all | solution.py:35
  70.6 1.2 order.1
  71.8 5.8 %collective-permute-start.1 = (bf16[1408,384]{1,0:T(8,128)(2,1)S(1)}, bf16[1408,384]{1,0:T(8,128)(2,1)S(1)}, u32[]{:S(2)}, u32[]{:S(2)}) collective-permute-start(bf16[1408,384]{1,0:T(8,128)(2,1)S(1)} %get-tuple-element.4.own_ref), channel_id=1, source_target_pairs={{0,8},{8,0},{1,9},{9,1},{2,10},{10,2},{3,11},{11,3},{4,12},{12,4},... | collective-permute-start | bytes 3244040 | tf_op jit(solution)/shard_map/ppermute | solution.py:272
  77.6 2.3 %collective-permute-done.1.other_ref = bf16[1408,384]{1,0:T(8,128)(2,1)S(1)} collective-permute-done((bf16[1408,384]{1,0:T(8,128)(2,1)S(1)}, bf16[1408,384]{1,0:T(8,128)(2,1)S(1)}, u32[]{:S(2)}, u32[]{:S(2)}) %collective-permute-start.1) | collective-permute-done | bytes 1081376 | tf_op jit(solution)/shard_map/ppermute | solution.py:272
  79.9 1.1 all-gather.4.cloned.1.call-done.tokens_ref
  81.1 7.7 %track.1 = bf16[16,2,6,8,128]{4,3,2,1,0:T(8,128)(2,1)} custom-call(s32[1]{0:T(128)} %bitcast.2.core_ref, bf16[8,128,1408]{2,1,0:T(8,128)(2,1)} %all-gather.4.cloned.1.call-done.tokens_ref, bf16[1408,384]{1,0:T(8,128)(2,1)S(1)} %get-tuple-element.4.own_ref, bf16[1408,384]{1,0:T(8,128)(2,1)S(1)} %collective-permute-done.1.other_ref), custom_call_target="tpu_custom_call" | custom-call | tf_op jit(solution)/shard_map/track/pallas_call | solution.py:275
  88.7 9.9 %all-to-all-start.3 = ((bf16[32,6,8,128]{3,2,1,0:T(8,128)(2,1)}), bf16[32,6,8,128]{3,2,1,0:T(8,128)(2,1)S(1)}, u32[]{:S(2)}, u32[]{:S(2)}) async-start(bf16[32,6,8,128]{3,2,1,0:T(8,128)(2,1)} %bitcast.9), calls=%async_computation.3 | async-start | bytes 786432 | tf_op jit(solution)/shard_map/all_to_all | solution.py:291
  98.7 4.9 %collective-permute-start = (s32[4]{0:T(128)S(1)}, s32[4]{0:T(128)S(1)}, u32[]{:S(2)}, u32[]{:S(2)}) collective-permute-start(s32[4]{0:T(128)S(1)} %copy-done.2), channel_id=1, source_target_pairs={{0,8},{8,0},{1,9},{9,1},{2,10},{10,2},{3,11},{11,3},{4,12},{12,4},... | collective-permute-start | bytes 56 | tf_op jit(solution)/shard_map/ppermute | solution.py:241
  103.6 0.8 collective-permute-done
  104.5 5.6 %all-to-all-done.3 = bf16[32,6,8,128]{3,2,1,0:T(8,128)(2,1)S(1)} async-done(((bf16[32,6,8,128]{3,2,1,0:T(8,128)(2,1)}), bf16[32,6,8,128]{3,2,1,0:T(8,128)(2,1)S(1)}, u32[]{:S(2)}, u32[]{:S(2)}) %all-to-all-start.3) | async-done | bytes 393248 | tf_op jit(solution)/shard_map/all_to_all | solution.py:291
  110.1 1.8 %pack.1 = bf16[16,24,8,128]{3,2,1,0:T(8,128)(2,1)} custom-call(s32[8]{0:T(128)S(1)} %broadcast_select_fusion.owner_ref, bf16[16,2,6,8,128]{4,3,2,1,0:T(8,128)(2,1)S(1)} %bitcast.19), custom_call_target="tpu_custom_call" | custom-call | tf_op jit(solution)/shard_map/pack/pallas_call | solution.py:298
  112.0 9.9 %all-to-all-start.4 = ((bf16[16,24,8,128]{3,2,1,0:T(8,128)(2,1)}), bf16[16,24,8,128]{3,2,1,0:T(8,128)(2,1)S(1)}, u32[]{:S(2)}, u32[]{:S(2)}) async-start(bf16[16,24,8,128]{3,2,1,0:T(8,128)(2,1)} %pack.1), calls=%async_computation.4 | async-start | bytes 1572864 | tf_op jit(solution)/shard_map/all_to_all | solution.py:310
  121.9 0.6 select_reduce_fusion
  122.5 0.6 reduce_or.9
  123.8 0.7 pad_add_fusion.pick_ref
  124.5 19.6 %all-to-all-done.4.y_ref = bf16[16,24,8,128]{3,2,1,0:T(8,128)(2,1)S(1)} async-done(((bf16[16,24,8,128]{3,2,1,0:T(8,128)(2,1)}), bf16[16,24,8,128]{3,2,1,0:T(8,128)(2,1)S(1)}, u32[]{:S(2)}, u32[]{:S(2)}) %all-to-all-start.4) | async-done | bytes 786464 | tf_op jit(solution)/shard_map/all_to_all | solution.py:310
  144.1 5.4 %deliver.1 = (bf16[1,256,1408]{2,1,0:T(8,128)(2,1)}, bf16[1,11,256]{2,1,0:T(8,128)(2,1)}) custom-call(s32[2]{0:T(128)S(1)} %pad_add_fusion.pick_ref, bf16[4,256,1408]{2,1,0:T(8,128)(2,1)} %frame_ref.1, bf16[16,24,8,128]{3,2,1,0:T(8,128)(2,1)S(1)} %all-to-all-done.4.y_ref, bf16[16,96,1408]{2,1,0:T(8,128)(2,1)} %bitcast.20), custom_call_target="tpu_custom_call" | custom-call | tf_op jit(solution)/shard_map/deliver/pallas_call | solution.py:316
  (24 shorter events, 0.7 us)
Async XLA Ops:
  7.2 73.9 %all-gather.4.cloned.1.call-start = ((), (), s32[]{:S(2)}) async-start(), calls=%async_computation.5 | async-start | bytes 3244032 | tf_op jit(solution)/shard_map/all_gather | solution.py:240
  10.2 30.4 %copy-start = (bf16[22,3,176]{2,0,1:T(8,128)(2,1)S(1)}, bf16[22,3,176]{2,0,1:T(8,128)(2,1)}, u32[]{:S(2)}) copy-start(bf16[22,3,176]{2,0,1:T(8,128)(2,1)} %param.6) | copy-start | bytes 69700
  10.2 30.6 %copy-start.1 = (bf16[176,22]{0,1:T(8,128)(2,1)S(1)}, bf16[176,22]{0,1:T(8,128)(2,1)}, u32[]{:S(2)}) copy-start(bf16[176,22]{0,1:T(8,128)(2,1)} %param.7) | copy-start | bytes 23236
  40.6 103.5 %all-gather.6.cloned.1.call-start = ((), (), s32[]{:S(2)}) async-start(), calls=%async_computation.6 | async-start | bytes 4595712 | tf_op jit(solution)/shard_map/all_gather | solution.py:273
  71.8 8.1 %collective-permute-start.1 = (bf16[1408,384]{1,0:T(8,128)(2,1)S(1)}, bf16[1408,384]{1,0:T(8,128)(2,1)S(1)}, u32[]{:S(2)}, u32[]{:S(2)}) collective-permute-start(bf16[1408,384]{1,0:T(8,128)(2,1)S(1)} %get-tuple-element.4.own_ref), channel_id=1, source_target_pairs={{0,8},{8,0},{1,9},{9,1},{2,10},{10,2},{3,11},{11,3},{4,12},{12,4},... | collective-permute-start | bytes 3244040 | tf_op jit(solution)/shard_map/ppermute | solution.py:272
  81.1 17.6 %copy-start.2 = (s32[4]{0:T(128)S(1)}, s32[4]{0:T(128)}, u32[]{:S(2)}) copy-start(s32[4]{0:T(128)} %param.8) | copy-start | bytes 52
  88.7 21.4 %all-to-all-start.3 = ((bf16[32,6,8,128]{3,2,1,0:T(8,128)(2,1)}), bf16[32,6,8,128]{3,2,1,0:T(8,128)(2,1)S(1)}, u32[]{:S(2)}, u32[]{:S(2)}) async-start(bf16[32,6,8,128]{3,2,1,0:T(8,128)(2,1)} %bitcast.9), calls=%async_computation.3 | async-start | bytes 786432 | tf_op jit(solution)/shard_map/all_to_all | solution.py:291
  98.7 5.7 %collective-permute-start = (s32[4]{0:T(128)S(1)}, s32[4]{0:T(128)S(1)}, u32[]{:S(2)}, u32[]{:S(2)}) collective-permute-start(s32[4]{0:T(128)S(1)} %copy-done.2), channel_id=1, source_target_pairs={{0,8},{8,0},{1,9},{9,1},{2,10},{10,2},{3,11},{11,3},{4,12},{12,4},... | collective-permute-start | bytes 56 | tf_op jit(solution)/shard_map/ppermute | solution.py:241
  112.0 9.9 %copy-start.3 = (s32[4]{0:T(128)S(1)}, s32[4]{0:T(128)}, u32[]{:S(2)}) copy-start(s32[4]{0:T(128)} %param.9) | copy-start | bytes 52
  112.0 32.1 %all-to-all-start.4 = ((bf16[16,24,8,128]{3,2,1,0:T(8,128)(2,1)}), bf16[16,24,8,128]{3,2,1,0:T(8,128)(2,1)S(1)}, u32[]{:S(2)}, u32[]{:S(2)}) async-start(bf16[16,24,8,128]{3,2,1,0:T(8,128)(2,1)} %pack.1), calls=%async_computation.4 | async-start | bytes 1572864 | tf_op jit(solution)/shard_map/all_to_all | solution.py:310
Sparse Core Ops, SparseCore 0:
  40.7 40.2 all-gather.3
  83.2 50.8 all-gather.5

commit v14 on v13

--- a/solution.py
+++ b/solution.py
@@ -35,20 +35,28 @@
     return lax.all_to_all(copies, axis, 0, 0, tiled=True)
 
 
-def share_kernel(at_ref, frames_ref, out_ref):
-    count, patches, width = frames_ref.shape
-    rows = out_ref.shape[0] * out_ref.shape[1]
-    row = lax.broadcasted_iota(jnp.int32, (rows, count * patches), 0)
-    column = lax.broadcasted_iota(jnp.int32, (rows, count * patches), 1)
-    wanted = (row & 1) * patches + (row >> 2) * 8 + ((row >> 1) & 1) * 4 + (at_ref[0] >> 1)
-    pick = jnp.where(column == wanted, 1.0, 0.0).astype(BF16)
-    tokens = frames_ref[...].reshape(count * patches, width)
-    xf = jnp.dot(pick, tokens, preferred_element_type=F32)
-    mean = jnp.mean(xf, axis=-1, keepdims=True)
-    centred = xf - mean
-    var = jnp.mean(centred * centred, axis=-1, keepdims=True)
-    normed = centred * lax.rsqrt(var + 1e-06)
-    out_ref[...] = normed.reshape(out_ref.shape).astype(BF16)
+def share_kernel(at_ref, frame_ref, out_ref, rows_ref):
+    step = pl.program_id(0)
+    patches, width = frame_ref.shape[1:]
+    shape = (rows_ref.shape[0], patches)
+    row = lax.broadcasted_iota(jnp.int32, shape, 0)
+    column = lax.broadcasted_iota(jnp.int32, shape, 1)
+    wanted = (row >> 2) * 8 + ((row >> 1) & 1) * 4 + (at_ref[0] >> 1)
+    pick = jnp.where((column == wanted) & ((row & 1) == step), 1.0, 0.0).astype(BF16)
+    part = jnp.dot(pick, frame_ref[0], preferred_element_type=F32)
+
+    @pl.when(step == 0)
+    def _():
+        rows_ref[...] = part
+
+    @pl.when(step == 1)
+    def _():
+        xf = rows_ref[...] + part
+        mean = jnp.mean(xf, axis=-1, keepdims=True)
+        centred = xf - mean
+        var = jnp.mean(centred * centred, axis=-1, keepdims=True)
+        normed = centred * lax.rsqrt(var + 1e-06)
+        out_ref[...] = normed.reshape(out_ref.shape).astype(BF16)
 
 
 def order_kernel(source_ref, right_ref, back_ref, order_ref):
@@ -228,9 +236,12 @@
         share_kernel,
         grid_spec=pltpu.PrefetchScalarGridSpec(
             num_scalar_prefetch=1,
-            grid=(1,),
-            in_specs=[pl.BlockSpec((2, patch_count, width), lambda g, at: (at[0] & 1, 0, 0))],
+            grid=(2,),
+            in_specs=[
+                pl.BlockSpec((1, patch_count, width), lambda g, at: (2 * (at[0] & 1) + g, 0, 0))
+            ],
             out_specs=pl.BlockSpec((2 * chips, 2, width), lambda g, at: (0, 0, 0)),
+            scratch_shapes=[pltpu.VMEM((4 * chips, width), F32)],
         ),
         out_shape=jax.ShapeDtypeStruct((2 * chips, 2, width), BF16),
         compiler_params=params(SHARE),

time: 157 us -> 157 us (level)
  no operation moved by 1% of the time
where the time goes in v14:
time: 157 us; the launch traced here: 156 us
  blocking collectives  58.5 us (37%)
  starting transfers between devices  30.6 us (19%)
  waiting for transfers between devices  29.5 us (19%)
  Pallas kernels  19.1 us (12%)
  between operations  14.8 us (9%)
  other arithmetic  2.07 us (1%)
  local copies, waits for them, and re-layouts  1.75 us (1%)
    all_to_all x1, blocking collectives, local(): lax.all_to_all(share, FRAME, 0, 0, tiled=True).reshape(4 * chips, width)  29.5 us
    all_to_all x2, blocking collectives, spread(): return lax.all_to_all(copies, axis, 0, 0, tiled=True)  27.2 us
    all_to_all x1, waiting for transfers between devices, local(): gathered = lax.all_to_all(packed, ('c', 'pool'), 0, 0, tiled=True)  19.6 us
    all_to_all x1, starting transfers between devices, local(): gathered = lax.all_to_all(packed, ('c', 'pool'), 0, 0, tiled=True)  9.93 us
    all_to_all x1, starting transfers between devices, local(): returned = lax.all_to_all(attended, CHIP, 0, 0, tiled=True)  9.88 us
    pallas_call x1, Pallas kernels, local(): pl.pallas_call(track_kernel, grid=(4 // STEP,), in_specs=[pl.BlockSpec(me...  7.68 us
    ppermute x1, starting transfers between devices, local(): mine_other = lax.ppermute(mine, 'c', swap)  5.79 us
    all_to_all x1, waiting for transfers between devices, local(): returned = lax.all_to_all(attended, CHIP, 0, 0, tiled=True)  5.63 us
  transfers between devices with their start and end apart: 6, of which 5 were waited for; matrix products, arithmetic and copies ran while one was open for 2% of the time, Pallas kernels for 7%

profile of v14, /device:TPU:1, one launch (start us, length us, event | category | flops | bytes accessed | tf_op | source)
XLA Modules:
  0.0 156.4 jit_solution(16453419745845713676)
XLA Ops:
  7.2 3.0 %share.1 = bf16[64,2,1408]{2,1,0:T(2,128)(2,1)} custom-call(s32[1]{0:T(128)} %bitcast.3.at_ref, bf16[4,256,1408]{2,1,0:T(8,128)(2,1)} %frame_ref.3), custom_call_target="tpu_custom_call" | custom-call | tf_op jit(solution)/shard_map/share/pallas_call | solution.py:235
  10.2 29.5 %all_to_all.25 = bf16[64,2,1408]{2,1,0:T(2,128)(2,1)S(1)} all-to-all(bf16[64,2,1408]{2,1,0:T(2,128)(2,1)} %share.1), channel_id=1, replica_groups=mesh['zh'=4,'zl'=2,'x'=4,'c'=2,'pool'=8] {'zh','zl','x','c'}, dimensions={0} | all-to-all | bytes 720896 | tf_op jit(solution)/shard_map/all_to_all | solution.py:250
  39.7 0.9 all_gather_reshape.3
  40.7 0.1 reshape.27
  41.1 0.2 concatenate.11
  41.4 1.9 %all_gather.13 = bf16[44,2,384]{2,1,0:T(2,128)(2,1)S(1)} all-gather(bf16[22,2,384]{2,1,0:T(2,128)(2,1)S(1)} %concatenate.11), channel_id=1, replica_groups=mesh['zh'=4,'zl'=2,'x'=4,'c'=2,'pool'=8] {'c'}, dimensions={0}, use_global_device_ids=true | all-gather | bytes 101376 | tf_op jit(solution)/shard_map/all_gather | solution.py:269
  43.3 10.7 %all_to_all.26 = bf16[4,44,384]{2,1,0:T(8,128)(2,1)S(1)} all-to-all(bf16[4,44,384]{2,1,0:T(8,128)(2,1)S(1)} %broadcast_in_dim.22), channel_id=1, replica_groups=mesh['zh'=4,'zl'=2,'x'=4,'c'=2,'pool'=8] {'zh'}, dimensions={0} | all-to-all | bytes 270336 | tf_op jit(solution)/shard_map/all_to_all | solution.py:35
  54.2 16.4 %all_to_all.27.source_ref = bf16[8,176,384]{2,1,0:T(8,128)(2,1)S(1)} all-to-all(bf16[8,176,384]{2,1,0:T(8,128)(2,1)S(1)} %broadcast_in_dim.24), channel_id=1, replica_groups=mesh['zh'=4,'zl'=2,'x'=4,'c'=2,'pool'=8] {'zl','x'}, dimensions={0} | all-to-all | bytes 2162688 | tf_op jit(solution)/shard_map/all_to_all | solution.py:35
  70.6 1.2 order.1
  71.8 5.8 %collective-permute-start.1 = (bf16[1408,384]{1,0:T(8,128)(2,1)S(1)}, bf16[1408,384]{1,0:T(8,128)(2,1)S(1)}, u32[]{:S(2)}, u32[]{:S(2)}) collective-permute-start(bf16[1408,384]{1,0:T(8,128)(2,1)S(1)} %get-tuple-element.4.own_ref), channel_id=1, source_target_pairs={{0,8},{8,0},{1,9},{9,1},{2,10},{10,2},{3,11},{11,3},{4,12},{12,4},... | collective-permute-start | bytes 3244040 | tf_op jit(solution)/shard_map/ppermute | solution.py:283
  77.6 2.3 %collective-permute-done.1.other_ref = bf16[1408,384]{1,0:T(8,128)(2,1)S(1)} collective-permute-done((bf16[1408,384]{1,0:T(8,128)(2,1)S(1)}, bf16[1408,384]{1,0:T(8,128)(2,1)S(1)}, u32[]{:S(2)}, u32[]{:S(2)}) %collective-permute-start.1) | collective-permute-done | bytes 1081376 | tf_op jit(solution)/shard_map/ppermute | solution.py:283
  79.9 1.2 all-gather.4.cloned.1.call-done.tokens_ref
  81.1 7.7 %track.1 = bf16[16,2,6,8,128]{4,3,2,1,0:T(8,128)(2,1)} custom-call(s32[1]{0:T(128)} %bitcast.2.core_ref, bf16[8,128,1408]{2,1,0:T(8,128)(2,1)} %all-gather.4.cloned.1.call-done.tokens_ref, bf16[1408,384]{1,0:T(8,128)(2,1)S(1)} %get-tuple-element.4.own_ref, bf16[1408,384]{1,0:T(8,128)(2,1)S(1)} %collective-permute-done.1.other_ref), custom_call_target="tpu_custom_call" | custom-call | tf_op jit(solution)/shard_map/track/pallas_call | solution.py:286
  88.8 9.9 %all-to-all-start.3 = ((bf16[32,6,8,128]{3,2,1,0:T(8,128)(2,1)}), bf16[32,6,8,128]{3,2,1,0:T(8,128)(2,1)S(1)}, u32[]{:S(2)}, u32[]{:S(2)}) async-start(bf16[32,6,8,128]{3,2,1,0:T(8,128)(2,1)} %bitcast.9), calls=%async_computation.3 | async-start | bytes 786432 | tf_op jit(solution)/shard_map/all_to_all | solution.py:302
  98.7 4.9 %collective-permute-start = (s32[4]{0:T(128)S(1)}, s32[4]{0:T(128)S(1)}, u32[]{:S(2)}, u32[]{:S(2)}) collective-permute-start(s32[4]{0:T(128)S(1)} %copy-done.2), channel_id=1, source_target_pairs={{0,8},{8,0},{1,9},{9,1},{2,10},{10,2},{3,11},{11,3},{4,12},{12,4},... | collective-permute-start | bytes 56 | tf_op jit(solution)/shard_map/ppermute | solution.py:252
  103.6 0.8 collective-permute-done
  104.5 5.6 %all-to-all-done.3 = bf16[32,6,8,128]{3,2,1,0:T(8,128)(2,1)S(1)} async-done(((bf16[32,6,8,128]{3,2,1,0:T(8,128)(2,1)}), bf16[32,6,8,128]{3,2,1,0:T(8,128)(2,1)S(1)}, u32[]{:S(2)}, u32[]{:S(2)}) %all-to-all-start.3) | async-done | bytes 393248 | tf_op jit(solution)/shard_map/all_to_all | solution.py:302
  110.1 1.8 %pack.1 = bf16[16,24,8,128]{3,2,1,0:T(8,128)(2,1)} custom-call(s32[8]{0:T(128)S(1)} %broadcast_select_fusion.owner_ref, bf16[16,2,6,8,128]{4,3,2,1,0:T(8,128)(2,1)S(1)} %bitcast.19), custom_call_target="tpu_custom_call" | custom-call | tf_op jit(solution)/shard_map/pack/pallas_call | solution.py:309
  112.0 9.9 %all-to-all-start.4 = ((bf16[16,24,8,128]{3,2,1,0:T(8,128)(2,1)}), bf16[16,24,8,128]{3,2,1,0:T(8,128)(2,1)S(1)}, u32[]{:S(2)}, u32[]{:S(2)}) async-start(bf16[16,24,8,128]{3,2,1,0:T(8,128)(2,1)} %pack.1), calls=%async_computation.4 | async-start | bytes 1572864 | tf_op jit(solution)/shard_map/all_to_all | solution.py:321
  121.9 0.6 select_reduce_fusion
  122.5 0.6 reduce_or.9
  123.8 0.7 pad_add_fusion.pick_ref
  124.5 19.6 %all-to-all-done.4.y_ref = bf16[16,24,8,128]{3,2,1,0:T(8,128)(2,1)S(1)} async-done(((bf16[16,24,8,128]{3,2,1,0:T(8,128)(2,1)}), bf16[16,24,8,128]{3,2,1,0:T(8,128)(2,1)S(1)}, u32[]{:S(2)}, u32[]{:S(2)}) %all-to-all-start.4) | async-done | bytes 786464 | tf_op jit(solution)/shard_map/all_to_all | solution.py:321
  144.1 5.4 %deliver.1 = (bf16[1,256,1408]{2,1,0:T(8,128)(2,1)}, bf16[1,11,256]{2,1,0:T(8,128)(2,1)}) custom-call(s32[2]{0:T(128)S(1)} %pad_add_fusion.pick_ref, bf16[4,256,1408]{2,1,0:T(8,128)(2,1)} %frame_ref.3, bf16[16,24,8,128]{3,2,1,0:T(8,128)(2,1)S(1)} %all-to-all-done.4.y_ref, bf16[16,96,1408]{2,1,0:T(8,128)(2,1)} %bitcast.20), custom_call_target="tpu_custom_call" | custom-call | tf_op jit(solution)/shard_map/deliver/pallas_call | solution.py:327
  (24 shorter events, 0.7 us)
Async XLA Ops:
  7.2 73.9 %all-gather.4.cloned.1.call-start = ((), (), s32[]{:S(2)}) async-start(), calls=%async_computation.5 | async-start | bytes 3244032 | tf_op jit(solution)/shard_map/all_gather | solution.py:251
  10.2 30.4 %copy-start = (bf16[22,3,176]{2,0,1:T(8,128)(2,1)S(1)}, bf16[22,3,176]{2,0,1:T(8,128)(2,1)}, u32[]{:S(2)}) copy-start(bf16[22,3,176]{2,0,1:T(8,128)(2,1)} %param.6) | copy-start | bytes 69700
  10.2 30.6 %copy-start.1 = (bf16[176,22]{0,1:T(8,128)(2,1)S(1)}, bf16[176,22]{0,1:T(8,128)(2,1)}, u32[]{:S(2)}) copy-start(bf16[176,22]{0,1:T(8,128)(2,1)} %param.7) | copy-start | bytes 23236
  40.6 103.5 %all-gather.6.cloned.1.call-start = ((), (), s32[]{:S(2)}) async-start(), calls=%async_computation.6 | async-start | bytes 4595712 | tf_op jit(solution)/shard_map/all_gather | solution.py:284
  71.8 8.1 %collective-permute-start.1 = (bf16[1408,384]{1,0:T(8,128)(2,1)S(1)}, bf16[1408,384]{1,0:T(8,128)(2,1)S(1)}, u32[]{:S(2)}, u32[]{:S(2)}) collective-permute-start(bf16[1408,384]{1,0:T(8,128)(2,1)S(1)} %get-tuple-element.4.own_ref), channel_id=1, source_target_pairs={{0,8},{8,0},{1,9},{9,1},{2,10},{10,2},{3,11},{11,3},{4,12},{12,4},... | collective-permute-start | bytes 3244040 | tf_op jit(solution)/shard_map/ppermute | solution.py:283
  81.1 17.6 %copy-start.2 = (s32[4]{0:T(128)S(1)}, s32[4]{0:T(128)}, u32[]{:S(2)}) copy-start(s32[4]{0:T(128)} %param.8) | copy-start | bytes 52
  88.8 21.4 %all-to-all-start.3 = ((bf16[32,6,8,128]{3,2,1,0:T(8,128)(2,1)}), bf16[32,6,8,128]{3,2,1,0:T(8,128)(2,1)S(1)}, u32[]{:S(2)}, u32[]{:S(2)}) async-start(bf16[32,6,8,128]{3,2,1,0:T(8,128)(2,1)} %bitcast.9), calls=%async_computation.3 | async-start | bytes 786432 | tf_op jit(solution)/shard_map/all_to_all | solution.py:302
  98.7 5.7 %collective-permute-start = (s32[4]{0:T(128)S(1)}, s32[4]{0:T(128)S(1)}, u32[]{:S(2)}, u32[]{:S(2)}) collective-permute-start(s32[4]{0:T(128)S(1)} %copy-done.2), channel_id=1, source_target_pairs={{0,8},{8,0},{1,9},{9,1},{2,10},{10,2},{3,11},{11,3},{4,12},{12,4},... | collective-permute-start | bytes 56 | tf_op jit(solution)/shard_map/ppermute | solution.py:252
  112.0 9.9 %copy-start.3 = (s32[4]{0:T(128)S(1)}, s32[4]{0:T(128)}, u32[]{:S(2)}) copy-start(s32[4]{0:T(128)} %param.9) | copy-start | bytes 52
  112.0 32.1 %all-to-all-start.4 = ((bf16[16,24,8,128]{3,2,1,0:T(8,128)(2,1)}), bf16[16,24,8,128]{3,2,1,0:T(8,128)(2,1)S(1)}, u32[]{:S(2)}, u32[]{:S(2)}) async-start(bf16[16,24,8,128]{3,2,1,0:T(8,128)(2,1)} %pack.1), calls=%async_computation.4 | async-start | bytes 1572864 | tf_op jit(solution)/shard_map/all_to_all | solution.py:321
Sparse Core Ops, SparseCore 0:
  40.7 40.2 all-gather.3
  83.2 50.8 all-gather.5
